TPU v7x, 512 devices: a whole 4x8x8 slice. The times are simulated.
512 devices in a mesh: row: 32 (over y, z_lo, core), col: 16 (over x, z_hi).
Axes of the slice: x: 4, y: 8, z: 8 (z_hi: 4, z_lo: 2; z = z_hi * 2 + z_lo), core: 2. Of those that a mesh axis runs over, the one named last changes fastest.
Arguments:
- pair_rep: bfloat16 [448, 448, 128], P('row', 'col'), may hold values from -6 to 6
- chain_lengths: int32 [4], replicated, may hold values from 1 to 112, 336 in all
- in_gain: float32 [2, 128], replicated, may hold values from 0.1 to 1.9
- in_bias: float32 [2, 128], replicated, may hold values from -3 to 3
- weight_in: bfloat16 [2, 128, 640], replicated, may hold values from -0.5 to 0.5
- out_gain: float32 [2, 128], replicated, may hold values from 0.1 to 1.9
- out_bias: float32 [2, 128], replicated, may hold values from -3 to 3
- weight_out: bfloat16 [2, 128, 128], replicated, may hold values from -0.5 to 0.5
Outputs:
- updated: bfloat16 [448, 448, 128], P('row', 'col')
Inputs may be any that keep to these rules, and one draw needn't show every extreme that they name: Chain c occupies token positions c * 112 to (c + 1) * 112 - 1 of both pair dimensions; its first chain_lengths[c] positions are real, the rest padding; the lengths sum to 336.
All inputs are finite; a program needn't handle non-finite values.
Results may differ from a plain program's by a relative error of at most 0.012.
Values may be sent and summed in bfloat16 or wider, within the bound.
No kernel may reach another device: no remote copies, remote signals or barrier semaphores. Data moves between devices by JAX's collectives and lax.ppermute only.
A program may use at most 64 MiB of HBM per device.

v0:
```python
import jax
import jax.numpy as jnp
from jax import lax
from jax.sharding import PartitionSpec as P

EPSILON = 1e-05


def spread(shard, axis, root):
    mine = lax.axis_index(axis) == root
    return lax.psum(jnp.where(mine, shard, jnp.zeros_like(shard)), axis)


def layer_norm(values, gain, bias):
    average = jnp.mean(values, axis=-1, keepdims=True)
    centered = values - average
    variance = jnp.mean(centered * centered, axis=-1, keepdims=True)
    return centered * lax.rsqrt(variance + EPSILON) * gain + bias


def token_valid(chain_lengths, first_token, token_total, slot_size):
    chain_count = chain_lengths.shape[0]
    position = first_token + jnp.arange(token_total, dtype=jnp.int32)
    chain_index = position // slot_size
    chain_ids = jnp.arange(chain_count, dtype=jnp.int32)
    limits = jnp.sum(
        jnp.where(chain_index[:, None] == chain_ids[None, :], chain_lengths[None, :], 0), axis=1
    )
    return (position - chain_index * slot_size < limits).astype(jnp.float32)


def project_tile(pair_tile, pair_mask, gain, bias, weight_in):
    tile_rows, tile_cols, channels = pair_tile.shape
    hidden = (weight_in.shape[1] - channels) // 4
    normed = layer_norm(pair_tile.astype(jnp.float32), gain, bias).astype(jnp.bfloat16)
    projected = jnp.dot(normed.reshape(-1, channels), weight_in, preferred_element_type=jnp.float32)
    projected = projected.reshape(tile_rows, tile_cols, -1)
    weighting = pair_mask[:, :, None]
    left_proj = (
        weighting * jax.nn.sigmoid(projected[:, :, hidden : 2 * hidden]) * projected[:, :, :hidden]
    ).astype(jnp.bfloat16)
    right_proj = (
        weighting
        * jax.nn.sigmoid(projected[:, :, 3 * hidden : 4 * hidden])
        * projected[:, :, 2 * hidden : 3 * hidden]
    ).astype(jnp.bfloat16)
    gating = jax.nn.sigmoid(projected[:, :, 4 * hidden :])
    return (left_proj, right_proj, gating)


def finish_tile(pair_tile, triangle, gating, gain, bias, weight_out):
    normed = layer_norm(triangle, gain, bias).astype(jnp.bfloat16)
    hidden = normed.shape[2]
    update = jnp.dot(normed.reshape(-1, hidden), weight_out, preferred_element_type=jnp.float32)
    update = update.reshape(pair_tile.shape)
    return (pair_tile.astype(jnp.float32) + gating * update).astype(jnp.bfloat16)


def on_device(pair_rep, chain_lengths, in_gain, in_bias, weight_in, out_gain, out_bias, weight_out):
    tile_rows = pair_rep.shape[0]
    tile_cols = pair_rep.shape[1]
    group_size = lax.axis_size("row") // lax.axis_size("col")
    token_count = tile_rows * lax.axis_size("row")
    slot_size = token_count // chain_lengths.shape[0]
    row_index = lax.axis_index("row")
    col_index = lax.axis_index("col")
    valid_rows = token_valid(chain_lengths, row_index * tile_rows, tile_rows, slot_size)
    valid_cols = token_valid(chain_lengths, col_index * tile_cols, tile_cols, slot_size)
    pair_mask = valid_rows[:, None] * valid_cols[None, :]
    left_proj, right_proj, gating = project_tile(
        pair_rep, pair_mask, in_gain[0], in_bias[0], weight_in[0]
    )
    left_rows, right_rows = (
        lax.all_gather(left_proj, "col", axis=1, tiled=True),
        lax.all_gather(right_proj, "col", axis=1, tiled=True),
    )
    members = []
    for member in range(group_size):
        root_row = col_index * group_size + member
        members.append(spread(right_rows, "row", root_row))
    right_panel = jnp.concatenate(members, axis=0)
    triangle = jnp.einsum(
        "ikh,jkh->ijh", left_rows, right_panel, preferred_element_type=jnp.float32
    )
    middle = finish_tile(pair_rep, triangle, gating, out_gain[0], out_bias[0], weight_out[0])
    left_proj, right_proj, gating = project_tile(
        middle, pair_mask, in_gain[1], in_bias[1], weight_in[1]
    )
    offset_in = row_index % group_size * tile_rows
    root_col = row_index // group_size
    left_cols, right_cols = (
        lax.all_gather(left_proj, "row", axis=0, tiled=True),
        lax.all_gather(right_proj, "row", axis=0, tiled=True),
    )
    own_left = lax.dynamic_slice_in_dim(left_cols, offset_in, tile_rows, 1)
    left_panel = spread(own_left, "col", root_col)
    triangle = jnp.einsum(
        "kih,kjh->ijh", left_panel, right_cols, preferred_element_type=jnp.float32
    )
    return finish_tile(middle, triangle, gating, out_gain[1], out_bias[1], weight_out[1])


def solution(mesh):
    placed = (P("row", "col", None), P(), P(), P(), P(), P(), P(), P())
    return jax.shard_map(
        on_device, mesh=mesh, in_specs=placed, out_specs=P("row", "col", None), check_vma=False
    )
```

profile of v0, /device:TPU:1, one launch (start us, length us, event | category | flops | bytes accessed | tf_op | source)
XLA Modules:
  0.0 735.4 jit_solution(2568701892599306387)
XLA Ops:
  6.5 0.0 all-gather.5.cloned.1.call-start
  6.6 0.7 select_reduce_fusion.1
  7.3 0.7 select_reduce_fusion
  8.1 1.0 convert_reduce_fusion
  9.1 1.1 fusion.11
  10.3 0.1 broadcast_multiply_fusion
  10.4 0.8 slice_bitcast_fusion.2
  11.1 1.3 fusion.43
  12.5 0.2 fusion.33
  12.7 0.7 copy.33
  13.3 0.0 all-gather.5.cloned.1.call-update
  13.4 0.0 all-gather.7.cloned.1.call-start
  13.4 0.7 copy.36
  14.1 0.0 all-gather.7.cloned.1.call-update
  14.1 0.0 all-reduce.6.cloned.1.call-start
  14.2 66.6 %all-gather.5.cloned.1.call-done = bf16[14,448,128]{2,0,1:T(8,128)(2,1)} async-done(((bf16[14,28,128]{2,0,1:T(8,128)(2,1)}), bf16[14,448,128]{2,0,1:T(8,128)(2,1)}) %all-gather.5.cloned.1.call-update) | async-done | bytes 1605648 | tf_op jit(solution)/shard_map/all_gather | solution.py:75
  80.8 3.9 copy.34
  84.7 2.3 broadcast_select_fusion.2
  87.0 0.0 copy-start.4
  87.0 0.0 copy-start.5
  87.0 0.0 all-reduce.6.cloned.1.call-update
  87.0 0.0 all-gather.11.cloned.1.call-start
  87.0 0.6 copy-done.4
  87.6 0.0 copy-done.5
  87.7 57.2 %all-gather.7.cloned.1.call-done = bf16[14,448,128]{2,0,1:T(8,128)(2,1)} async-done(((bf16[14,28,128]{2,0,1:T(8,128)(2,1)}), bf16[14,448,128]{2,0,1:T(8,128)(2,1)}) %all-gather.7.cloned.1.call-update) | async-done | bytes 1605648 | tf_op jit(solution)/shard_map/all_gather | solution.py:74
  144.8 3.9 copy.37
  148.7 242.9 %all-reduce.6.cloned.1.call-done = (bf16[14,448,128]{1,0,2:T(8,128)(2,1)}, bf16[14,448,128]{1,0,2:T(8,128)(2,1)}) async-done(((bf16[14,448,128]{1,0,2:T(8,128)(2,1)}, bf16[14,448,128]{1,0,2:T(8,128)(2,1)}), (bf16[14,448,128]{1,0,2:T(8,128)(2,1)}, bf16[14,448,128]{1,0,2:T(8,128)(2,1)})) %all-reduce.6.cloned.1.call-update) | async-done | bytes 3211280 | tf_op jit(solution)/shard_map/psum | solution.py:11
  391.6 0.0 copy-start
  391.6 0.0 copy-start.6
  391.6 4.5 fusion
  396.1 0.0 copy-start.3
  396.1 1.6 copy.38
  397.7 0.1 bitcast_reduce_fusion.1
  397.9 0.2 multiply_reduce_fusion.2
  398.1 0.0 copy-done
  398.1 0.0 copy-done.6
  398.1 0.4 fusion.69
  398.5 0.0 copy-start.1
  398.6 0.2 multiply_reduce_fusion.1
  398.8 0.0 copy-done.3
  398.8 0.4 fusion.41
  399.2 0.9 fusion.15
  400.1 0.0 all-gather.11.cloned.1.call-update
  400.1 0.0 all-gather.9.cloned.1.call-start
  400.1 0.5 all-gather.9.cloned.1.call-update
  400.7 0.0 all-reduce.4.cloned.1.call-start
  400.8 69.1 %all-gather.11.cloned.1.call-done = bf16[448,28,128]{2,1,0:T(8,128)(2,1)} async-done(((bf16[14,28,128]{2,1,0:T(8,128)(2,1)}), bf16[448,28,128]{2,1,0:T(8,128)(2,1)}) %all-gather.11.cloned.1.call-update) | async-done | bytes 3211280 | tf_op jit(solution)/shard_map/all_gather | solution.py:92
  469.9 0.0 copy-done.1
  469.9 3.9 constant_dynamic-slice_fusion
  473.8 3.9 copy.42
  477.7 1.5 broadcast_select_fusion
  479.2 0.0 all-reduce.4.cloned.1.call-update
  479.2 62.0 %all-gather.9.cloned.1.call-done = bf16[448,28,128]{2,1,0:T(8,128)(2,1)} async-done(((bf16[14,28,128]{2,1,0:T(8,128)(2,1)}), bf16[448,28,128]{2,1,0:T(8,128)(2,1)}) %all-gather.9.cloned.1.call-update) | async-done | bytes 3211280 | tf_op jit(solution)/shard_map/all_gather | solution.py:93
  541.1 22.0 %copy.40 = bf16[448,28,128]{1,0,2:T(8,128)(2,1)} copy(bf16[448,28,128]{2,1,0:T(8,128)(2,1)} %all-gather.9.cloned.1.call-done) | data formatting | bytes 6422528 | tf_op jit(solution)/shard_map/all_gather | solution.py:93
  563.1 0.0 copy-start.2
  563.1 156.4 %all-reduce.4.cloned.1.call-done = bf16[448,14,128]{0,1,2:T(8,128)(2,1)} async-done(((bf16[448,14,128]{0,1,2:T(8,128)(2,1)}), bf16[448,14,128]{0,1,2:T(8,128)(2,1)}) %all-reduce.4.cloned.1.call-update) | async-done | bytes 1605648 | tf_op jit(solution)/shard_map/psum | solution.py:11
  719.6 7.2 fusion.70
  726.7 0.4 copy.41
  727.2 0.1 bitcast_reduce_fusion
  727.3 0.2 multiply_reduce_fusion
  727.6 0.0 copy-done.2
  727.6 1.0 fusion.7
  (13 shorter events, 0.1 us)
Async XLA Ops:
  6.5 74.3 %all-gather.5.cloned.1.call-start = ((), (), s32[]{:S(2)}) async-start(), calls=%async_computation | async-start | bytes 1949696 | tf_op jit(solution)/shard_map/all_gather | solution.py:75
  13.4 131.5 %all-gather.7.cloned.1.call-start = ((), (), s32[]{:S(2)}) async-start(), calls=%async_computation.1 | async-start | bytes 1949696 | tf_op jit(solution)/shard_map/all_gather | solution.py:74
  14.1 377.5 %all-reduce.6.cloned.1.call-start = ((), (), s32[]{:S(2)}) async-start(), calls=%async_computation.5 | async-start | bytes 8388608 | tf_op jit(solution)/shard_map/psum | solution.py:11
  87.0 0.7 copy-start.4
  87.0 0.7 copy-start.5
  87.0 382.9 %all-gather.11.cloned.1.call-start = ((), (), s32[]{:S(2)}) async-start(), calls=%async_computation.3 | async-start | bytes 3784704 | tf_op jit(solution)/shard_map/all_gather | solution.py:92
  391.6 6.5 copy-start
  391.6 6.5 copy-start.6
  396.1 2.7 copy-start.3
  398.5 71.3 %copy-start.1 = (f32[14,28,128]{2,1,0:T(8,128)}, f32[14,28,128]{2,1,0:T(8,128)S(1)}, u32[]{:S(2)}) copy-start(f32[14,28,128]{2,1,0:T(8,128)S(1)} %get-tuple-element.22) | copy-start | bytes 602116
  400.1 141.1 %all-gather.9.cloned.1.call-start = ((), (), s32[]{:S(2)}) async-start(), calls=%async_computation.2 | async-start | bytes 3784704 | tf_op jit(solution)/shard_map/all_gather | solution.py:93
  400.7 318.9 %all-reduce.4.cloned.1.call-start = ((), (), s32[]{:S(2)}) async-start(), calls=%async_computation.4 | async-start | bytes 4194304 | tf_op jit(solution)/shard_map/psum | solution.py:11
  563.1 164.4 %copy-start.2 = (f32[14,28,128]{2,1,0:T(8,128)S(1)}, f32[14,28,128]{2,1,0:T(8,128)}, u32[]{:S(2)}) copy-start(f32[14,28,128]{2,1,0:T(8,128)} %copy-done.1) | copy-start | bytes 602116
Sparse Core Ops, SparseCore 0:
  13.5 67.2 all-gather.4
  83.9 60.9 all-gather.6
  147.8 243.7 all-reduce.5
  400.2 69.6 all-gather.10
  471.9 69.2 all-gather.8
  543.9 175.5 all-reduce.3
where the time goes:
time: 746 us; the launch traced here: 735 us
  waiting for transfers between devices  655 us (88%)
  local copies, waits for them, and re-layouts  42.4 us (6%)
  matrix products  14.7 us (2%)
  between operations  13.7 us (2%)
  other arithmetic  9.58 us (1%)
    psum x2, waiting for transfers between devices, spread(): return lax.psum(jnp.where(mine, shard, jnp.zeros_like(shard)), axis)  399 us
    all_gather x1, waiting for transfers between devices, on_device(): lax.all_gather(left_proj, 'row', axis=0, tiled=True)  69.1 us
    all_gather x1, waiting for transfers between devices, on_device(): lax.all_gather(right_proj, 'col', axis=1, tiled=True)  66.6 us
    all_gather x1, waiting for transfers between devices, on_device(): lax.all_gather(right_proj, 'row', axis=0, tiled=True)  62 us
    all_gather x1, waiting for transfers between devices, on_device(): lax.all_gather(left_proj, 'col', axis=1, tiled=True)  57.2 us
    all_gather x1, local copies, waits for them, and re-layouts, on_device(): lax.all_gather(right_proj, 'row', axis=0, tiled=True)  22 us
  transfers between devices with their start and end apart: 6, of which 6 were waited for; matrix products, arithmetic and copies ran while one was open for 6% of the time, Pallas kernels for 0%

commit v1 on v0

v1 whole, which is shorter than its diff:
```python
import jax
import jax.numpy as jnp
from jax import lax
from jax.experimental import pallas as pl
from jax.experimental.pallas import tpu as pltpu
from jax.sharding import Mesh, PartitionSpec as P

EPSILON = 1e-05
F32 = jnp.float32
BF16 = jnp.bfloat16

ROWS = 14
COLS = 28
WIDE = 32
CELLS = 512
GROUPS = 4
LANES = 128
SLOT = 112
CHAINS = 4

ROW_AXES = ("y", "zl", "core")
COL_AXES = ("x", "zh")
GROUP1 = ("x", "zh", "y")
GROUP2 = ("zh",) + ROW_AXES


def nt_dot(left, right):
    return lax.dot_general(left, right, (((1,), (1,)), ((), ())), preferred_element_type=F32)


def tn_dot(left, right):
    return lax.dot_general(left, right, (((0,), (0,)), ((), ())), preferred_element_type=F32)


def nn_dot(left, right):
    return jnp.dot(left, right, preferred_element_type=F32)


def norm_rows(values, gain, bias):
    average = jnp.mean(values, axis=0, keepdims=True)
    centered = values - average
    variance = jnp.mean(centered * centered, axis=0, keepdims=True)
    return (centered * lax.rsqrt(variance + EPSILON) * gain + bias).astype(BF16)


def one_hot(row_code, col_code):
    return (row_code == col_code).astype(F32).astype(BF16)


def swap_matrix():
    row = lax.broadcasted_iota(jnp.int32, (CELLS, 1), 0)
    col = lax.broadcasted_iota(jnp.int32, (1, CELLS), 1)
    swapped = ((col >> 5) & 3) * 128 + (col >> 7) * 32 + (col & 31)
    return one_hot(row, swapped)


def fields(code, *widths):
    out = []
    for width in reversed(widths):
        out.append(code & (width - 1))
        code = code >> (width.bit_length() - 1)
    return out[::-1]


def token_of_row(row, a, skip):
    return jnp.where(a < ROWS, row * ROWS + a, skip)


def token_of_col(x, zh, b, skip):
    return jnp.where(b < COLS, x * SLOT + zh * COLS + b, skip)


def valid_token(token, lengths_ref):
    valid = jnp.zeros(token.shape, jnp.bool_)
    for chain in range(CHAINS):
        start = chain * SLOT
        valid = valid | ((token >= start) & (token < start + lengths_ref[chain]))
    return valid


def cell_mask(place_ref, lengths_ref):
    lane = lax.broadcasted_iota(jnp.int32, (1, CELLS), 1)
    a, b = lane >> 5, lane & 31
    row = valid_token(place_ref[0] * ROWS + a, lengths_ref)
    col = valid_token(place_ref[1] * COLS + b, lengths_ref)
    inside = (a < ROWS) & (b < COLS)
    return jnp.where(row & col & inside, 1.0, 0.0).astype(F32)


def project(columns, mask, gain, bias, weight, send, send_ref, gate_ref):
    for m in range(GROUPS):
        lanes = slice(m * LANES, (m + 1) * LANES)
        normed = norm_rows(columns[:, lanes], gain, bias)
        projected = tn_dot(weight, normed)
        weighting = mask[:, lanes]
        left = weighting * jax.nn.sigmoid(projected[128:256]) * projected[0:128]
        right = weighting * jax.nn.sigmoid(projected[384:512]) * projected[256:384]
        send[pl.ds(m, 128, stride=8), :] = left
        send[pl.ds(4 + m, 128, stride=8), :] = right
        gate_ref[:, lanes] = jax.nn.sigmoid(projected[512:640])
    send_ref[...] = send[...].astype(BF16)


def turn_vectors(in_gain, in_bias, out_gain, out_bias):
    rows = jnp.concatenate([in_gain[...], in_bias[...], out_gain[...], out_bias[...]], axis=0)
    return rows.T


def first_kernel(
    place, lengths, pair, in_gain, in_bias, weight, out_gain, out_bias,
    send_ref, gate_ref, columns_ref, cells, send,
):
    vectors = turn_vectors(in_gain, in_bias, out_gain, out_bias)
    cells[...] = jnp.zeros_like(cells)
    for a in range(ROWS):
        cells[pl.ds(a * WIDE, COLS), :] = pair[a].astype(F32)
    columns = cells[...].T
    columns_ref[...] = columns
    mask = cell_mask(place, lengths)
    project(columns, mask, vectors[:, 0:1], vectors[:, 2:3], weight[0], send, send_ref, gate_ref)


def finish(back, update, gate, columns, vectors, weight_out, got):
    got[...] = back[...].astype(F32)
    parts = []
    for m in range(GROUPS):
        lanes = slice(m * LANES, (m + 1) * LANES)
        triangle = got[pl.ds(m, 128, stride=4), :]
        normed = norm_rows(triangle, vectors[:, 4 + update : 5 + update], vectors[:, 6 + update : 7 + update])
        change = tn_dot(weight_out, normed)
        parts.append(columns[:, lanes] + gate[:, lanes] * change)
    return jnp.concatenate(parts, axis=1).astype(BF16)


def middle_kernel(
    place, lengths, back, gate, columns, in_gain, in_bias, weight, out_gain, out_bias, weight_out,
    send_ref, gate_ref, columns_ref, got, send,
):
    vectors = turn_vectors(in_gain, in_bias, out_gain, out_bias)
    middle = finish(back, 0, gate, columns, vectors, weight_out[0], got).astype(F32)
    columns_ref[...] = middle
    mask = cell_mask(place, lengths)
    project(middle, mask, vectors[:, 1:2], vectors[:, 3:4], weight[1], send, send_ref, gate_ref)


def last_kernel(
    back, gate, columns, in_gain, in_bias, out_gain, out_bias, weight_out, out_ref, got, cells
):
    vectors = turn_vectors(in_gain, in_bias, out_gain, out_bias)
    updated = finish(back, 1, gate, columns, vectors, weight_out[1], got).astype(F32)
    cells[...] = updated.T
    for a in range(ROWS):
        out_ref[a] = cells[pl.ds(a * WIDE, COLS), :].astype(BF16)


def outgoing_kernel(mine, gathered, out_ref, mine_f, right_f, out_f):
    swap = swap_matrix()
    mine_f[...] = mine[...].astype(F32)
    right_f[...] = gathered[...].astype(F32)

    def matrix(source, base, stride):
        rows = []
        for m in range(GROUPS):
            for x in range(4):
                rows.append(jnp.concatenate([
                    source[pl.ds(base + (x * 4 + zh) * 8 * stride + m, 8, stride=stride), :] for zh in range(4)
                ], axis=1))
        turned = nn_dot(jnp.concatenate(rows, axis=0).astype(BF16), swap)
        rows = []
        for q in range(4):
            for m in range(GROUPS):
                rows.append(jnp.concatenate([
                    turned[(m * 4 + x) * 8 : (m * 4 + x) * 8 + 8, q * 128 : q * 128 + 128] for x in range(4)
                ], axis=1))
        return jnp.concatenate(rows, axis=0).astype(BF16)

    left = matrix(mine_f, 0, 8)
    right = jnp.concatenate([matrix(right_f, g * 512, 4) for g in range(4)], axis=0)
    triangle = nt_dot(left, right).astype(BF16)
    code = lax.broadcasted_iota(jnp.int32, (CELLS, 1), 0)
    g, q, m, y = fields(code, 4, 4, 4, 8)
    from_token = token_of_row(y * 4 + g, m * 4 + q, -1)
    code = lax.broadcasted_iota(jnp.int32, (1, CELLS), 1)
    x, zh, b = fields(code, 4, 4, 32)
    to_token = token_of_col(x, zh, b, -2)
    triangle = nn_dot(triangle, one_hot(from_token, to_token))
    rows = []
    for m in range(GROUPS):
        for x in range(4):
            rows.append(jnp.concatenate([
                triangle[(q * 4 + m) * 8 : (q * 4 + m) * 8 + 8, x * 128 : x * 128 + 128] for q in range(4)
            ], axis=1))
    turned = nn_dot(jnp.concatenate(rows, axis=0).astype(BF16), swap)
    for m in range(GROUPS):
        for x in range(4):
            for zh in range(4):
                out_f[pl.ds((x * 4 + zh) * 32 + m, 8, stride=4), :] = turned[
                    (m * 4 + x) * 8 : (m * 4 + x) * 8 + 8, zh * 128 : zh * 128 + 128
                ]
    out_ref[...] = out_f[...].astype(BF16)


def incoming_kernel(mine, gathered, out_ref, mine_f, left_f, out_f):
    swap = swap_matrix()
    mine_f[...] = mine[...].astype(F32)
    left_f[...] = gathered[...].astype(F32)

    def stacked(source, base, stride):
        return jnp.concatenate([
            jnp.concatenate([
                source[pl.ds(base + zh * 32 * stride + m, 32, stride=stride), :] for zh in range(4)
            ], axis=1)
            for m in range(GROUPS)
        ], axis=0).astype(BF16)

    def tall(source, base, stride):
        turned = nn_dot(stacked(source, base, stride), swap)
        return jnp.concatenate([turned[:, q * 128 : q * 128 + 128] for q in range(4)], axis=0).astype(BF16)

    turned = nt_dot(swap, stacked(mine_f, 4, 8))
    right = jnp.concatenate([turned[q * 128 : q * 128 + 128] for q in range(4)], axis=1).astype(BF16)
    left = jnp.concatenate([tall(left_f, x * 512, 4) for x in range(4)], axis=1)
    triangle = nn_dot(right, left).astype(BF16)
    code = lax.broadcasted_iota(jnp.int32, (CELLS, 1), 0)
    q, m, row = fields(code, 4, 4, 32)
    to_token = token_of_row(row, m * 4 + q, -1)
    code = lax.broadcasted_iota(jnp.int32, (1, CELLS), 1)
    x, zh, b = fields(code, 4, 4, 32)
    from_token = token_of_col(x, zh, b, -2)
    triangle = nt_dot(one_hot(to_token, from_token), triangle)
    wide = jnp.concatenate([triangle[q * 128 : q * 128 + 128] for q in range(4)], axis=1).astype(BF16)
    turned = nn_dot(wide, swap)
    for m in range(GROUPS):
        for zh in range(4):
            out_f[pl.ds(zh * 128 + m, 32, stride=4), :] = turned[m * 32 : m * 32 + 32, zh * 128 : zh * 128 + 128]
    out_ref[...] = out_f[...].astype(BF16)


def call(kernel, outs, scratch, name, scalars=0):
    specs = [pl.BlockSpec(memory_space=pltpu.SMEM)] * scalars

    def run(*args):
        return pl.pallas_call(
            kernel,
            out_shape=outs,
            in_specs=specs + [pl.BlockSpec(memory_space=pltpu.VMEM)] * (len(args) - scalars),
            out_specs=jax.tree.map(lambda _: pl.BlockSpec(memory_space=pltpu.VMEM), outs),
            scratch_shapes=[pltpu.VMEM(shape, F32) for shape in scratch],
            compiler_params=pltpu.CompilerParams(vmem_limit_bytes=32 * 1024 * 1024),
            name=name,
        )(*args)

    return run


def exchange(array, axes):
    return lax.all_to_all(array, axes, 0, 0, tiled=True)


def on_device(pair_rep, chain_lengths, in_gain, in_bias, weight_in, out_gain, out_bias, weight_out):
    place = jnp.stack([lax.axis_index(ROW_AXES), lax.axis_index(COL_AXES)]).astype(jnp.int32)
    tile = jax.ShapeDtypeStruct((LANES, CELLS), F32)
    sent = jax.ShapeDtypeStruct((1024, LANES), BF16)
    returned = jax.ShapeDtypeStruct((512, LANES), BF16)
    norms = (in_gain, in_bias)
    ends = (out_gain, out_bias)

    send, gate, columns = call(
        first_kernel, (sent, tile, tile), [(CELLS, LANES), (1024, LANES)], "first", 2
    )(place, chain_lengths, pair_rep, *norms, weight_in, *ends)
    mine = exchange(send.reshape(128, 8, LANES), GROUP1)
    gathered = lax.all_gather(mine[:, 4:], ("zl", "core"), axis=0, tiled=True)
    back = call(
        outgoing_kernel, returned, [(1024, LANES), (2048, LANES), (512, LANES)], "outgoing"
    )(mine.reshape(1024, LANES), gathered.reshape(2048, LANES))
    back = exchange(back.reshape(128, 4, LANES), GROUP1)

    send, gate, columns = call(
        middle_kernel, (sent, tile, tile), [(512, LANES), (1024, LANES)], "middle", 2
    )(place, chain_lengths, back.reshape(512, LANES), gate, columns, *norms, weight_in, *ends, weight_out)
    mine = exchange(send.reshape(128, 8, LANES), GROUP2)
    own = mine[:, :4].reshape(1, 512, LANES)
    gathered = exchange(jnp.broadcast_to(own, (4, 512, LANES)), "x")
    back = call(
        incoming_kernel, returned, [(1024, LANES), (2048, LANES), (512, LANES)], "incoming"
    )(mine.reshape(1024, LANES), gathered.reshape(2048, LANES))
    back = exchange(back.reshape(128, 4, LANES), GROUP2)

    out = jax.ShapeDtypeStruct(pair_rep.shape, BF16)
    return call(last_kernel, out, [(512, LANES), (CELLS, LANES)], "last")(
        back.reshape(512, LANES), gate, columns, *norms, *ends, weight_out
    )


def solution(mesh):
    fine = Mesh(mesh.devices.reshape(8, 2, 2, 4, 4), ROW_AXES + COL_AXES)
    placed = P(ROW_AXES, COL_AXES, None)
    return jax.shard_map(
        on_device, mesh=fine, in_specs=(placed,) + (P(),) * 7, out_specs=placed, check_vma=False
    )
```

time: 746 us -> 125 us (0.17); the launches traced: 735 us -> 125 us
  waiting for transfers between devices: 655 us -> 0 us
  blocking collectives: 0 us -> 116 us
  local copies, waits for them, and re-layouts: 42.4 us -> 2.69 us
  matrix products: 14.7 us -> 0 us
  between operations: 13.7 us -> 0.09 us
  other arithmetic: 9.58 us -> 0.08 us
    psum x2 -> x0, waiting for transfers between devices: 399 us -> none  [spread(): return lax.psum(jnp.where(mine, shard, jnp.zeros_like(shard)), axis)]
    all_gather x4 -> x0, waiting for transfers between devices: 255 us -> none  [the longest x1 69.1 us: on_device(): lax.all_gather(left_proj, 'row', axis=0, tiled=True)]
    all_to_all x0 -> x5, blocking collectives: none -> 106 us  [exchange(): return lax.all_to_all(array, axes, 0, 0, tiled=True)]
    all_gather x3 -> x0, local copies, waits for them, and re-layouts: 29.8 us -> none  [the longest x1 22 us: on_device(): lax.all_gather(right_proj, 'row', axis=0, tiled=True)]
    dot_general x6 -> x0, matrix products: 14.7 us -> none  [the longest x1 7.17 us: on_device(): jnp.einsum('kih,kjh->ijh', left_panel, right_cols, preferred_element_type...]
    all_gather x0 -> x1, blocking collectives: none -> 9.83 us  [on_device(): gathered = lax.all_gather(mine[:, 4:], ('zl', 'core'), axis=0, tiled=True)]
  transfers between devices with their start and end apart: 6 -> 0, of which waited for: 6 -> 0; matrix products, arithmetic and copies ran while one was open for 6% -> 0% of each run, Pallas kernels for 0% -> 0%
where the time goes in v1:
time: 125 us
  blocking collectives  116 us (93%)
  Pallas kernels  6.15 us (5%)
  local copies, waits for them, and re-layouts  2.69 us (2%)
    all_to_all x5, blocking collectives, exchange(): return lax.all_to_all(array, axes, 0, 0, tiled=True)  106 us
    all_gather x1, blocking collectives, on_device(): gathered = lax.all_gather(mine[:, 4:], ('zl', 'core'), axis=0, tiled=True)  9.83 us
    pallas_call x5, Pallas kernels, run(): pl.pallas_call(kernel, out_shape=outs, in_specs=specs + [pl.BlockSpec(mem...  6.15 us
    unnamed x18, local copies, waits for them, and re-layouts  2.51 us

profile of v1, /device:TPU:1, one launch (start us, length us, event | category | flops | bytes accessed | tf_op | source)
XLA Modules:
  0.0 124.9 jit_solution(13861200804237282045)
XLA Ops:
  0.0 0.0 copy-start.7
  0.0 0.0 copy-start.5
  0.0 0.0 copy-start.6
  0.0 0.0 copy-start.4
  0.0 0.0 copy-start.8
  0.0 0.1 pad_add_fusion.place
  0.1 0.6 copy-done.7
  0.7 0.0 copy-done.5
  0.7 0.0 copy-done.6
  0.7 0.0 copy-done.4
  0.7 0.0 copy-done.8
  0.7 0.0 copy-start
  0.7 1.0 copy-done
  1.7 0.0 copy-start.3
  1.7 0.9 copy-done.3
  2.6 1.1 first.1
  3.8 35.2 %all_to_all.25 = bf16[128,8,128]{2,1,0:T(8,128)(2,1)S(1)} all-to-all(bf16[128,8,128]{2,1,0:T(8,128)(2,1)S(1)} %bitcast.22), channel_id=1, replica_groups=mesh['y'=8,'zl'=2,'core'=2,'x'=4,'zh'=4] {'x','zh','y'}, dimensions={0} | all-to-all | bytes 524288 | tf_op jit(solution)/shard_map/all_to_all | solution.py:257
  38.9 0.1 slice.8
  39.0 9.8 %all_gather.3 = bf16[512,4,128]{2,1,0:T(4,128)(2,1)S(1)} all-gather(bf16[128,4,128]{2,1,0:T(4,128)(2,1)S(1)} %slice.8), channel_id=1, replica_groups=mesh['y'=8,'zl'=2,'core'=2,'x'=4,'zh'=4] {'zl','core'}, dimensions={0}, use_global_device_ids=true | all-gather | bytes 655360 | tf_op jit(solution)/shard_map/all_gather | solution.py:272
  48.8 0.0 copy-start.1
  48.8 1.2 outgoing.1
  50.0 0.0 copy-start.2
  50.0 19.0 %all_to_all.26 = bf16[128,4,128]{2,1,0:T(4,128)(2,1)S(1)} all-to-all(bf16[128,4,128]{2,1,0:T(4,128)(2,1)S(1)} %bitcast.19), channel_id=1, replica_groups=mesh['y'=8,'zl'=2,'core'=2,'x'=4,'zh'=4] {'x','zh','y'}, dimensions={0} | all-to-all | bytes 262144 | tf_op jit(solution)/shard_map/all_to_all | solution.py:257
  69.1 0.0 copy-done.1
  69.1 0.0 copy-done.2
  69.1 1.3 %middle.1 = (bf16[1024,128]{1,0:T(8,128)(2,1)S(1)}, f32[128,512]{1,0:T(8,128)S(1)}, f32[128,512]{1,0:T(8,128)S(1)}) custom-call(s32[2]{0:T(128)S(1)} %pad_add_fusion.place, s32[4]{0:T(128)S(1)} %copy-done.8, bf16[512,128]{1,0:T(8,128)(2,1)S(1)} %bitcast.17, f32[128,512]{1,0:T(8,128)S(1)} %get-tuple-element.12.gate, ...), custom_call_target="tpu_custom_call" | custom-call | tf_op jit(solution)/shard_map/middle/pallas_call | solution.py:243
  70.4 20.8 %all_to_all.27 = bf16[128,8,128]{2,1,0:T(8,128)(2,1)S(1)} all-to-all(bf16[128,8,128]{2,1,0:T(8,128)(2,1)S(1)} %bitcast.21), channel_id=1, replica_groups=mesh['y'=8,'zl'=2,'core'=2,'x'=4,'zh'=4] {'zh','y','zl','core'}, dimensions={0} | all-to-all | bytes 524288 | tf_op jit(solution)/shard_map/all_to_all | solution.py:257
  91.2 0.1 broadcast_in_dim.8
  91.3 10.2 %all_to_all.28 = bf16[4,512,128]{2,1,0:T(8,128)(2,1)S(1)} all-to-all(bf16[4,512,128]{2,1,0:T(8,128)(2,1)S(1)} %broadcast_in_dim.8), channel_id=1, replica_groups=mesh['y'=8,'zl'=2,'core'=2,'x'=4,'zh'=4] {'x'}, dimensions={0} | all-to-all | bytes 1048576 | tf_op jit(solution)/shard_map/all_to_all | solution.py:257
  101.5 1.3 %incoming.1 = bf16[512,128]{1,0:T(8,128)(2,1)S(1)} custom-call(bf16[1024,128]{1,0:T(8,128)(2,1)S(1)} %bitcast.15, bf16[2048,128]{1,0:T(8,128)(2,1)S(1)} %bitcast.14), custom_call_target="tpu_custom_call" | custom-call | tf_op jit(solution)/shard_map/incoming/pallas_call | solution.py:243
  102.9 20.9 %all_to_all.29 = bf16[128,4,128]{2,1,0:T(4,128)(2,1)S(1)} all-to-all(bf16[128,4,128]{2,1,0:T(4,128)(2,1)S(1)} %bitcast.20), channel_id=1, replica_groups=mesh['y'=8,'zl'=2,'core'=2,'x'=4,'zh'=4] {'zh','y','zl','core'}, dimensions={0} | all-to-all | bytes 262144 | tf_op jit(solution)/shard_map/all_to_all | solution.py:257
  123.7 1.1 last.1
  (1 shorter events, 0.0 us)
Async XLA Ops:
  0.0 0.7 copy-start.7
  0.0 0.7 copy-start.5
  0.0 0.7 copy-start.6
  0.0 0.7 copy-start.4
  0.0 0.7 copy-start.8
  0.7 1.0 copy-start
  1.7 0.9 copy-start.3
  48.8 20.3 %copy-start.1 = (bf16[2,128,640]{2,1,0:T(8,128)(2,1)S(1)}, bf16[2,128,640]{2,1,0:T(8,128)(2,1)}, u32[]{:S(2)}) copy-start(bf16[2,128,640]{2,1,0:T(8,128)(2,1)} %weight.3) | copy-start | bytes 983044
  50.0 19.0 %copy-start.2 = (bf16[2,128,128]{2,1,0:T(8,128)(2,1)S(1)}, bf16[2,128,128]{2,1,0:T(8,128)(2,1)}, u32[]{:S(2)}) copy-start(bf16[2,128,128]{2,1,0:T(8,128)(2,1)} %weight_out.3) | copy-start | bytes 196612

commit v2 on v1

--- a/solution.py
+++ b/solution.py
@@ -20,8 +20,8 @@
 
 ROW_AXES = ("y", "zl", "core")
 COL_AXES = ("x", "zh")
-GROUP1 = ("x", "zh", "y")
-GROUP2 = ("zh",) + ROW_AXES
+GROUP1 = ("x", "y", "zh")
+GROUP2 = ("zl", "core", "zh", "y")
 
 
 def nt_dot(left, right):
@@ -107,17 +107,27 @@
 
 
 def first_kernel(
-    place, lengths, pair, in_gain, in_bias, weight, out_gain, out_bias,
-    send_ref, gate_ref, columns_ref, cells, send,
+    place, lengths_hbm, pair_hbm, gain_hbm, bias_hbm, weight_hbm,
+    send_ref, gate_ref, columns_ref, cells, send, lengths, pair, gain, bias, weight, sems,
 ):
-    vectors = turn_vectors(in_gain, in_bias, out_gain, out_bias)
+    copies = [
+        pltpu.make_async_copy(source, target, sems.at[at])
+        for at, (source, target) in enumerate((
+            (pair_hbm, pair), (weight_hbm.at[0], weight), (gain_hbm, gain), (bias_hbm, bias), (lengths_hbm, lengths),
+        ))
+    ]
+    for copy in copies:
+        copy.start()
     cells[...] = jnp.zeros_like(cells)
+    for copy in copies:
+        copy.wait()
+    mask = cell_mask(place, lengths)
+    vectors = jnp.concatenate([gain[...], bias[...], gain[...], bias[...]], axis=0).T
     for a in range(ROWS):
         cells[pl.ds(a * WIDE, COLS), :] = pair[a].astype(F32)
     columns = cells[...].T
     columns_ref[...] = columns
-    mask = cell_mask(place, lengths)
-    project(columns, mask, vectors[:, 0:1], vectors[:, 2:3], weight[0], send, send_ref, gate_ref)
+    project(columns, mask, vectors[:, 0:1], vectors[:, 2:3], weight[...], send, send_ref, gate_ref)
 
 
 def finish(back, update, gate, columns, vectors, weight_out, got):
@@ -163,7 +173,7 @@
         for m in range(GROUPS):
             for x in range(4):
                 rows.append(jnp.concatenate([
-                    source[pl.ds(base + (x * 4 + zh) * 8 * stride + m, 8, stride=stride), :] for zh in range(4)
+                    source[pl.ds(base + (x * 32 + zh) * stride + m, 8, stride=4 * stride), :] for zh in range(4)
                 ], axis=1))
         turned = nn_dot(jnp.concatenate(rows, axis=0).astype(BF16), swap)
         rows = []
@@ -194,7 +204,7 @@
     for m in range(GROUPS):
         for x in range(4):
             for zh in range(4):
-                out_f[pl.ds((x * 4 + zh) * 32 + m, 8, stride=4), :] = turned[
+                out_f[pl.ds((x * 32 + zh) * 4 + m, 8, stride=16), :] = turned[
                     (m * 4 + x) * 8 : (m * 4 + x) * 8 + 8, zh * 128 : zh * 128 + 128
                 ]
     out_ref[...] = out_f[...].astype(BF16)
@@ -208,9 +218,9 @@
     def stacked(source, base, stride):
         return jnp.concatenate([
             jnp.concatenate([
-                source[pl.ds(base + zh * 32 * stride + m, 32, stride=stride), :] for zh in range(4)
+                source[pl.ds(base + (g * 32 + zh * 8) * stride + m, 8, stride=stride), :] for zh in range(4)
             ], axis=1)
-            for m in range(GROUPS)
+            for m in range(GROUPS) for g in range(4)
         ], axis=0).astype(BF16)
 
     def tall(source, base, stride):
@@ -222,8 +232,8 @@
     left = jnp.concatenate([tall(left_f, x * 512, 4) for x in range(4)], axis=1)
     triangle = nn_dot(right, left).astype(BF16)
     code = lax.broadcasted_iota(jnp.int32, (CELLS, 1), 0)
-    q, m, row = fields(code, 4, 4, 32)
-    to_token = token_of_row(row, m * 4 + q, -1)
+    q, m, g, y = fields(code, 4, 4, 4, 8)
+    to_token = token_of_row(y * 4 + g, m * 4 + q, -1)
     code = lax.broadcasted_iota(jnp.int32, (1, CELLS), 1)
     x, zh, b = fields(code, 4, 4, 32)
     from_token = token_of_col(x, zh, b, -2)
@@ -231,26 +241,33 @@
     wide = jnp.concatenate([triangle[q * 128 : q * 128 + 128] for q in range(4)], axis=1).astype(BF16)
     turned = nn_dot(wide, swap)
     for m in range(GROUPS):
-        for zh in range(4):
-            out_f[pl.ds(zh * 128 + m, 32, stride=4), :] = turned[m * 32 : m * 32 + 32, zh * 128 : zh * 128 + 128]
+        for g in range(4):
+            for zh in range(4):
+                out_f[pl.ds((g * 32 + zh * 8) * 4 + m, 8, stride=4), :] = turned[
+                    (m * 4 + g) * 8 : (m * 4 + g) * 8 + 8, zh * 128 : zh * 128 + 128
+                ]
     out_ref[...] = out_f[...].astype(BF16)
 
 
-def call(kernel, outs, scratch, name, scalars=0):
+def call(kernel, outs, scratch, name, scalars=0, space=pltpu.VMEM, more=()):
     specs = [pl.BlockSpec(memory_space=pltpu.SMEM)] * scalars
 
     def run(*args):
         return pl.pallas_call(
             kernel,
             out_shape=outs,
-            in_specs=specs + [pl.BlockSpec(memory_space=pltpu.VMEM)] * (len(args) - scalars),
+            in_specs=specs + [pl.BlockSpec(memory_space=space)] * (len(args) - scalars),
             out_specs=jax.tree.map(lambda _: pl.BlockSpec(memory_space=pltpu.VMEM), outs),
-            scratch_shapes=[pltpu.VMEM(shape, F32) for shape in scratch],
+            scratch_shapes=[pltpu.VMEM(shape, F32) for shape in scratch] + list(more),
             compiler_params=pltpu.CompilerParams(vmem_limit_bytes=32 * 1024 * 1024),
             name=name,
         )(*args)
 
     return run
+
+
+def in_hbm(array):
+    return pltpu.with_memory_space_constraint(array, pltpu.HBM)
 
 
 def exchange(array, axes):
@@ -266,8 +283,13 @@
     ends = (out_gain, out_bias)
 
     send, gate, columns = call(
-        first_kernel, (sent, tile, tile), [(CELLS, LANES), (1024, LANES)], "first", 2
-    )(place, chain_lengths, pair_rep, *norms, weight_in, *ends)
+        first_kernel, (sent, tile, tile), [(CELLS, LANES), (1024, LANES)], "first", 1, pltpu.HBM,
+        [
+            pltpu.SMEM(chain_lengths.shape, jnp.int32),
+            pltpu.VMEM(pair_rep.shape, BF16), pltpu.VMEM(in_gain.shape, F32), pltpu.VMEM(in_bias.shape, F32),
+            pltpu.VMEM(weight_in.shape[1:], BF16), pltpu.SemaphoreType.DMA((5,)),
+        ],
+    )(place, *(in_hbm(array) for array in (chain_lengths, pair_rep, *norms, weight_in)))
     mine = exchange(send.reshape(128, 8, LANES), GROUP1)
     gathered = lax.all_gather(mine[:, 4:], ("zl", "core"), axis=0, tiled=True)
     back = call(

time: 125 us -> 125 us (level)
  local copies, waits for them, and re-layouts: 2.69 us -> 0.85 us
    unnamed x18 -> x14, local copies, waits for them, and re-layouts: 2.51 us -> 0.67 us
where the time goes in v2:
time: 125 us
  blocking collectives  116 us (93%)
  Pallas kernels  7.39 us (6%)
    all_to_all x5, blocking collectives, exchange(): return lax.all_to_all(array, axes, 0, 0, tiled=True)  106 us
    all_gather x1, blocking collectives, on_device(): gathered = lax.all_gather(mine[:, 4:], ('zl', 'core'), axis=0, tiled=True)  10.1 us
    pallas_call x5, Pallas kernels, run(): pl.pallas_call(kernel, out_shape=outs, in_specs=specs + [pl.BlockSpec(mem...  7.39 us

profile of v2, /device:TPU:1, one launch (start us, length us, event | category | flops | bytes accessed | tf_op | source)
XLA Modules:
  0.0 124.7 jit_solution(10693250099733591401)
XLA Ops:
  0.0 0.1 pad_add_fusion.place
  0.1 2.2 %first.1 = (bf16[1024,128]{1,0:T(8,128)(2,1)S(1)}, f32[128,512]{1,0:T(8,128)S(1)}, f32[128,512]{1,0:T(8,128)S(1)}) custom-call(s32[2]{0:T(128)S(1)} %pad_add_fusion.place, s32[4]{0:T(128)} %lengths.1, bf16[14,28,128]{2,1,0:T(8,128)(2,1)} %pair_hbm.1, f32[2,128]{1,0:T(2,128)} %in_gain.3, f32[2,128]{1,0:T(2,128)} %in_bias.3, bf16[2,128,640]{2,1,0:T(8,128)(2,1)} %weight.1), custom_call_target="tpu_custom_call" | custom-call | tf_op jit(solution)/shard_map/first/pallas_call | solution.py:256
  2.3 35.4 %all_to_all.25 = bf16[128,8,128]{2,1,0:T(8,128)(2,1)S(1)} all-to-all(bf16[128,8,128]{2,1,0:T(8,128)(2,1)S(1)} %bitcast.22), channel_id=1, replica_groups=mesh['y'=8,'zl'=2,'core'=2,'x'=4,'zh'=4] {'x','y','zh'}, dimensions={0} | all-to-all | bytes 524288 | tf_op jit(solution)/shard_map/all_to_all | solution.py:274
  37.6 0.1 slice.8
  37.7 10.1 %all_gather.3 = bf16[512,4,128]{2,1,0:T(4,128)(2,1)S(1)} all-gather(bf16[128,4,128]{2,1,0:T(4,128)(2,1)S(1)} %slice.8), channel_id=1, replica_groups=mesh['y'=8,'zl'=2,'core'=2,'x'=4,'zh'=4] {'zl','core'}, dimensions={0}, use_global_device_ids=true | all-gather | bytes 655360 | tf_op jit(solution)/shard_map/all_gather | solution.py:294
  47.8 0.0 copy-start
  47.8 1.4 %outgoing.1 = bf16[512,128]{1,0:T(8,128)(2,1)S(1)} custom-call(bf16[1024,128]{1,0:T(8,128)(2,1)S(1)} %bitcast.16, bf16[2048,128]{1,0:T(8,128)(2,1)S(1)} %bitcast.13), custom_call_target="tpu_custom_call" | custom-call | tf_op jit(solution)/shard_map/outgoing/pallas_call | solution.py:256
  49.3 0.0 copy-start.1
  49.3 0.0 copy-start.3
  49.3 0.0 copy-start.4
  49.3 0.0 copy-start.5
  49.3 19.6 %all_to_all.26 = bf16[128,4,128]{2,1,0:T(4,128)(2,1)S(1)} all-to-all(bf16[128,4,128]{2,1,0:T(4,128)(2,1)S(1)} %bitcast.19), channel_id=1, replica_groups=mesh['y'=8,'zl'=2,'core'=2,'x'=4,'zh'=4] {'x','y','zh'}, dimensions={0} | all-to-all | bytes 262144 | tf_op jit(solution)/shard_map/all_to_all | solution.py:274
  68.9 0.0 copy-start.2
  68.9 0.0 copy-start.6
  68.9 0.0 copy-done
  68.9 0.0 copy-done.1
  68.9 0.0 copy-done.3
  68.9 0.0 copy-done.4
  68.9 0.0 copy-done.5
  68.9 0.6 copy-done.2
  69.5 0.0 copy-done.6
  69.5 1.3 %middle.1 = (bf16[1024,128]{1,0:T(8,128)(2,1)S(1)}, f32[128,512]{1,0:T(8,128)S(1)}, f32[128,512]{1,0:T(8,128)S(1)}) custom-call(s32[2]{0:T(128)S(1)} %pad_add_fusion.place, s32[4]{0:T(128)S(1)} %copy-done.6, bf16[512,128]{1,0:T(8,128)(2,1)S(1)} %bitcast.17, f32[128,512]{1,0:T(8,128)S(1)} %get-tuple-element.12.gate, ...), custom_call_target="tpu_custom_call" | custom-call | tf_op jit(solution)/shard_map/middle/pallas_call | solution.py:256
  70.9 20.6 %all_to_all.27 = bf16[128,8,128]{2,1,0:T(8,128)(2,1)S(1)} all-to-all(bf16[128,8,128]{2,1,0:T(8,128)(2,1)S(1)} %bitcast.21), channel_id=1, replica_groups=mesh['y'=8,'zl'=2,'core'=2,'x'=4,'zh'=4] {'zl','core','zh','y'}, dimensions={0} | all-to-all | bytes 524288 | tf_op jit(solution)/shard_map/all_to_all | solution.py:274
  91.6 0.1 broadcast_in_dim.8
  91.6 11.6 %all_to_all.28 = bf16[4,512,128]{2,1,0:T(8,128)(2,1)S(1)} all-to-all(bf16[4,512,128]{2,1,0:T(8,128)(2,1)S(1)} %broadcast_in_dim.8), channel_id=1, replica_groups=mesh['y'=8,'zl'=2,'core'=2,'x'=4,'zh'=4] {'x'}, dimensions={0} | all-to-all | bytes 1048576 | tf_op jit(solution)/shard_map/all_to_all | solution.py:274
  103.2 1.3 %incoming.1 = bf16[512,128]{1,0:T(8,128)(2,1)S(1)} custom-call(bf16[1024,128]{1,0:T(8,128)(2,1)S(1)} %bitcast.15, bf16[2048,128]{1,0:T(8,128)(2,1)S(1)} %bitcast.14), custom_call_target="tpu_custom_call" | custom-call | tf_op jit(solution)/shard_map/incoming/pallas_call | solution.py:256
  104.6 19.0 %all_to_all.29 = bf16[128,4,128]{2,1,0:T(4,128)(2,1)S(1)} all-to-all(bf16[128,4,128]{2,1,0:T(4,128)(2,1)S(1)} %bitcast.20), channel_id=1, replica_groups=mesh['y'=8,'zl'=2,'core'=2,'x'=4,'zh'=4] {'zl','core','zh','y'}, dimensions={0} | all-to-all | bytes 262144 | tf_op jit(solution)/shard_map/all_to_all | solution.py:274
  123.5 1.1 last.1
  (1 shorter events, 0.0 us)
Async XLA Ops:
  47.8 21.0 %copy-start = (bf16[2,128,640]{2,1,0:T(8,128)(2,1)S(1)}, bf16[2,128,640]{2,1,0:T(8,128)(2,1)}, u32[]{:S(2)}) copy-start(bf16[2,128,640]{2,1,0:T(8,128)(2,1)} %weight.1) | copy-start | bytes 983044
  49.3 19.6 %copy-start.1 = (bf16[2,128,128]{2,1,0:T(8,128)(2,1)S(1)}, bf16[2,128,128]{2,1,0:T(8,128)(2,1)}, u32[]{:S(2)}) copy-start(bf16[2,128,128]{2,1,0:T(8,128)(2,1)} %weight_out.3) | copy-start | bytes 196612
  49.3 19.6 %copy-start.3 = (f32[2,128]{1,0:T(2,128)S(1)}, f32[2,128]{1,0:T(2,128)}, u32[]{:S(2)}) copy-start(f32[2,128]{1,0:T(2,128)} %in_bias.3) | copy-start | bytes 3076
  49.3 19.6 %copy-start.4 = (f32[2,128]{1,0:T(2,128)S(1)}, f32[2,128]{1,0:T(2,128)}, u32[]{:S(2)}) copy-start(f32[2,128]{1,0:T(2,128)} %out_gain.3) | copy-start | bytes 3076
  49.3 19.6 %copy-start.5 = (f32[2,128]{1,0:T(2,128)S(1)}, f32[2,128]{1,0:T(2,128)}, u32[]{:S(2)}) copy-start(f32[2,128]{1,0:T(2,128)} %out_bias.3) | copy-start | bytes 3076
  68.9 0.7 copy-start.2
  68.9 0.7 copy-start.6

commit v3 on v2

v3 whole, which is shorter than its diff:
```python
import jax
import jax.numpy as jnp
from jax import lax
from jax.experimental import pallas as pl
from jax.experimental.pallas import tpu as pltpu
from jax.sharding import Mesh, PartitionSpec as P

EPSILON = 1e-05
F32 = jnp.float32
BF16 = jnp.bfloat16

ROWS = 14
COLS = 28
WIDE = 32
CELLS = 512
GROUPS = 4
LANES = 128
SLOT = 112
CHAINS = 4

ROW_AXES = ("y", "zl", "core")
COL_AXES = ("xh", "xl", "zh")
GROUP1 = ("zl", "xl", "zh", "y")
GROUP2 = ("xh", "xl", "zh", "y")
BACK = ("zl", "zh", "y", "xh", "xl")


def nt_dot(left, right):
    return lax.dot_general(left, right, (((1,), (1,)), ((), ())), preferred_element_type=F32)


def tn_dot(left, right):
    return lax.dot_general(left, right, (((0,), (0,)), ((), ())), preferred_element_type=F32)


def nn_dot(left, right):
    return jnp.dot(left, right, preferred_element_type=F32)


def norm_rows(values, gain, bias):
    average = jnp.mean(values, axis=0, keepdims=True)
    centered = values - average
    variance = jnp.mean(centered * centered, axis=0, keepdims=True)
    return (centered * lax.rsqrt(variance + EPSILON) * gain + bias).astype(BF16)


def one_hot(row_code, col_code):
    return (row_code == col_code).astype(F32).astype(BF16)


def swap_matrix():
    row = lax.broadcasted_iota(jnp.int32, (CELLS, 1), 0)
    col = lax.broadcasted_iota(jnp.int32, (1, CELLS), 1)
    swapped = ((col >> 5) & 3) * 128 + (col >> 7) * 32 + (col & 31)
    return one_hot(row, swapped)


def fields(code, *widths):
    out = []
    for width in reversed(widths):
        out.append(code & (width - 1))
        code = code >> (width.bit_length() - 1)
    return out[::-1]


def token_of_row(row, a, skip):
    return jnp.where(a < ROWS, row * ROWS + a, skip)


def token_of_col(x, zh, b, skip):
    return jnp.where(b < COLS, x * SLOT + zh * COLS + b, skip)


def valid_token(token, lengths_ref):
    valid = jnp.zeros(token.shape, jnp.bool_)
    for chain in range(CHAINS):
        start = chain * SLOT
        valid = valid | ((token >= start) & (token < start + lengths_ref[chain]))
    return valid


def cell_mask(place_ref, lengths_ref):
    lane = lax.broadcasted_iota(jnp.int32, (1, CELLS), 1)
    a, b = lane >> 5, lane & 31
    row = valid_token(place_ref[0] * ROWS + a, lengths_ref)
    col = valid_token(place_ref[1] * COLS + b, lengths_ref)
    inside = (a < ROWS) & (b < COLS)
    return jnp.where(row & col & inside, 1.0, 0.0).astype(F32)


def project(columns, mask, gain, bias, weight, send, send_ref, gate_ref):
    for m in range(GROUPS):
        lanes = slice(m * LANES, (m + 1) * LANES)
        normed = norm_rows(columns[:, lanes], gain, bias)
        projected = tn_dot(weight, normed)
        weighting = mask[:, lanes]
        left = weighting * jax.nn.sigmoid(projected[128:256]) * projected[0:128]
        right = weighting * jax.nn.sigmoid(projected[384:512]) * projected[256:384]
        send[pl.ds(m, 128, stride=8), :] = left
        send[pl.ds(4 + m, 128, stride=8), :] = right
        gate_ref[:, lanes] = jax.nn.sigmoid(projected[512:640])
    send_ref[...] = send[...].astype(BF16)


def first_kernel(
    place, lengths_hbm, pair_hbm, in_gain_hbm, in_bias_hbm, weight_hbm, out_gain_hbm, out_bias_hbm,
    send_ref, gate_ref, columns_ref, vectors_ref, cells, send, norms, lengths, pair, in_gain, in_bias, out_gain, out_bias, weight, sems,
):
    copies = [
        pltpu.make_async_copy(source, target, sems.at[at])
        for at, (source, target) in enumerate((
            (pair_hbm, pair), (weight_hbm.at[0], weight), (in_gain_hbm, in_gain), (in_bias_hbm, in_bias),
            (out_gain_hbm, out_gain), (out_bias_hbm, out_bias), (lengths_hbm, lengths),
        ))
    ]
    for copy in copies:
        copy.start()
    cells[...] = jnp.zeros_like(cells)
    norms[...] = jnp.zeros_like(norms)
    for copy in copies:
        copy.wait()
    mask = cell_mask(place, lengths)
    for at, pair_of in enumerate((in_gain, in_bias, out_gain, out_bias)):
        norms[pl.ds(2 * at, 2), :] = pair_of[...]
    vectors = norms[...].T
    vectors_ref[...] = vectors
    for a in range(ROWS):
        cells[pl.ds(a * WIDE, COLS), :] = pair[a].astype(F32)
    columns = cells[...].T
    columns_ref[...] = columns
    project(columns, mask, vectors[:, 0:1], vectors[:, 2:3], weight[...], send, send_ref, gate_ref)


def finish(home, source_rows, gain, bias, gate, columns, weight_out, got):
    got[...] = home[...].astype(F32)
    parts = []
    for m in range(GROUPS):
        lanes = slice(m * LANES, (m + 1) * LANES)
        triangle = source_rows(got, 0, m) + source_rows(got, 1, m)
        change = tn_dot(weight_out, norm_rows(triangle, gain, bias))
        parts.append(columns[:, lanes] + gate[:, lanes] * change)
    return jnp.concatenate(parts, axis=1).astype(BF16)


def rows_after_first(got, xh, m):
    return jnp.concatenate([
        got[pl.ds(zl * 512 + xh * 8 + xl * 4 + m, 32, stride=16), :] for zl in range(2) for xl in range(2)
    ], axis=0)


def rows_after_second(got, zl, m):
    return jnp.concatenate([got[pl.ds(zl * 512 + x * 4 + m, 32, stride=16), :] for x in range(4)], axis=0)


def middle_kernel(
    place, lengths, home, gate, columns, vectors, weight, weight_out, send_ref, gate_ref, columns_ref, got, send
):
    middle = finish(
        home, rows_after_first, vectors[:, 4:5], vectors[:, 6:7], gate, columns, weight_out[0], got
    ).astype(F32)
    columns_ref[...] = middle
    mask = cell_mask(place, lengths)
    project(middle, mask, vectors[:, 1:2], vectors[:, 3:4], weight[1], send, send_ref, gate_ref)


def last_kernel(home, gate, columns, vectors, weight_out, out_ref, got, cells):
    updated = finish(
        home, rows_after_second, vectors[:, 5:6], vectors[:, 7:8], gate, columns, weight_out[1], got
    ).astype(F32)
    cells[...] = updated.T
    for a in range(ROWS):
        out_ref[a] = cells[pl.ds(a * WIDE, COLS), :].astype(BF16)


def group_lanes(rows, swap):
    return nn_dot(jnp.concatenate(rows, axis=0).astype(BF16), swap)


def send_home(triangle, swap, out_ref, out_f):
    rows = []
    for m in range(GROUPS):
        for zl in range(2):
            for x in range(4):
                rows.append(jnp.concatenate([
                    triangle[((q * 4 + m) * 2 + zl) * 8 : ((q * 4 + m) * 2 + zl) * 8 + 8, x * 128 : x * 128 + 128]
                    for q in range(4)
                ], axis=1))
    turned = group_lanes(rows, swap)
    for m in range(GROUPS):
        for zl in range(2):
            for x in range(4):
                at = ((m * 2 + zl) * 4 + x) * 8
                for zh in range(4):
                    out_f[pl.ds((zl * 4 + zh) * 128 + x * 4 + m, 8, stride=16), :] = turned[
                        at : at + 8, zh * 128 : zh * 128 + 128
                    ]
    out_ref[...] = out_f[...].astype(BF16)


def outgoing_kernel(mine, both, out_ref, mine_f, both_f, out_f):
    swap = swap_matrix()
    mine_f[...] = mine[...].astype(F32)
    both_f[...] = both[...].astype(F32)

    def matrix(source, base):
        turned = group_lanes([
            jnp.concatenate([
                source[pl.ds(base + ((zl * 2 + xl) * 4 + zh) * 64 + m, 8, stride=8), :] for zh in range(4)
            ], axis=1)
            for m in range(GROUPS) for zl in range(2) for xl in range(2)
        ], swap)
        rows = []
        for q in range(4):
            for m in range(GROUPS):
                for zl in range(2):
                    rows.append(jnp.concatenate([
                        turned[((m * 2 + zl) * 2 + xl) * 8 : ((m * 2 + zl) * 2 + xl) * 8 + 8, q * 128 : q * 128 + 128]
                        for xl in range(2)
                    ], axis=1))
        return jnp.concatenate(rows, axis=0).astype(BF16)

    left = matrix(mine_f, 0)
    right = jnp.concatenate([matrix(both_f, core * 1024 + 4) for core in range(2)], axis=0)
    triangle = nt_dot(left, right).astype(BF16)
    code = lax.broadcasted_iota(jnp.int32, (CELLS, 1), 0)
    core, q, m, zl, y = fields(code, 2, 4, 4, 2, 8)
    from_token = token_of_row(y * 4 + zl * 2 + core, m * 4 + q, -1)
    code = lax.broadcasted_iota(jnp.int32, (1, CELLS), 1)
    x, zh, b = fields(code, 4, 4, 32)
    to_token = token_of_col(x, zh, b, -2)
    send_home(nn_dot(triangle, one_hot(from_token, to_token)), swap, out_ref, out_f)


def incoming_kernel(place, both, out_ref, both_f, out_f):
    swap = swap_matrix()
    both_f[...] = both[...].astype(F32)

    def matrix(base):
        turned = group_lanes([
            jnp.concatenate([
                both_f[pl.ds(base + core * 1024 + (x * 4 + zh) * 64 + m, 8, stride=8), :] for zh in range(4)
            ], axis=1)
            for m in range(GROUPS) for core in range(2) for x in range(4)
        ], swap)
        rows = []
        for q in range(4):
            for m in range(GROUPS):
                for core in range(2):
                    rows.append(jnp.concatenate([
                        turned[((m * 2 + core) * 4 + x) * 8 : ((m * 2 + core) * 4 + x) * 8 + 8, q * 128 : q * 128 + 128]
                        for x in range(4)
                    ], axis=1))
        return jnp.concatenate(rows, axis=0).astype(BF16)

    code = lax.broadcasted_iota(jnp.int32, (CELLS // 2, 1), 0)
    q, m, zl, y = fields(code, 4, 4, 2, 8)
    to_token = token_of_row(y * 4 + zl * 2 + (place[0] & 1), m * 4 + q, -1)
    code = lax.broadcasted_iota(jnp.int32, (1, CELLS), 1)
    x, zh, b = fields(code, 4, 4, 32)
    from_token = token_of_col(x, zh, b, -2)
    left = nt_dot(one_hot(to_token, from_token), matrix(0)).astype(BF16)
    send_home(nn_dot(left, matrix(4)).astype(BF16).astype(F32), swap, out_ref, out_f)


def call(kernel, outs, scratch, name, scalars=0, space=pltpu.VMEM, more=()):
    specs = [pl.BlockSpec(memory_space=pltpu.SMEM)] * scalars

    def run(*args):
        return pl.pallas_call(
            kernel,
            out_shape=outs,
            in_specs=specs + [pl.BlockSpec(memory_space=space)] * (len(args) - scalars),
            out_specs=jax.tree.map(lambda _: pl.BlockSpec(memory_space=pltpu.VMEM), outs),
            scratch_shapes=[pltpu.VMEM(shape, F32) for shape in scratch] + list(more),
            compiler_params=pltpu.CompilerParams(vmem_limit_bytes=32 * 1024 * 1024),
            name=name,
        )(*args)

    return run


def in_hbm(array):
    return pltpu.with_memory_space_constraint(array, pltpu.HBM)


def exchange(array, axes):
    return lax.all_to_all(array, axes, 0, 0, tiled=True)


def on_device(pair_rep, chain_lengths, in_gain, in_bias, weight_in, out_gain, out_bias, weight_out):
    place = jnp.stack([lax.axis_index(ROW_AXES), lax.axis_index(COL_AXES)]).astype(jnp.int32)
    tile = jax.ShapeDtypeStruct((LANES, CELLS), F32)
    sent = jax.ShapeDtypeStruct((1024, LANES), BF16)

    send, gate, columns, vectors = call(
        first_kernel, (sent, tile, tile, jax.ShapeDtypeStruct((LANES, 8), F32)),
        [(CELLS, LANES), (1024, LANES), (8, LANES)], "first", 1, pltpu.HBM,
        [
            pltpu.SMEM(chain_lengths.shape, jnp.int32), pltpu.VMEM(pair_rep.shape, BF16),
            pltpu.VMEM(in_gain.shape, F32), pltpu.VMEM(in_bias.shape, F32),
            pltpu.VMEM(out_gain.shape, F32), pltpu.VMEM(out_bias.shape, F32),
            pltpu.VMEM(weight_in.shape[1:], BF16), pltpu.SemaphoreType.DMA((7,)),
        ],
    )(place, *map(in_hbm, (chain_lengths, pair_rep, in_gain, in_bias, weight_in, out_gain, out_bias)))
    mine = exchange(send.reshape(128, 8, LANES), GROUP1).reshape(1024, LANES)
    both = lax.all_gather(mine, "core", axis=0, tiled=True)
    home = call(
        outgoing_kernel, sent, [(1024, LANES), (2048, LANES), (1024, LANES)], "outgoing"
    )(mine, both)
    home = exchange(home.reshape(256, 4, LANES), BACK).reshape(1024, LANES)

    send, gate, columns = call(
        middle_kernel, (sent, tile, tile), [(1024, LANES), (1024, LANES)], "middle", 2
    )(place, chain_lengths, home, gate, columns, vectors, weight_in, weight_out)
    mine = exchange(send.reshape(128, 8, LANES), GROUP2).reshape(1024, LANES)
    both = lax.all_gather(mine, "core", axis=0, tiled=True)
    home = call(
        incoming_kernel, sent, [(2048, LANES), (1024, LANES)], "incoming", 1
    )(place, both)
    home = exchange(home.reshape(256, 4, LANES), BACK).reshape(1024, LANES)

    out = jax.ShapeDtypeStruct(pair_rep.shape, BF16)
    return call(last_kernel, out, [(1024, LANES), (CELLS, LANES)], "last")(home, gate, columns, vectors, weight_out)


def solution(mesh):
    fine = Mesh(mesh.devices.reshape(8, 2, 2, 2, 2, 4), ROW_AXES + COL_AXES)
    placed = P(ROW_AXES, COL_AXES, None)
    return jax.shard_map(
        on_device, mesh=fine, in_specs=(placed,) + (P(),) * 7, out_specs=placed, check_vma=False
    )
```

time: 125 us -> 119 us (0.952)
  blocking collectives: 116 us -> 109 us
    all_to_all x5 -> x4, blocking collectives: 106 us -> 99.2 us  [exchange(): return lax.all_to_all(array, axes, 0, 0, tiled=True)]
    all_gather x1 -> x2, blocking collectives: 10.1 us -> 10.3 us  [on_device(): both = lax.all_gather(mine, 'core', axis=0, tiled=True)]
where the time goes in v3:
time: 119 us; the launch traced here: 118 us
  blocking collectives  109 us (92%)
  Pallas kernels  8.06 us (7%)
    all_to_all x4, blocking collectives, exchange(): return lax.all_to_all(array, axes, 0, 0, tiled=True)  99.2 us
    all_gather x2, blocking collectives, on_device(): both = lax.all_gather(mine, 'core', axis=0, tiled=True)  10.3 us
    pallas_call x5, Pallas kernels, run(): pl.pallas_call(kernel, out_shape=outs, in_specs=specs + [pl.BlockSpec(mem...  8.06 us

profile of v3, /device:TPU:1, one launch (start us, length us, event | category | flops | bytes accessed | tf_op | source)
XLA Modules:
  0.0 118.3 jit_solution(11999068258457347336)
XLA Ops:
  0.0 0.1 pad_add_fusion.place
  0.1 2.2 %first.1 = (bf16[1024,128]{1,0:T(8,128)(2,1)S(1)}, f32[128,512]{1,0:T(8,128)S(1)}, f32[128,512]{1,0:T(8,128)S(1)}, f32[128,8]{1,0:T(8,128)S(1)}) custom-call(s32[2]{0:T(128)S(1)} %pad_add_fusion.place, s32[4]{0:T(128)} %lengths.1, bf16[14,28,128]{2,1,0:T(8,128)(2,1)} %pair_hbm.1, f32[2,128]{1,0:T(2,128)} %in_gain_hbm.1, f32[2,128]{1,0:T(2,128)} %in_bias_hbm.1, ...), custom_call_target="tpu_custom_call" | custom-call | tf_op jit(solution)/shard_map/first/pallas_call | solution.py:269
  2.3 31.6 %all_to_all.20 = bf16[128,8,128]{2,1,0:T(8,128)(2,1)S(1)} all-to-all(bf16[128,8,128]{2,1,0:T(8,128)(2,1)S(1)} %bitcast.17), channel_id=1, replica_groups=mesh['y'=8,'zl'=2,'core'=2,'xh'=2,'xl'=2,'zh'=4] {'zl','xl','zh','y'}, dimensions={0} | all-to-all | bytes 524288 | tf_op jit(solution)/shard_map/all_to_all | solution.py:287
  33.9 5.1 %all_gather.6.both = bf16[2048,128]{1,0:T(8,128)(2,1)S(1)} all-gather(bf16[1024,128]{1,0:T(8,128)(2,1)S(1)} %bitcast.10), channel_id=1, replica_groups=mesh['y'=8,'zl'=2,'core'=2,'xh'=2,'xl'=2,'zh'=4] {'core'}, dimensions={0}, use_global_device_ids=true | all-gather | bytes 786432 | tf_op jit(solution)/shard_map/all_gather | solution.py:306
  39.0 1.3 %outgoing.1 = bf16[1024,128]{1,0:T(8,128)(2,1)S(1)} custom-call(bf16[1024,128]{1,0:T(8,128)(2,1)S(1)} %bitcast.11, bf16[2048,128]{1,0:T(8,128)(2,1)S(1)} %all_gather.6.both), custom_call_target="tpu_custom_call" | custom-call | tf_op jit(solution)/shard_map/outgoing/pallas_call | solution.py:269
  40.3 0.0 copy-start
  40.3 0.0 copy-start.1
  40.3 23.9 %all_to_all.21 = bf16[256,4,128]{2,1,0:T(4,128)(2,1)S(1)} all-to-all(bf16[256,4,128]{2,1,0:T(4,128)(2,1)S(1)} %bitcast.14), channel_id=1, replica_groups=mesh['y'=8,'zl'=2,'core'=2,'xh'=2,'xl'=2,'zh'=4] {'zl','zh','y','xh','xl'}, dimensions={0} | all-to-all | bytes 524288 | tf_op jit(solution)/shard_map/all_to_all | solution.py:287
  64.3 0.0 copy-start.2
  64.3 0.0 copy-done
  64.3 0.0 copy-done.1
  64.3 0.6 copy-done.2
  64.9 1.4 %middle.1 = (bf16[1024,128]{1,0:T(8,128)(2,1)S(1)}, f32[128,512]{1,0:T(8,128)S(1)}, f32[128,512]{1,0:T(8,128)S(1)}) custom-call(s32[2]{0:T(128)S(1)} %pad_add_fusion.place, s32[4]{0:T(128)S(1)} %copy-done.2, bf16[1024,128]{1,0:T(8,128)(2,1)S(1)} %bitcast.12, f32[128,512]{1,0:T(8,128)S(1)} %get-tuple-element.13.gate, ...), custom_call_target="tpu_custom_call" | custom-call | tf_op jit(solution)/shard_map/middle/pallas_call | solution.py:269
  66.3 20.4 %all_to_all.22 = bf16[128,8,128]{2,1,0:T(8,128)(2,1)S(1)} all-to-all(bf16[128,8,128]{2,1,0:T(8,128)(2,1)S(1)} %bitcast.16), channel_id=1, replica_groups=mesh['y'=8,'zl'=2,'core'=2,'xh'=2,'xl'=2,'zh'=4] {'xh','xl','zh','y'}, dimensions={0} | all-to-all | bytes 524288 | tf_op jit(solution)/shard_map/all_to_all | solution.py:287
  86.6 5.2 %all_gather.7.both = bf16[2048,128]{1,0:T(8,128)(2,1)S(1)} all-gather(bf16[1024,128]{1,0:T(8,128)(2,1)S(1)} %bitcast.18), channel_id=1, replica_groups=mesh['y'=8,'zl'=2,'core'=2,'xh'=2,'xl'=2,'zh'=4] {'core'}, dimensions={0}, use_global_device_ids=true | all-gather | bytes 786432 | tf_op jit(solution)/shard_map/all_gather | solution.py:316
  91.9 2.0 %incoming.1 = bf16[1024,128]{1,0:T(8,128)(2,1)S(1)} custom-call(s32[2]{0:T(128)S(1)} %pad_add_fusion.place, bf16[2048,128]{1,0:T(8,128)(2,1)S(1)} %all_gather.7.both), custom_call_target="tpu_custom_call" | custom-call | tf_op jit(solution)/shard_map/incoming/pallas_call | solution.py:269
  93.9 23.2 %all_to_all.23 = bf16[256,4,128]{2,1,0:T(4,128)(2,1)S(1)} all-to-all(bf16[256,4,128]{2,1,0:T(4,128)(2,1)S(1)} %bitcast.15), channel_id=1, replica_groups=mesh['y'=8,'zl'=2,'core'=2,'xh'=2,'xl'=2,'zh'=4] {'zl','zh','y','xh','xl'}, dimensions={0} | all-to-all | bytes 524288 | tf_op jit(solution)/shard_map/all_to_all | solution.py:287
  117.1 1.2 last.1
Async XLA Ops:
  40.3 24.0 %copy-start = (bf16[2,128,640]{2,1,0:T(8,128)(2,1)S(1)}, bf16[2,128,640]{2,1,0:T(8,128)(2,1)}, u32[]{:S(2)}) copy-start(bf16[2,128,640]{2,1,0:T(8,128)(2,1)} %weight.1) | copy-start | bytes 983044
  40.3 24.0 %copy-start.1 = (bf16[2,128,128]{2,1,0:T(8,128)(2,1)S(1)}, bf16[2,128,128]{2,1,0:T(8,128)(2,1)}, u32[]{:S(2)}) copy-start(bf16[2,128,128]{2,1,0:T(8,128)(2,1)} %weight_out.3) | copy-start | bytes 196612
  64.3 0.7 copy-start.2

commit v4 on v3

v4 whole, which is shorter than its diff:
```python
import jax
import jax.numpy as jnp
from jax import lax
from jax.experimental import pallas as pl
from jax.experimental.pallas import tpu as pltpu
from jax.sharding import Mesh, PartitionSpec as P

EPSILON = 1e-05
F32 = jnp.float32
BF16 = jnp.bfloat16

ROWS = 14
COLS = 28
WIDE = 32
CELLS = 512
GROUPS = 4
LANES = 128
SLOT = 112
CHAINS = 4

ROW_AXES = ("y", "zl", "core")
COL_AXES = ("xh", "xl", "zh")
GROUP1 = ("zl", "xl", "zh", "y")
GROUP2 = ("xh", "xl", "zh", "y")
BACK = ("zl", "zh", "y", "xh", "xl")


def nt_dot(left, right):
    return lax.dot_general(left, right, (((1,), (1,)), ((), ())), preferred_element_type=F32)


def tn_dot(left, right):
    return lax.dot_general(left, right, (((0,), (0,)), ((), ())), preferred_element_type=F32)


def nn_dot(left, right):
    return jnp.dot(left, right, preferred_element_type=F32)


def norm_rows(values, gain, bias):
    average = jnp.mean(values, axis=0, keepdims=True)
    centered = values - average
    variance = jnp.mean(centered * centered, axis=0, keepdims=True)
    return (centered * lax.rsqrt(variance + EPSILON) * gain + bias).astype(BF16)


def swap_groups(tiles):
    group = lax.broadcasted_iota(jnp.int32, tiles[0].shape, 1) >> 5
    for bit in (1, 2):
        keep = (group & bit) == 0
        out = list(tiles)
        for p in range(4):
            if p & bit == 0:
                low, high = tiles[p], tiles[p + bit]
                out[p] = jnp.where(keep, low, pltpu.roll(high, 32 * bit, 1))
                out[p + bit] = jnp.where(keep, pltpu.roll(low, LANES - 32 * bit, 1), high)
        tiles = out
    return tiles


def token_matrix(cores):
    code = lax.broadcasted_iota(jnp.int32, (8, CELLS), 1)
    b = code & 31
    token = jnp.where(b < COLS, (code >> 5) * COLS + b, -4096)
    token = token - 4 * ROWS * lax.broadcasted_iota(jnp.int32, (8, CELLS), 0)
    none = jnp.zeros((8, CELLS), F32)
    rows = []
    for core in cores:
        for q in range(4):
            for m in range(GROUPS):
                for zl in range(2):
                    a = 4 * m + q
                    first = (zl * 2 + core) * ROWS + a
                    rows.append(jnp.where(token == first, 1.0, 0.0).astype(F32) if a < ROWS else none)
    return jnp.concatenate(rows, axis=0).astype(BF16)


def fields(code, *widths):
    out = []
    for width in reversed(widths):
        out.append(code & (width - 1))
        code = code >> (width.bit_length() - 1)
    return out[::-1]


def own_matrix(core):
    q, m, zl, y = fields(lax.broadcasted_iota(jnp.int32, (8, CELLS // 2), 1), 4, 4, 2, 8)
    a = 4 * m + q
    sub = lax.broadcasted_iota(jnp.int32, (8, CELLS // 2), 0)
    token = jnp.where(a < ROWS, ((y * 2 + zl) * 2 + core) * ROWS + a, -4096) - sub
    last = jnp.where(sub < COLS - 24, token, -4096)
    return jnp.concatenate([
        jnp.where((last if b == 24 else token) == c * COLS + b, 1.0, 0.0).astype(F32)
        for c in range(16) for b in range(0, WIDE, 8)
    ], axis=0).astype(BF16)


def valid_token(token, lengths_ref):
    valid = jnp.zeros(token.shape, jnp.bool_)
    for chain in range(CHAINS):
        start = chain * SLOT
        valid = valid | ((token >= start) & (token < start + lengths_ref[chain]))
    return valid


def cell_mask(place, lengths_ref):
    lane = lax.broadcasted_iota(jnp.int32, (1, CELLS), 1)
    a, b = lane >> 5, lane & 31
    row = valid_token(place[0:1, 0:1] * ROWS + a, lengths_ref)
    col = valid_token(place[8:9, 0:1] * COLS + b, lengths_ref)
    inside = (a < ROWS) & (b < COLS)
    return jnp.where(row & col & inside, 1.0, 0.0).astype(F32)


def project(columns, mask, gain, bias, weight, send, send_ref, gate_ref):
    for m in range(GROUPS):
        lanes = slice(m * LANES, (m + 1) * LANES)
        normed = norm_rows(columns[:, lanes], gain, bias)
        projected = tn_dot(weight, normed)
        weighting = mask[:, lanes]
        left = weighting * jax.nn.sigmoid(projected[128:256]) * projected[0:128]
        right = weighting * jax.nn.sigmoid(projected[384:512]) * projected[256:384]
        send[pl.ds(m, 128, stride=8), :] = left
        send[pl.ds(4 + m, 128, stride=8), :] = right
        gate_ref[:, lanes] = jax.nn.sigmoid(projected[512:640])
    send_ref[...] = send[...].astype(BF16)


def first_kernel(
    place, lengths_hbm, pair_hbm, in_gain_hbm, in_bias_hbm, weight_hbm, out_gain_hbm, out_bias_hbm,
    send_ref, gate_ref, columns_ref, vectors_ref, mask_ref, cells, send, norms, lengths, pair, in_gain, in_bias, out_gain, out_bias, weight, sems,
):
    copies = [
        pltpu.make_async_copy(source, target, sems.at[at])
        for at, (source, target) in enumerate((
            (pair_hbm, pair), (weight_hbm.at[0], weight), (in_gain_hbm, in_gain), (in_bias_hbm, in_bias),
            (out_gain_hbm, out_gain), (out_bias_hbm, out_bias), (lengths_hbm, lengths),
        ))
    ]
    for copy in copies:
        copy.start()
    cells[...] = jnp.zeros_like(cells)
    norms[...] = jnp.zeros_like(norms)
    for copy in copies:
        copy.wait()
    mask = cell_mask(place, lengths)
    mask_ref[...] = mask
    for at, pair_of in enumerate((in_gain, in_bias, out_gain, out_bias)):
        norms[pl.ds(2 * at, 2), :] = pair_of[...]
    vectors = norms[...].T
    vectors_ref[...] = vectors
    for a in range(ROWS):
        cells[pl.ds(a * WIDE, COLS), :] = pair[a].astype(F32)
    columns = cells[...].T
    columns_ref[...] = columns
    project(columns, mask, vectors[:, 0:1], vectors[:, 2:3], weight[...], send, send_ref, gate_ref)


def finish(home, source_rows, gain, bias, gate, columns, weight_out, got):
    got[...] = home[...].astype(F32)
    parts = []
    for m in range(GROUPS):
        lanes = slice(m * LANES, (m + 1) * LANES)
        triangle = source_rows(got, 0, m) + source_rows(got, 1, m)
        change = tn_dot(weight_out, norm_rows(triangle, gain, bias))
        parts.append(columns[:, lanes] + gate[:, lanes] * change)
    return jnp.concatenate(parts, axis=1).astype(BF16)


def rows_after_first(got, xh, m):
    return jnp.concatenate([
        got[pl.ds(zl * 512 + xh * 8 + xl * 4 + m, 32, stride=16), :] for zl in range(2) for xl in range(2)
    ], axis=0)


def rows_after_second(got, zl, m):
    return jnp.concatenate([got[pl.ds(zl * 512 + x * 4 + m, 32, stride=16), :] for x in range(4)], axis=0)


def middle_kernel(
    home, gate, columns, vectors, mask, weight, weight_out, send_ref, gate_ref, columns_ref, got, send
):
    middle = finish(
        home, rows_after_first, vectors[:, 4:5], vectors[:, 6:7], gate, columns, weight_out[0], got
    ).astype(F32)
    columns_ref[...] = middle
    project(middle, mask, vectors[:, 1:2], vectors[:, 3:4], weight[1], send, send_ref, gate_ref)


def last_kernel(home, gate, columns, vectors, weight_out, out_ref, got, cells):
    updated = finish(
        home, rows_after_second, vectors[:, 5:6], vectors[:, 7:8], gate, columns, weight_out[1], got
    ).astype(F32)
    cells[...] = updated.T
    for a in range(ROWS):
        out_ref[a] = cells[pl.ds(a * WIDE, COLS), :].astype(BF16)


def stack(pieces):
    return jnp.concatenate(list(pieces), axis=0)


def send_home(triangle, out_ref, out_f):
    tiles = swap_groups([
        stack(
            triangle[((q * 4 + m) * 2 + zl) * 8 : ((q * 4 + m) * 2 + zl) * 8 + 8, x * 128 : x * 128 + 128]
            for m in range(GROUPS) for zl in range(2) for x in range(4)
        )
        for q in range(4)
    ])
    for m in range(GROUPS):
        for zl in range(2):
            for x in range(4):
                at = ((m * 2 + zl) * 4 + x) * 8
                for zh in range(4):
                    out_f[pl.ds((zl * 4 + zh) * 128 + x * 4 + m, 8, stride=16), :] = tiles[zh][at : at + 8]
    out_ref[...] = out_f[...].astype(BF16)


def outgoing_kernel(mine, both, out_ref, mine_f, both_f, out_f):
    mine_f[...] = mine[...].astype(F32)
    both_f[...] = both[...].astype(F32)

    def matrix(source, base):
        tiles = swap_groups([
            stack(
                source[pl.ds(base + ((zl * 2 + xl) * 4 + zh) * 64 + m, 8, stride=8), :]
                for xl in range(2) for m in range(GROUPS) for zl in range(2)
            )
            for zh in range(4)
        ])
        half = tiles[0].shape[0] // 2
        return stack(jnp.concatenate([tile[:half], tile[half:]], axis=1) for tile in tiles).astype(BF16)

    left = matrix(mine_f, 0)
    right = stack(matrix(both_f, core * 1024 + 4) for core in range(2))
    triangle = nt_dot(left, right).astype(BF16)
    send_home(nn_dot(triangle, token_matrix(range(2))), out_ref, out_f)


def incoming_kernel(place, both, out_ref, both_f, out_f):
    both_f[...] = both[...].astype(F32)

    def matrix(base):
        tiles = swap_groups([
            stack(
                both_f[pl.ds(base + core * 1024 + (x * 4 + zh) * 64 + m, 8, stride=8), :]
                for x in range(4) for m in range(GROUPS) for core in range(2)
            )
            for zh in range(4)
        ])
        return stack(
            jnp.concatenate([tile[x * 64 : x * 64 + 64] for x in range(4)], axis=1) for tile in tiles
        ).astype(BF16)

    left = nn_dot(matrix(0), own_matrix(place[0:1, 0:1] & 1)).astype(BF16)
    send_home(tn_dot(left, matrix(4)), out_ref, out_f)


def call(kernel, outs, scratch, name, held=()):
    def run(*args):
        return pl.pallas_call(
            kernel,
            out_shape=outs,
            in_specs=[pl.BlockSpec(memory_space=pltpu.HBM if at in held else pltpu.VMEM) for at in range(len(args))],
            out_specs=jax.tree.map(lambda _: pl.BlockSpec(memory_space=pltpu.VMEM), outs),
            scratch_shapes=[pltpu.VMEM(entry, F32) if isinstance(entry, tuple) else entry for entry in scratch],
            compiler_params=pltpu.CompilerParams(vmem_limit_bytes=32 * 1024 * 1024),
            name=name,
        )(*args)

    return run


def in_hbm(array):
    return pltpu.with_memory_space_constraint(array, pltpu.HBM)


def exchange(array, axes):
    return lax.all_to_all(array, axes, 0, 0, tiled=True)


def on_device(pair_rep, chain_lengths, in_gain, in_bias, weight_in, out_gain, out_bias, weight_out):
    place = jnp.concatenate([
        jnp.full((8, LANES), lax.axis_index(axes), jnp.int32) for axes in (ROW_AXES, COL_AXES)
    ])
    tile = jax.ShapeDtypeStruct((LANES, CELLS), F32)
    sent = jax.ShapeDtypeStruct((1024, LANES), BF16)

    small = (jax.ShapeDtypeStruct((LANES, 8), F32), jax.ShapeDtypeStruct((1, CELLS), F32))
    send, gate, columns, vectors, mask = call(
        first_kernel, (sent, tile, tile) + small, [
            (CELLS, LANES), (1024, LANES), (8, LANES), pltpu.SMEM(chain_lengths.shape, jnp.int32),
            pltpu.VMEM(pair_rep.shape, BF16), in_gain.shape, in_bias.shape, out_gain.shape, out_bias.shape,
            pltpu.VMEM(weight_in.shape[1:], BF16), pltpu.SemaphoreType.DMA((7,)),
        ], "first", range(1, 8),
    )(place, *map(in_hbm, (chain_lengths, pair_rep, in_gain, in_bias, weight_in, out_gain, out_bias)))
    mine = exchange(send.reshape(128, 8, LANES), GROUP1).reshape(1024, LANES)
    both = lax.all_gather(mine, "core", axis=0, tiled=True)
    home = call(
        outgoing_kernel, sent, [(1024, LANES), (2048, LANES), (1024, LANES)], "outgoing"
    )(mine, both)
    home = exchange(home.reshape(256, 4, LANES), BACK).reshape(1024, LANES)

    send, gate, columns = call(
        middle_kernel, (sent, tile, tile), [(1024, LANES), (1024, LANES)], "middle"
    )(home, gate, columns, vectors, mask, weight_in, weight_out)
    mine = exchange(send.reshape(128, 8, LANES), GROUP2).reshape(1024, LANES)
    both = lax.all_gather(mine, "core", axis=0, tiled=True)
    home = call(
        incoming_kernel, sent, [(2048, LANES), (1024, LANES)], "incoming"
    )(place, both)
    home = exchange(home.reshape(256, 4, LANES), BACK).reshape(1024, LANES)

    out = jax.ShapeDtypeStruct(pair_rep.shape, BF16)
    return call(last_kernel, out, [(1024, LANES), (CELLS, LANES)], "last")(home, gate, columns, vectors, weight_out)


def solution(mesh):
    fine = Mesh(mesh.devices.reshape(8, 2, 2, 2, 2, 4), ROW_AXES + COL_AXES)
    placed = P(ROW_AXES, COL_AXES, None)
    return jax.shard_map(
        on_device, mesh=fine, in_specs=(placed,) + (P(),) * 7, out_specs=placed, check_vma=False
    )
```

time: 119 us -> 116 us (0.975)
  Pallas kernels: 8.06 us -> 5.85 us
    pallas_call x5, Pallas kernels: 8.06 us -> 5.85 us  [run(): pl.pallas_call(kernel, out_shape=outs, in_specs=[pl.BlockSpec(memory_spac...]
where the time goes in v4:
time: 116 us; the launch traced here: 115 us
  blocking collectives  109 us (94%)
  Pallas kernels  5.85 us (5%)
    all_to_all x4, blocking collectives, exchange(): return lax.all_to_all(array, axes, 0, 0, tiled=True)  99.2 us
    all_gather x2, blocking collectives, on_device(): both = lax.all_gather(mine, 'core', axis=0, tiled=True)  10.3 us
    pallas_call x5, Pallas kernels, run(): pl.pallas_call(kernel, out_shape=outs, in_specs=[pl.BlockSpec(memory_spac...  5.85 us

profile of v4, /device:TPU:1, one launch (start us, length us, event | category | flops | bytes accessed | tf_op | source)
XLA Modules:
  0.0 115.5 jit_solution(11000218601768668642)
XLA Ops:
  0.0 0.1 concatenate.6.place
  0.1 1.7 %first.1 = (bf16[1024,128]{1,0:T(8,128)(2,1)S(1)}, f32[128,512]{1,0:T(8,128)S(1)}, f32[128,512]{1,0:T(8,128)S(1)}, f32[128,8]{1,0:T(8,128)S(1)}, f32[1,512]{1,0:T(1,128)S(1)}) custom-call(s32[16,128]{1,0:T(8,128)S(1)} %concatenate.6.place, s32[4]{0:T(128)} %lengths_hbm.1, bf16[14,28,128]{2,1,0:T(8,128)(2,1)} %pair_hbm.1, f32[2,128]{1,0:T(2,128)} %in_gain_hbm.1, ...), custom_call_target="tpu_custom_call" | custom-call | tf_op jit(solution)/shard_map/first/pallas_call | solution.py:262
  1.8 31.6 %all_to_all.20 = bf16[128,8,128]{2,1,0:T(8,128)(2,1)S(1)} all-to-all(bf16[128,8,128]{2,1,0:T(8,128)(2,1)S(1)} %bitcast.15), channel_id=1, replica_groups=mesh['y'=8,'zl'=2,'core'=2,'xh'=2,'xl'=2,'zh'=4] {'zl','xl','zh','y'}, dimensions={0} | all-to-all | bytes 524288 | tf_op jit(solution)/shard_map/all_to_all | solution.py:280
  33.4 5.1 %all_gather.6.both = bf16[2048,128]{1,0:T(8,128)(2,1)S(1)} all-gather(bf16[1024,128]{1,0:T(8,128)(2,1)S(1)} %bitcast.8), channel_id=1, replica_groups=mesh['y'=8,'zl'=2,'core'=2,'xh'=2,'xl'=2,'zh'=4] {'core'}, dimensions={0}, use_global_device_ids=true | all-gather | bytes 786432 | tf_op jit(solution)/shard_map/all_gather | solution.py:299
  38.5 1.1 outgoing.1
  39.5 0.0 copy-start
  39.5 0.0 copy-start.1
  39.6 23.9 %all_to_all.21 = bf16[256,4,128]{2,1,0:T(4,128)(2,1)S(1)} all-to-all(bf16[256,4,128]{2,1,0:T(4,128)(2,1)S(1)} %bitcast.13), channel_id=1, replica_groups=mesh['y'=8,'zl'=2,'core'=2,'xh'=2,'xl'=2,'zh'=4] {'zl','zh','y','xh','xl'}, dimensions={0} | all-to-all | bytes 524288 | tf_op jit(solution)/shard_map/all_to_all | solution.py:280
  63.5 0.0 copy-done
  63.5 0.0 copy-done.1
  63.5 0.8 middle.1
  64.3 20.4 %all_to_all.22 = bf16[128,8,128]{2,1,0:T(8,128)(2,1)S(1)} all-to-all(bf16[128,8,128]{2,1,0:T(8,128)(2,1)S(1)} %bitcast.14), channel_id=1, replica_groups=mesh['y'=8,'zl'=2,'core'=2,'xh'=2,'xl'=2,'zh'=4] {'xh','xl','zh','y'}, dimensions={0} | all-to-all | bytes 524288 | tf_op jit(solution)/shard_map/all_to_all | solution.py:280
  84.7 5.3 %all_gather.7.both = bf16[2048,128]{1,0:T(8,128)(2,1)S(1)} all-gather(bf16[1024,128]{1,0:T(8,128)(2,1)S(1)} %bitcast.16), channel_id=1, replica_groups=mesh['y'=8,'zl'=2,'core'=2,'xh'=2,'xl'=2,'zh'=4] {'core'}, dimensions={0}, use_global_device_ids=true | all-gather | bytes 786432 | tf_op jit(solution)/shard_map/all_gather | solution.py:309
  89.9 1.1 incoming.1
  91.1 23.2 %all_to_all.23 = bf16[256,4,128]{2,1,0:T(4,128)(2,1)S(1)} all-to-all(bf16[256,4,128]{2,1,0:T(4,128)(2,1)S(1)} %bitcast.11), channel_id=1, replica_groups=mesh['y'=8,'zl'=2,'core'=2,'xh'=2,'xl'=2,'zh'=4] {'zl','zh','y','xh','xl'}, dimensions={0} | all-to-all | bytes 524288 | tf_op jit(solution)/shard_map/all_to_all | solution.py:280
  114.3 1.2 %last.1 = bf16[14,28,128]{2,1,0:T(8,128)(2,1)} custom-call(bf16[1024,128]{1,0:T(8,128)(2,1)S(1)} %bitcast.12, f32[128,512]{1,0:T(8,128)S(1)} %get-tuple-element.19.gate, f32[128,512]{1,0:T(8,128)S(1)} %get-tuple-element.20.columns, f32[128,8]{1,0:T(8,128)S(1)} %get-tuple-element.16.vectors, bf16[2,128,128]{2,1,0:T(8,128)(2,1)S(1)} %copy-done.1), custom_call_target="tpu_custom_call" | custom-call | tf_op jit(solution)/shard_map/last/pallas_call | solution.py:262
  (2 shorter events, 0.0 us)
Async XLA Ops:
  39.5 24.0 %copy-start = (bf16[2,128,640]{2,1,0:T(8,128)(2,1)S(1)}, bf16[2,128,640]{2,1,0:T(8,128)(2,1)}, u32[]{:S(2)}) copy-start(bf16[2,128,640]{2,1,0:T(8,128)(2,1)} %weight.1) | copy-start | bytes 983044
  39.5 24.0 %copy-start.1 = (bf16[2,128,128]{2,1,0:T(8,128)(2,1)S(1)}, bf16[2,128,128]{2,1,0:T(8,128)(2,1)}, u32[]{:S(2)}) copy-start(bf16[2,128,128]{2,1,0:T(8,128)(2,1)} %weight_out.3) | copy-start | bytes 196612

commit v5 on v4

--- a/solution.py
+++ b/solution.py
@@ -18,11 +18,11 @@
 SLOT = 112
 CHAINS = 4
 
-ROW_AXES = ("y", "zl", "core")
+ROW_AXES = ("yh", "yl", "zl", "core")
 COL_AXES = ("xh", "xl", "zh")
-GROUP1 = ("zl", "xl", "zh", "y")
-GROUP2 = ("xh", "xl", "zh", "y")
-BACK = ("zl", "zh", "y", "xh", "xl")
+GROUP1 = ("xl", "zh", "yh", "yl", "zl")
+GROUP2 = ("zh", "xh", "xl", "yl", "zl")
+BACK = ("zh", "yh", "yl", "zl", "xh", "xl")
 
 
 def nt_dot(left, right):
@@ -35,6 +35,10 @@
 
 def nn_dot(left, right):
     return jnp.dot(left, right, preferred_element_type=F32)
+
+
+def stack(pieces):
+    return jnp.concatenate(list(pieces), axis=0)
 
 
 def norm_rows(values, gain, bias):
@@ -58,19 +62,18 @@
     return tiles
 
 
-def token_matrix(cores):
+def token_matrix():
     code = lax.broadcasted_iota(jnp.int32, (8, CELLS), 1)
-    b = code & 31
-    token = jnp.where(b < COLS, (code >> 5) * COLS + b, -4096)
-    token = token - 4 * ROWS * lax.broadcasted_iota(jnp.int32, (8, CELLS), 0)
+    token = jnp.where(code & 31 < COLS, (code >> 5) * COLS + (code & 31), -4096)
+    token = token - COLS * lax.broadcasted_iota(jnp.int32, (8, CELLS), 0)
     none = jnp.zeros((8, CELLS), F32)
     rows = []
-    for core in cores:
+    for core in range(2):
         for q in range(4):
             for m in range(GROUPS):
-                for zl in range(2):
+                for yh in range(2):
                     a = 4 * m + q
-                    first = (zl * 2 + core) * ROWS + a
+                    first = yh * 8 * COLS + core * ROWS + a
                     rows.append(jnp.where(token == first, 1.0, 0.0).astype(F32) if a < ROWS else none)
     return jnp.concatenate(rows, axis=0).astype(BF16)
 
@@ -84,10 +87,10 @@
 
 
 def own_matrix(core):
-    q, m, zl, y = fields(lax.broadcasted_iota(jnp.int32, (8, CELLS // 2), 1), 4, 4, 2, 8)
+    q, m, yh, s = fields(lax.broadcasted_iota(jnp.int32, (8, CELLS // 2), 1), 4, 4, 2, 8)
     a = 4 * m + q
     sub = lax.broadcasted_iota(jnp.int32, (8, CELLS // 2), 0)
-    token = jnp.where(a < ROWS, ((y * 2 + zl) * 2 + core) * ROWS + a, -4096) - sub
+    token = jnp.where(a < ROWS, ((yh * 8 + s) * 2 + core) * ROWS + a, -4096) - sub
     last = jnp.where(sub < COLS - 24, token, -4096)
     return jnp.concatenate([
         jnp.where((last if b == 24 else token) == c * COLS + b, 1.0, 0.0).astype(F32)
@@ -168,13 +171,13 @@
 
 
 def rows_after_first(got, xh, m):
-    return jnp.concatenate([
-        got[pl.ds(zl * 512 + xh * 8 + xl * 4 + m, 32, stride=16), :] for zl in range(2) for xl in range(2)
-    ], axis=0)
-
-
-def rows_after_second(got, zl, m):
-    return jnp.concatenate([got[pl.ds(zl * 512 + x * 4 + m, 32, stride=16), :] for x in range(4)], axis=0)
+    return stack(got[pl.ds(xh * 8 + xl * 4 + m, 64, stride=16), :] for xl in range(2))
+
+
+def rows_after_second(got, yh, m):
+    return stack(
+        got[pl.ds((zh * 2 + yh) * 128 + x * 4 + m, 8, stride=16), :] for zh in range(4) for x in range(4)
+    )
 
 
 def middle_kernel(
@@ -196,24 +199,20 @@
         out_ref[a] = cells[pl.ds(a * WIDE, COLS), :].astype(BF16)
 
 
-def stack(pieces):
-    return jnp.concatenate(list(pieces), axis=0)
-
-
 def send_home(triangle, out_ref, out_f):
     tiles = swap_groups([
         stack(
-            triangle[((q * 4 + m) * 2 + zl) * 8 : ((q * 4 + m) * 2 + zl) * 8 + 8, x * 128 : x * 128 + 128]
-            for m in range(GROUPS) for zl in range(2) for x in range(4)
+            triangle[((q * 4 + m) * 2 + yh) * 8 : ((q * 4 + m) * 2 + yh) * 8 + 8, x * 128 : x * 128 + 128]
+            for m in range(GROUPS) for yh in range(2) for x in range(4)
         )
         for q in range(4)
     ])
     for m in range(GROUPS):
-        for zl in range(2):
+        for yh in range(2):
             for x in range(4):
-                at = ((m * 2 + zl) * 4 + x) * 8
+                at = ((m * 2 + yh) * 4 + x) * 8
                 for zh in range(4):
-                    out_f[pl.ds((zl * 4 + zh) * 128 + x * 4 + m, 8, stride=16), :] = tiles[zh][at : at + 8]
+                    out_f[pl.ds((zh * 2 + yh) * 128 + x * 4 + m, 8, stride=16), :] = tiles[zh][at : at + 8]
     out_ref[...] = out_f[...].astype(BF16)
 
 
@@ -224,8 +223,8 @@
     def matrix(source, base):
         tiles = swap_groups([
             stack(
-                source[pl.ds(base + ((zl * 2 + xl) * 4 + zh) * 64 + m, 8, stride=8), :]
-                for xl in range(2) for m in range(GROUPS) for zl in range(2)
+                source[pl.ds(base + ((xl * 4 + zh) * 2 + yh) * 64 + m, 8, stride=8), :]
+                for xl in range(2) for m in range(GROUPS) for yh in range(2)
             )
             for zh in range(4)
         ])
@@ -235,7 +234,7 @@
     left = matrix(mine_f, 0)
     right = stack(matrix(both_f, core * 1024 + 4) for core in range(2))
     triangle = nt_dot(left, right).astype(BF16)
-    send_home(nn_dot(triangle, token_matrix(range(2))), out_ref, out_f)
+    send_home(nn_dot(triangle, token_matrix()), out_ref, out_f)
 
 
 def incoming_kernel(place, both, out_ref, both_f, out_f):
@@ -244,7 +243,7 @@
     def matrix(base):
         tiles = swap_groups([
             stack(
-                both_f[pl.ds(base + core * 1024 + (x * 4 + zh) * 64 + m, 8, stride=8), :]
+                both_f[pl.ds(base + core * 1024 + (zh * 4 + x) * 64 + m, 8, stride=8), :]
                 for x in range(4) for m in range(GROUPS) for core in range(2)
             )
             for zh in range(4)
@@ -317,7 +316,7 @@
 
 
 def solution(mesh):
-    fine = Mesh(mesh.devices.reshape(8, 2, 2, 2, 2, 4), ROW_AXES + COL_AXES)
+    fine = Mesh(mesh.devices.reshape(2, 4, 2, 2, 2, 2, 4), ROW_AXES + COL_AXES)
     placed = P(ROW_AXES, COL_AXES, None)
     return jax.shard_map(
         on_device, mesh=fine, in_specs=(placed,) + (P(),) * 7, out_specs=placed, check_vma=False

time: 116 us -> 115 us (level)
  no operation moved by 1% of the time
where the time goes in v5:
time: 115 us; the launch traced here: 114 us
  blocking collectives  108 us (94%)
  Pallas kernels  5.85 us (5%)
    all_to_all x4, blocking collectives, exchange(): return lax.all_to_all(array, axes, 0, 0, tiled=True)  98.3 us
    all_gather x2, blocking collectives, on_device(): both = lax.all_gather(mine, 'core', axis=0, tiled=True)  9.6 us
    pallas_call x5, Pallas kernels, run(): pl.pallas_call(kernel, out_shape=outs, in_specs=[pl.BlockSpec(memory_spac...  5.85 us

profile of v5, /device:TPU:1, one launch (start us, length us, event | category | flops | bytes accessed | tf_op | source)
XLA Modules:
  0.0 113.9 jit_solution(16750212449885396844)
XLA Ops:
  0.0 0.1 concatenate.6.place
  0.1 1.7 %first.1 = (bf16[1024,128]{1,0:T(8,128)(2,1)S(1)}, f32[128,512]{1,0:T(8,128)S(1)}, f32[128,512]{1,0:T(8,128)S(1)}, f32[128,8]{1,0:T(8,128)S(1)}, f32[1,512]{1,0:T(1,128)S(1)}) custom-call(s32[16,128]{1,0:T(8,128)S(1)} %concatenate.6.place, s32[4]{0:T(128)} %lengths_hbm.1, bf16[14,28,128]{2,1,0:T(8,128)(2,1)} %pair_hbm.1, f32[2,128]{1,0:T(2,128)} %in_gain_hbm.1, ...), custom_call_target="tpu_custom_call" | custom-call | tf_op jit(solution)/shard_map/first/pallas_call | solution.py:261
  1.8 31.8 %all_to_all.20 = bf16[128,8,128]{2,1,0:T(8,128)(2,1)S(1)} all-to-all(bf16[128,8,128]{2,1,0:T(8,128)(2,1)S(1)} %bitcast.15), channel_id=1, replica_groups=mesh['yh'=2,'yl'=4,'zl'=2,'core'=2,'xh'=2,'xl'=2,'zh'=4] {'xl','zh','yh'..., dimensions={0} | all-to-all | bytes 524288 | tf_op jit(solution)/shard_map/all_to_all | solution.py:279
  33.5 5.1 %all_gather.6.both = bf16[2048,128]{1,0:T(8,128)(2,1)S(1)} all-gather(bf16[1024,128]{1,0:T(8,128)(2,1)S(1)} %bitcast.8), channel_id=1, replica_groups=mesh['yh'=2,'yl'=4,'zl'=2,'core'=2,'xh'=2,'xl'=2,'zh'=4] {'core'}, dimensions={0}, use_global_device_ids=true | all-gather | bytes 786432 | tf_op jit(solution)/shard_map/all_gather | solution.py:298
  38.6 1.1 outgoing.1
  39.7 0.0 copy-start
  39.7 0.0 copy-start.1
  39.7 24.0 %all_to_all.21 = bf16[256,4,128]{2,1,0:T(4,128)(2,1)S(1)} all-to-all(bf16[256,4,128]{2,1,0:T(4,128)(2,1)S(1)} %bitcast.13), channel_id=1, replica_groups=mesh['yh'=2,'yl'=4,'zl'=2,'core'=2,'xh'=2,'xl'=2,'zh'=4] {'zh','yh','yl'..., dimensions={0} | all-to-all | bytes 524288 | tf_op jit(solution)/shard_map/all_to_all | solution.py:279
  63.7 0.0 copy-done
  63.7 0.0 copy-done.1
  63.7 0.8 middle.1
  64.5 19.0 %all_to_all.22 = bf16[128,8,128]{2,1,0:T(8,128)(2,1)S(1)} all-to-all(bf16[128,8,128]{2,1,0:T(8,128)(2,1)S(1)} %bitcast.14), channel_id=1, replica_groups=mesh['yh'=2,'yl'=4,'zl'=2,'core'=2,'xh'=2,'xl'=2,'zh'=4] {'zh','xh','xl'..., dimensions={0} | all-to-all | bytes 524288 | tf_op jit(solution)/shard_map/all_to_all | solution.py:279
  83.5 4.5 %all_gather.7.both = bf16[2048,128]{1,0:T(8,128)(2,1)S(1)} all-gather(bf16[1024,128]{1,0:T(8,128)(2,1)S(1)} %bitcast.16), channel_id=1, replica_groups=mesh['yh'=2,'yl'=4,'zl'=2,'core'=2,'xh'=2,'xl'=2,'zh'=4] {'core'}, dimensions={0}, use_global_device_ids=true | all-gather | bytes 786432 | tf_op jit(solution)/shard_map/all_gather | solution.py:308
  88.1 1.1 incoming.1
  89.2 23.5 %all_to_all.23 = bf16[256,4,128]{2,1,0:T(4,128)(2,1)S(1)} all-to-all(bf16[256,4,128]{2,1,0:T(4,128)(2,1)S(1)} %bitcast.11), channel_id=1, replica_groups=mesh['yh'=2,'yl'=4,'zl'=2,'core'=2,'xh'=2,'xl'=2,'zh'=4] {'zh','yh','yl'..., dimensions={0} | all-to-all | bytes 524288 | tf_op jit(solution)/shard_map/all_to_all | solution.py:279
  112.7 1.2 %last.1 = bf16[14,28,128]{2,1,0:T(8,128)(2,1)} custom-call(bf16[1024,128]{1,0:T(8,128)(2,1)S(1)} %bitcast.12, f32[128,512]{1,0:T(8,128)S(1)} %get-tuple-element.19.gate, f32[128,512]{1,0:T(8,128)S(1)} %get-tuple-element.20.columns, f32[128,8]{1,0:T(8,128)S(1)} %get-tuple-element.16.vectors, bf16[2,128,128]{2,1,0:T(8,128)(2,1)S(1)} %copy-done.1), custom_call_target="tpu_custom_call" | custom-call | tf_op jit(solution)/shard_map/last/pallas_call | solution.py:261
  (2 shorter events, 0.0 us)
Async XLA Ops:
  39.7 24.0 %copy-start = (bf16[2,128,640]{2,1,0:T(8,128)(2,1)S(1)}, bf16[2,128,640]{2,1,0:T(8,128)(2,1)}, u32[]{:S(2)}) copy-start(bf16[2,128,640]{2,1,0:T(8,128)(2,1)} %weight.1) | copy-start | bytes 983044
  39.7 24.0 %copy-start.1 = (bf16[2,128,128]{2,1,0:T(8,128)(2,1)S(1)}, bf16[2,128,128]{2,1,0:T(8,128)(2,1)}, u32[]{:S(2)}) copy-start(bf16[2,128,128]{2,1,0:T(8,128)(2,1)} %weight_out.3) | copy-start | bytes 196612

commit v6 on v5

--- a/solution.py
+++ b/solution.py
@@ -20,7 +20,7 @@
 
 ROW_AXES = ("yh", "yl", "zl", "core")
 COL_AXES = ("xh", "xl", "zh")
-GROUP1 = ("xl", "zh", "yh", "yl", "zl")
+GROUP1 = ("zh", "xl", "yh", "yl", "zl")
 GROUP2 = ("zh", "xh", "xl", "yl", "zl")
 BACK = ("zh", "yh", "yl", "zl", "xh", "xl")
 
@@ -171,7 +171,9 @@
 
 
 def rows_after_first(got, xh, m):
-    return stack(got[pl.ds(xh * 8 + xl * 4 + m, 64, stride=16), :] for xl in range(2))
+    return stack(
+        got[pl.ds(zh * 256 + xh * 8 + xl * 4 + m, 16, stride=16), :] for zh in range(4) for xl in range(2)
+    )
 
 
 def rows_after_second(got, yh, m):
@@ -223,7 +225,7 @@
     def matrix(source, base):
         tiles = swap_groups([
             stack(
-                source[pl.ds(base + ((xl * 4 + zh) * 2 + yh) * 64 + m, 8, stride=8), :]
+                source[pl.ds(base + ((zh * 2 + xl) * 2 + yh) * 64 + m, 8, stride=8), :]
                 for xl in range(2) for m in range(GROUPS) for yh in range(2)
             )
             for zh in range(4)

time: 115 us -> 115 us (level)
  no operation moved by 1% of the time
where the time goes in v6:
time: 115 us; the launch traced here: 114 us
  blocking collectives  108 us (94%)
  Pallas kernels  5.83 us (5%)
    all_to_all x4, blocking collectives, exchange(): return lax.all_to_all(array, axes, 0, 0, tiled=True)  98.7 us
    all_gather x2, blocking collectives, on_device(): both = lax.all_gather(mine, 'core', axis=0, tiled=True)  9.24 us
    pallas_call x5, Pallas kernels, run(): pl.pallas_call(kernel, out_shape=outs, in_specs=[pl.BlockSpec(memory_spac...  5.83 us

profile of v6, /device:TPU:1, one launch (start us, length us, event | category | flops | bytes accessed | tf_op | source)
XLA Modules:
  0.0 113.9 jit_solution(7169312088107543912)
XLA Ops:
  0.0 0.1 concatenate.6.place
  0.1 1.7 %first.1 = (bf16[1024,128]{1,0:T(8,128)(2,1)S(1)}, f32[128,512]{1,0:T(8,128)S(1)}, f32[128,512]{1,0:T(8,128)S(1)}, f32[128,8]{1,0:T(8,128)S(1)}, f32[1,512]{1,0:T(1,128)S(1)}) custom-call(s32[16,128]{1,0:T(8,128)S(1)} %concatenate.6.place, s32[4]{0:T(128)} %lengths_hbm.1, bf16[14,28,128]{2,1,0:T(8,128)(2,1)} %pair_hbm.1, f32[2,128]{1,0:T(2,128)} %in_gain_hbm.1, ...), custom_call_target="tpu_custom_call" | custom-call | tf_op jit(solution)/shard_map/first/pallas_call | solution.py:263
  1.8 32.7 %all_to_all.20 = bf16[128,8,128]{2,1,0:T(8,128)(2,1)S(1)} all-to-all(bf16[128,8,128]{2,1,0:T(8,128)(2,1)S(1)} %bitcast.15), channel_id=1, replica_groups=mesh['yh'=2,'yl'=4,'zl'=2,'core'=2,'xh'=2,'xl'=2,'zh'=4] {'zh','xl','yh'..., dimensions={0} | all-to-all | bytes 524288 | tf_op jit(solution)/shard_map/all_to_all | solution.py:281
  34.4 4.7 %all_gather.6.both = bf16[2048,128]{1,0:T(8,128)(2,1)S(1)} all-gather(bf16[1024,128]{1,0:T(8,128)(2,1)S(1)} %bitcast.8), channel_id=1, replica_groups=mesh['yh'=2,'yl'=4,'zl'=2,'core'=2,'xh'=2,'xl'=2,'zh'=4] {'core'}, dimensions={0}, use_global_device_ids=true | all-gather | bytes 786432 | tf_op jit(solution)/shard_map/all_gather | solution.py:300
  39.1 1.1 outgoing.1
  40.2 0.0 copy-start
  40.2 0.0 copy-start.1
  40.2 23.5 %all_to_all.21 = bf16[256,4,128]{2,1,0:T(4,128)(2,1)S(1)} all-to-all(bf16[256,4,128]{2,1,0:T(4,128)(2,1)S(1)} %bitcast.13), channel_id=1, replica_groups=mesh['yh'=2,'yl'=4,'zl'=2,'core'=2,'xh'=2,'xl'=2,'zh'=4] {'zh','yh','yl'..., dimensions={0} | all-to-all | bytes 524288 | tf_op jit(solution)/shard_map/all_to_all | solution.py:281
  63.7 0.0 copy-done
  63.7 0.0 copy-done.1
  63.7 0.8 middle.1
  64.5 19.0 %all_to_all.22 = bf16[128,8,128]{2,1,0:T(8,128)(2,1)S(1)} all-to-all(bf16[128,8,128]{2,1,0:T(8,128)(2,1)S(1)} %bitcast.14), channel_id=1, replica_groups=mesh['yh'=2,'yl'=4,'zl'=2,'core'=2,'xh'=2,'xl'=2,'zh'=4] {'zh','xh','xl'..., dimensions={0} | all-to-all | bytes 524288 | tf_op jit(solution)/shard_map/all_to_all | solution.py:281
  83.5 4.5 %all_gather.7.both = bf16[2048,128]{1,0:T(8,128)(2,1)S(1)} all-gather(bf16[1024,128]{1,0:T(8,128)(2,1)S(1)} %bitcast.16), channel_id=1, replica_groups=mesh['yh'=2,'yl'=4,'zl'=2,'core'=2,'xh'=2,'xl'=2,'zh'=4] {'core'}, dimensions={0}, use_global_device_ids=true | all-gather | bytes 786432 | tf_op jit(solution)/shard_map/all_gather | solution.py:310
  88.1 1.1 incoming.1
  89.2 23.5 %all_to_all.23 = bf16[256,4,128]{2,1,0:T(4,128)(2,1)S(1)} all-to-all(bf16[256,4,128]{2,1,0:T(4,128)(2,1)S(1)} %bitcast.11), channel_id=1, replica_groups=mesh['yh'=2,'yl'=4,'zl'=2,'core'=2,'xh'=2,'xl'=2,'zh'=4] {'zh','yh','yl'..., dimensions={0} | all-to-all | bytes 524288 | tf_op jit(solution)/shard_map/all_to_all | solution.py:281
  112.7 1.2 %last.1 = bf16[14,28,128]{2,1,0:T(8,128)(2,1)} custom-call(bf16[1024,128]{1,0:T(8,128)(2,1)S(1)} %bitcast.12, f32[128,512]{1,0:T(8,128)S(1)} %get-tuple-element.19.gate, f32[128,512]{1,0:T(8,128)S(1)} %get-tuple-element.20.columns, f32[128,8]{1,0:T(8,128)S(1)} %get-tuple-element.16.vectors, bf16[2,128,128]{2,1,0:T(8,128)(2,1)S(1)} %copy-done.1), custom_call_target="tpu_custom_call" | custom-call | tf_op jit(solution)/shard_map/last/pallas_call | solution.py:263
  (2 shorter events, 0.0 us)
Async XLA Ops:
  40.2 23.5 %copy-start = (bf16[2,128,640]{2,1,0:T(8,128)(2,1)S(1)}, bf16[2,128,640]{2,1,0:T(8,128)(2,1)}, u32[]{:S(2)}) copy-start(bf16[2,128,640]{2,1,0:T(8,128)(2,1)} %weight.1) | copy-start | bytes 983044
  40.2 23.5 %copy-start.1 = (bf16[2,128,128]{2,1,0:T(8,128)(2,1)S(1)}, bf16[2,128,128]{2,1,0:T(8,128)(2,1)}, u32[]{:S(2)}) copy-start(bf16[2,128,128]{2,1,0:T(8,128)(2,1)} %weight_out.3) | copy-start | bytes 196612

commit v7 on v6

--- a/solution.py
+++ b/solution.py
@@ -8,6 +8,8 @@
 EPSILON = 1e-05
 F32 = jnp.float32
 BF16 = jnp.bfloat16
+
+SPARE = 16
 
 ROWS = 14
 COLS = 28
@@ -126,7 +128,7 @@
         send[pl.ds(m, 128, stride=8), :] = left
         send[pl.ds(4 + m, 128, stride=8), :] = right
         gate_ref[:, lanes] = jax.nn.sigmoid(projected[512:640])
-    send_ref[...] = send[...].astype(BF16)
+    send_ref[...] = send[pl.ds(0, 1024), :].astype(BF16)
 
 
 def first_kernel(
@@ -160,7 +162,7 @@
 
 
 def finish(home, source_rows, gain, bias, gate, columns, weight_out, got):
-    got[...] = home[...].astype(F32)
+    got[pl.ds(0, 1024), :] = home[...].astype(F32)
     parts = []
     for m in range(GROUPS):
         lanes = slice(m * LANES, (m + 1) * LANES)
@@ -215,12 +217,12 @@
                 at = ((m * 2 + yh) * 4 + x) * 8
                 for zh in range(4):
                     out_f[pl.ds((zh * 2 + yh) * 128 + x * 4 + m, 8, stride=16), :] = tiles[zh][at : at + 8]
-    out_ref[...] = out_f[...].astype(BF16)
+    out_ref[...] = out_f[pl.ds(0, 1024), :].astype(BF16)
 
 
 def outgoing_kernel(mine, both, out_ref, mine_f, both_f, out_f):
-    mine_f[...] = mine[...].astype(F32)
-    both_f[...] = both[...].astype(F32)
+    mine_f[pl.ds(0, 1024), :] = mine[...].astype(F32)
+    both_f[pl.ds(0, 2048), :] = both[...].astype(F32)
 
     def matrix(source, base):
         tiles = swap_groups([
@@ -240,7 +242,7 @@
 
 
 def incoming_kernel(place, both, out_ref, both_f, out_f):
-    both_f[...] = both[...].astype(F32)
+    both_f[pl.ds(0, 2048), :] = both[...].astype(F32)
 
     def matrix(base):
         tiles = swap_groups([
@@ -288,10 +290,11 @@
     tile = jax.ShapeDtypeStruct((LANES, CELLS), F32)
     sent = jax.ShapeDtypeStruct((1024, LANES), BF16)
 
+    strided = (1024 + SPARE, LANES)
     small = (jax.ShapeDtypeStruct((LANES, 8), F32), jax.ShapeDtypeStruct((1, CELLS), F32))
     send, gate, columns, vectors, mask = call(
         first_kernel, (sent, tile, tile) + small, [
-            (CELLS, LANES), (1024, LANES), (8, LANES), pltpu.SMEM(chain_lengths.shape, jnp.int32),
+            (CELLS, LANES), strided, (8, LANES), pltpu.SMEM(chain_lengths.shape, jnp.int32),
             pltpu.VMEM(pair_rep.shape, BF16), in_gain.shape, in_bias.shape, out_gain.shape, out_bias.shape,
             pltpu.VMEM(weight_in.shape[1:], BF16), pltpu.SemaphoreType.DMA((7,)),
         ], "first", range(1, 8),
@@ -299,22 +302,22 @@
     mine = exchange(send.reshape(128, 8, LANES), GROUP1).reshape(1024, LANES)
     both = lax.all_gather(mine, "core", axis=0, tiled=True)
     home = call(
-        outgoing_kernel, sent, [(1024, LANES), (2048, LANES), (1024, LANES)], "outgoing"
+        outgoing_kernel, sent, [strided, (2048 + SPARE, LANES), strided], "outgoing"
     )(mine, both)
     home = exchange(home.reshape(256, 4, LANES), BACK).reshape(1024, LANES)
 
     send, gate, columns = call(
-        middle_kernel, (sent, tile, tile), [(1024, LANES), (1024, LANES)], "middle"
+        middle_kernel, (sent, tile, tile), [strided, strided], "middle"
     )(home, gate, columns, vectors, mask, weight_in, weight_out)
     mine = exchange(send.reshape(128, 8, LANES), GROUP2).reshape(1024, LANES)
     both = lax.all_gather(mine, "core", axis=0, tiled=True)
     home = call(
-        incoming_kernel, sent, [(2048, LANES), (1024, LANES)], "incoming"
+        incoming_kernel, sent, [(2048 + SPARE, LANES), strided], "incoming"
     )(place, both)
     home = exchange(home.reshape(256, 4, LANES), BACK).reshape(1024, LANES)
 
     out = jax.ShapeDtypeStruct(pair_rep.shape, BF16)
-    return call(last_kernel, out, [(1024, LANES), (CELLS, LANES)], "last")(home, gate, columns, vectors, weight_out)
+    return call(last_kernel, out, [strided, (CELLS, LANES)], "last")(home, gate, columns, vectors, weight_out)
 
 
 def solution(mesh):

time: 115 us -> 115 us (level)
  no operation moved by 1% of the time
where the time goes in v7:
time: 115 us; the launch traced here: 114 us
  blocking collectives  108 us (94%)
  Pallas kernels  5.83 us (5%)
    all_to_all x4, blocking collectives, exchange(): return lax.all_to_all(array, axes, 0, 0, tiled=True)  98.7 us
    all_gather x2, blocking collectives, on_device(): both = lax.all_gather(mine, 'core', axis=0, tiled=True)  9.24 us
    pallas_call x5, Pallas kernels, run(): pl.pallas_call(kernel, out_shape=outs, in_specs=[pl.BlockSpec(memory_spac...  5.83 us

profile of v7, /device:TPU:1, one launch (start us, length us, event | category | flops | bytes accessed | tf_op | source)
XLA Modules:
  0.0 113.9 jit_solution(7977967790839023514)
XLA Ops:
  0.0 0.1 concatenate.6.place
  0.1 1.7 %first.1 = (bf16[1024,128]{1,0:T(8,128)(2,1)S(1)}, f32[128,512]{1,0:T(8,128)S(1)}, f32[128,512]{1,0:T(8,128)S(1)}, f32[128,8]{1,0:T(8,128)S(1)}, f32[1,512]{1,0:T(1,128)S(1)}) custom-call(s32[16,128]{1,0:T(8,128)S(1)} %concatenate.6.place, s32[4]{0:T(128)} %lengths_hbm.1, bf16[14,28,128]{2,1,0:T(8,128)(2,1)} %pair_hbm.1, f32[2,128]{1,0:T(2,128)} %in_gain_hbm.1, ...), custom_call_target="tpu_custom_call" | custom-call | tf_op jit(solution)/shard_map/first/pallas_call | solution.py:265
  1.8 32.7 %all_to_all.20 = bf16[128,8,128]{2,1,0:T(8,128)(2,1)S(1)} all-to-all(bf16[128,8,128]{2,1,0:T(8,128)(2,1)S(1)} %bitcast.15), channel_id=1, replica_groups=mesh['yh'=2,'yl'=4,'zl'=2,'core'=2,'xh'=2,'xl'=2,'zh'=4] {'zh','xl','yh'..., dimensions={0} | all-to-all | bytes 524288 | tf_op jit(solution)/shard_map/all_to_all | solution.py:283
  34.4 4.7 %all_gather.6.both = bf16[2048,128]{1,0:T(8,128)(2,1)S(1)} all-gather(bf16[1024,128]{1,0:T(8,128)(2,1)S(1)} %bitcast.8), channel_id=1, replica_groups=mesh['yh'=2,'yl'=4,'zl'=2,'core'=2,'xh'=2,'xl'=2,'zh'=4] {'core'}, dimensions={0}, use_global_device_ids=true | all-gather | bytes 786432 | tf_op jit(solution)/shard_map/all_gather | solution.py:303
  39.1 1.1 outgoing.1
  40.2 0.0 copy-start
  40.2 0.0 copy-start.1
  40.2 23.5 %all_to_all.21 = bf16[256,4,128]{2,1,0:T(4,128)(2,1)S(1)} all-to-all(bf16[256,4,128]{2,1,0:T(4,128)(2,1)S(1)} %bitcast.13), channel_id=1, replica_groups=mesh['yh'=2,'yl'=4,'zl'=2,'core'=2,'xh'=2,'xl'=2,'zh'=4] {'zh','yh','yl'..., dimensions={0} | all-to-all | bytes 524288 | tf_op jit(solution)/shard_map/all_to_all | solution.py:283
  63.7 0.0 copy-done
  63.7 0.0 copy-done.1
  63.7 0.8 middle.1
  64.5 19.0 %all_to_all.22 = bf16[128,8,128]{2,1,0:T(8,128)(2,1)S(1)} all-to-all(bf16[128,8,128]{2,1,0:T(8,128)(2,1)S(1)} %bitcast.14), channel_id=1, replica_groups=mesh['yh'=2,'yl'=4,'zl'=2,'core'=2,'xh'=2,'xl'=2,'zh'=4] {'zh','xh','xl'..., dimensions={0} | all-to-all | bytes 524288 | tf_op jit(solution)/shard_map/all_to_all | solution.py:283
  83.5 4.5 %all_gather.7.both = bf16[2048,128]{1,0:T(8,128)(2,1)S(1)} all-gather(bf16[1024,128]{1,0:T(8,128)(2,1)S(1)} %bitcast.16), channel_id=1, replica_groups=mesh['yh'=2,'yl'=4,'zl'=2,'core'=2,'xh'=2,'xl'=2,'zh'=4] {'core'}, dimensions={0}, use_global_device_ids=true | all-gather | bytes 786432 | tf_op jit(solution)/shard_map/all_gather | solution.py:313
  88.1 1.1 incoming.1
  89.2 23.5 %all_to_all.23 = bf16[256,4,128]{2,1,0:T(4,128)(2,1)S(1)} all-to-all(bf16[256,4,128]{2,1,0:T(4,128)(2,1)S(1)} %bitcast.11), channel_id=1, replica_groups=mesh['yh'=2,'yl'=4,'zl'=2,'core'=2,'xh'=2,'xl'=2,'zh'=4] {'zh','yh','yl'..., dimensions={0} | all-to-all | bytes 524288 | tf_op jit(solution)/shard_map/all_to_all | solution.py:283
  112.7 1.2 %last.1 = bf16[14,28,128]{2,1,0:T(8,128)(2,1)} custom-call(bf16[1024,128]{1,0:T(8,128)(2,1)S(1)} %bitcast.12, f32[128,512]{1,0:T(8,128)S(1)} %get-tuple-element.19.gate, f32[128,512]{1,0:T(8,128)S(1)} %get-tuple-element.20.columns, f32[128,8]{1,0:T(8,128)S(1)} %get-tuple-element.16.vectors, bf16[2,128,128]{2,1,0:T(8,128)(2,1)S(1)} %copy-done.1), custom_call_target="tpu_custom_call" | custom-call | tf_op jit(solution)/shard_map/last/pallas_call | solution.py:265
  (2 shorter events, 0.0 us)
Async XLA Ops:
  40.2 23.5 %copy-start = (bf16[2,128,640]{2,1,0:T(8,128)(2,1)S(1)}, bf16[2,128,640]{2,1,0:T(8,128)(2,1)}, u32[]{:S(2)}) copy-start(bf16[2,128,640]{2,1,0:T(8,128)(2,1)} %weight.1) | copy-start | bytes 983044
  40.2 23.5 %copy-start.1 = (bf16[2,128,128]{2,1,0:T(8,128)(2,1)S(1)}, bf16[2,128,128]{2,1,0:T(8,128)(2,1)}, u32[]{:S(2)}) copy-start(bf16[2,128,128]{2,1,0:T(8,128)(2,1)} %weight_out.3) | copy-start | bytes 196612

commit v8 on v7

--- a/solution.py
+++ b/solution.py
@@ -20,11 +20,11 @@
 SLOT = 112
 CHAINS = 4
 
-ROW_AXES = ("yh", "yl", "zl", "core")
+ROW_AXES = ("yh", "ym", "yl", "zl", "core")
 COL_AXES = ("xh", "xl", "zh")
-GROUP1 = ("zh", "xl", "yh", "yl", "zl")
-GROUP2 = ("zh", "xh", "xl", "yl", "zl")
-BACK = ("zh", "yh", "yl", "zl", "xh", "xl")
+GROUP1 = ("xh", "xl", "yh", "ym", "yl", "zl")
+GROUP2 = ("xh", "xl", "zh", "yl", "zl")
+BACK = ("zh", "xh", "xl", "yh", "ym", "yl", "zl")
 
 
 def nt_dot(left, right):
@@ -64,22 +64,6 @@
     return tiles
 
 
-def token_matrix():
-    code = lax.broadcasted_iota(jnp.int32, (8, CELLS), 1)
-    token = jnp.where(code & 31 < COLS, (code >> 5) * COLS + (code & 31), -4096)
-    token = token - COLS * lax.broadcasted_iota(jnp.int32, (8, CELLS), 0)
-    none = jnp.zeros((8, CELLS), F32)
-    rows = []
-    for core in range(2):
-        for q in range(4):
-            for m in range(GROUPS):
-                for yh in range(2):
-                    a = 4 * m + q
-                    first = yh * 8 * COLS + core * ROWS + a
-                    rows.append(jnp.where(token == first, 1.0, 0.0).astype(F32) if a < ROWS else none)
-    return jnp.concatenate(rows, axis=0).astype(BF16)
-
-
 def fields(code, *widths):
     out = []
     for width in reversed(widths):
@@ -88,16 +72,18 @@
     return out[::-1]
 
 
-def own_matrix(core):
-    q, m, yh, s = fields(lax.broadcasted_iota(jnp.int32, (8, CELLS // 2), 1), 4, 4, 2, 8)
+def token_matrix(core=None):
+    lane = lax.broadcasted_iota(jnp.int32, (8, CELLS if core is None else CELLS // 2), 1)
+    lane_core, q, m, yh, s = fields(lane, 2, 4, 4, 2, 8)
+    core = lane_core if core is None else core
     a = 4 * m + q
-    sub = lax.broadcasted_iota(jnp.int32, (8, CELLS // 2), 0)
+    sub = lax.broadcasted_iota(jnp.int32, lane.shape, 0)
     token = jnp.where(a < ROWS, ((yh * 8 + s) * 2 + core) * ROWS + a, -4096) - sub
     last = jnp.where(sub < COLS - 24, token, -4096)
-    return jnp.concatenate([
+    return stack(
         jnp.where((last if b == 24 else token) == c * COLS + b, 1.0, 0.0).astype(F32)
         for c in range(16) for b in range(0, WIDE, 8)
-    ], axis=0).astype(BF16)
+    ).astype(BF16)
 
 
 def valid_token(token, lengths_ref):
@@ -125,8 +111,10 @@
         weighting = mask[:, lanes]
         left = weighting * jax.nn.sigmoid(projected[128:256]) * projected[0:128]
         right = weighting * jax.nn.sigmoid(projected[384:512]) * projected[256:384]
-        send[pl.ds(m, 128, stride=8), :] = left
-        send[pl.ds(4 + m, 128, stride=8), :] = right
+        for channel in range(2):
+            half = slice(channel * 64, channel * 64 + 64)
+            send[pl.ds(channel * 8 + m, 64, stride=16), :] = left[half]
+            send[pl.ds(channel * 8 + 4 + m, 64, stride=16), :] = right[half]
         gate_ref[:, lanes] = jax.nn.sigmoid(projected[512:640])
     send_ref[...] = send[pl.ds(0, 1024), :].astype(BF16)
 
@@ -162,25 +150,32 @@
 
 
 def finish(home, source_rows, gain, bias, gate, columns, weight_out, got):
-    got[pl.ds(0, 1024), :] = home[...].astype(F32)
+    got[pl.ds(0, 2048), :] = home[...].astype(F32)
     parts = []
     for m in range(GROUPS):
         lanes = slice(m * LANES, (m + 1) * LANES)
-        triangle = source_rows(got, 0, m) + source_rows(got, 1, m)
-        change = tn_dot(weight_out, norm_rows(triangle, gain, bias))
+        change = tn_dot(weight_out, norm_rows(source_rows(got, m), gain, bias))
         parts.append(columns[:, lanes] + gate[:, lanes] * change)
     return jnp.concatenate(parts, axis=1).astype(BF16)
 
 
-def rows_after_first(got, xh, m):
+def rows_after_first(got, m):
     return stack(
-        got[pl.ds(zh * 256 + xh * 8 + xl * 4 + m, 16, stride=16), :] for zh in range(4) for xl in range(2)
+        sum(got[pl.ds((zh * 4 + x) * 128 + channel * 4 + m, 16, stride=8), :] for zh in range(4))
+        for channel in range(2) for x in range(4)
     )
 
 
-def rows_after_second(got, yh, m):
+def rows_after_second(got, m):
+    low = lax.broadcasted_iota(jnp.int32, (8, LANES), 0) < 4
+
+    def total(channel, x, zh):
+        half = sum(got[pl.ds(((zh * 4 + x) * 2 + yh) * 64 + channel * 4 + m, 8, stride=8), :] for yh in range(2))
+        return half + pltpu.roll(half, 4, 0)
+
     return stack(
-        got[pl.ds((zh * 2 + yh) * 128 + x * 4 + m, 8, stride=16), :] for zh in range(4) for x in range(4)
+        jnp.where(low, total(channel, x, zh), total(channel, x, zh + 1))
+        for channel in range(2) for x in range(4) for zh in range(0, 4, 2)
     )
 
 
@@ -203,21 +198,24 @@
         out_ref[a] = cells[pl.ds(a * WIDE, COLS), :].astype(BF16)
 
 
-def send_home(triangle, out_ref, out_f):
-    tiles = swap_groups([
-        stack(
-            triangle[((q * 4 + m) * 2 + yh) * 8 : ((q * 4 + m) * 2 + yh) * 8 + 8, x * 128 : x * 128 + 128]
-            for m in range(GROUPS) for yh in range(2) for x in range(4)
-        )
-        for q in range(4)
-    ])
-    for m in range(GROUPS):
-        for yh in range(2):
-            for x in range(4):
-                at = ((m * 2 + yh) * 4 + x) * 8
-                for zh in range(4):
-                    out_f[pl.ds((zh * 2 + yh) * 128 + x * 4 + m, 8, stride=16), :] = tiles[zh][at : at + 8]
-    out_ref[...] = out_f[pl.ds(0, 1024), :].astype(BF16)
+def send_home(triangles, out_ref, out_f):
+    for channel, triangle in enumerate(triangles):
+        tiles = swap_groups([
+            stack(
+                triangle[((q * 4 + m) * 2 + yh) * 8 : ((q * 4 + m) * 2 + yh) * 8 + 8, x * 128 : x * 128 + 128]
+                for m in range(GROUPS) for yh in range(2) for x in range(4)
+            )
+            for q in range(4)
+        ])
+        for m in range(GROUPS):
+            for yh in range(2):
+                for x in range(4):
+                    at = ((m * 2 + yh) * 4 + x) * 8
+                    for zh in range(4):
+                        out_f[pl.ds(((zh * 4 + x) * 2 + yh) * 64 + channel * 4 + m, 8, stride=8), :] = tiles[zh][
+                            at : at + 8
+                        ]
+    out_ref[...] = out_f[pl.ds(0, 2048), :].astype(BF16)
 
 
 def outgoing_kernel(mine, both, out_ref, mine_f, both_f, out_f):
@@ -225,39 +223,45 @@
     both_f[pl.ds(0, 2048), :] = both[...].astype(F32)
 
     def matrix(source, base):
-        tiles = swap_groups([
+        return stack(swap_groups([
             stack(
-                source[pl.ds(base + ((zh * 2 + xl) * 2 + yh) * 64 + m, 8, stride=8), :]
-                for xl in range(2) for m in range(GROUPS) for yh in range(2)
+                source[pl.ds(base + (x * 2 + yh) * 128 + m, 8, stride=16), :]
+                for m in range(GROUPS) for yh in range(2)
             )
-            for zh in range(4)
-        ])
-        half = tiles[0].shape[0] // 2
-        return stack(jnp.concatenate([tile[:half], tile[half:]], axis=1) for tile in tiles).astype(BF16)
-
-    left = matrix(mine_f, 0)
-    right = stack(matrix(both_f, core * 1024 + 4) for core in range(2))
-    triangle = nt_dot(left, right).astype(BF16)
-    send_home(nn_dot(triangle, token_matrix()), out_ref, out_f)
+            for x in range(4)
+        ])).astype(BF16)
+
+    right = jnp.concatenate([
+        stack(matrix(both_f, core * 1024 + channel * 8 + 4) for core in range(2)) for channel in range(2)
+    ], axis=1)
+    right = nn_dot(token_matrix(), right).astype(BF16)
+    send_home([
+        nt_dot(matrix(mine_f, channel * 8), right[:, channel * LANES : (channel + 1) * LANES]) for channel in range(2)
+    ], out_ref, out_f)
 
 
 def incoming_kernel(place, both, out_ref, both_f, out_f):
-    both_f[pl.ds(0, 2048), :] = both[...].astype(F32)
+    for core in range(2):
+        for at in range(64):
+            both_f[pl.ds((at * 2 + core) * 16, 16), :] = both[pl.ds((core * 64 + at) * 16, 16), :].astype(F32)
 
     def matrix(base):
         tiles = swap_groups([
             stack(
-                both_f[pl.ds(base + core * 1024 + (zh * 4 + x) * 64 + m, 8, stride=8), :]
-                for x in range(4) for m in range(GROUPS) for core in range(2)
+                both_f[pl.ds(base + (x * 4 + zh) * 128 + m, 8, stride=16), :]
+                for x in range(4) for m in range(GROUPS)
             )
             for zh in range(4)
         ])
         return stack(
-            jnp.concatenate([tile[x * 64 : x * 64 + 64] for x in range(4)], axis=1) for tile in tiles
+            jnp.concatenate([tile[x * 32 : x * 32 + 32] for x in range(4)], axis=1) for tile in tiles
         ).astype(BF16)
 
-    left = nn_dot(matrix(0), own_matrix(place[0:1, 0:1] & 1)).astype(BF16)
-    send_home(tn_dot(left, matrix(4)), out_ref, out_f)
+    left = stack(matrix(channel * 8) for channel in range(2))
+    left = nn_dot(left, token_matrix(place[0:1, 0:1] & 1)).astype(BF16)
+    send_home([
+        tn_dot(left[channel * 128 : channel * 128 + 128], matrix(channel * 8 + 4)) for channel in range(2)
+    ], out_ref, out_f)
 
 
 def call(kernel, outs, scratch, name, held=()):
@@ -289,8 +293,9 @@
     ])
     tile = jax.ShapeDtypeStruct((LANES, CELLS), F32)
     sent = jax.ShapeDtypeStruct((1024, LANES), BF16)
-
-    strided = (1024 + SPARE, LANES)
+    returned = jax.ShapeDtypeStruct((2048, LANES), BF16)
+
+    strided, longer = (1024 + SPARE, LANES), (2048 + SPARE, LANES)
     small = (jax.ShapeDtypeStruct((LANES, 8), F32), jax.ShapeDtypeStruct((1, CELLS), F32))
     send, gate, columns, vectors, mask = call(
         first_kernel, (sent, tile, tile) + small, [
@@ -299,29 +304,29 @@
             pltpu.VMEM(weight_in.shape[1:], BF16), pltpu.SemaphoreType.DMA((7,)),
         ], "first", range(1, 8),
     )(place, *map(in_hbm, (chain_lengths, pair_rep, in_gain, in_bias, weight_in, out_gain, out_bias)))
-    mine = exchange(send.reshape(128, 8, LANES), GROUP1).reshape(1024, LANES)
+    mine = exchange(send.reshape(64, 16, LANES), GROUP1).reshape(1024, LANES)
     both = lax.all_gather(mine, "core", axis=0, tiled=True)
     home = call(
-        outgoing_kernel, sent, [strided, (2048 + SPARE, LANES), strided], "outgoing"
+        outgoing_kernel, returned, [strided, longer, longer], "outgoing"
     )(mine, both)
-    home = exchange(home.reshape(256, 4, LANES), BACK).reshape(1024, LANES)
+    home = exchange(home.reshape(256, 8, LANES), BACK).reshape(2048, LANES)
 
     send, gate, columns = call(
-        middle_kernel, (sent, tile, tile), [strided, strided], "middle"
+        middle_kernel, (sent, tile, tile), [longer, strided], "middle"
     )(home, gate, columns, vectors, mask, weight_in, weight_out)
-    mine = exchange(send.reshape(128, 8, LANES), GROUP2).reshape(1024, LANES)
+    mine = exchange(send.reshape(64, 16, LANES), GROUP2).reshape(1024, LANES)
     both = lax.all_gather(mine, "core", axis=0, tiled=True)
     home = call(
-        incoming_kernel, sent, [(2048 + SPARE, LANES), strided], "incoming"
+        incoming_kernel, returned, [longer, longer], "incoming"
     )(place, both)
-    home = exchange(home.reshape(256, 4, LANES), BACK).reshape(1024, LANES)
+    home = exchange(home.reshape(256, 8, LANES), BACK).reshape(2048, LANES)
 
     out = jax.ShapeDtypeStruct(pair_rep.shape, BF16)
-    return call(last_kernel, out, [strided, (CELLS, LANES)], "last")(home, gate, columns, vectors, weight_out)
+    return call(last_kernel, out, [longer, (CELLS, LANES)], "last")(home, gate, columns, vectors, weight_out)
 
 
 def solution(mesh):
-    fine = Mesh(mesh.devices.reshape(2, 4, 2, 2, 2, 2, 4), ROW_AXES + COL_AXES)
+    fine = Mesh(mesh.devices.reshape(2, 2, 2, 2, 2, 2, 2, 4), ROW_AXES + COL_AXES)
     placed = P(ROW_AXES, COL_AXES, None)
     return jax.shard_map(
         on_device, mesh=fine, in_specs=(placed,) + (P(),) * 7, out_specs=placed, check_vma=False

time: 115 us -> 121 us (1.052)
  blocking collectives: 108 us -> 113 us
    all_to_all x4, blocking collectives: 98.7 us -> 103 us  [exchange(): return lax.all_to_all(array, axes, 0, 0, tiled=True)]
where the time goes in v8:
time: 121 us; the launch traced here: 120 us
  blocking collectives  113 us (93%)
  Pallas kernels  6.94 us (6%)
    all_to_all x4, blocking collectives, exchange(): return lax.all_to_all(array, axes, 0, 0, tiled=True)  103 us
    all_gather x2, blocking collectives, on_device(): both = lax.all_gather(mine, 'core', axis=0, tiled=True)  9.76 us
    pallas_call x5, Pallas kernels, run(): pl.pallas_call(kernel, out_shape=outs, in_specs=[pl.BlockSpec(memory_spac...  6.94 us

profile of v8, /device:TPU:1, one launch (start us, length us, event | category | flops | bytes accessed | tf_op | source)
XLA Modules:
  0.0 120.2 jit_solution(504961355398826950)
XLA Ops:
  0.0 0.1 concatenate.6.place
  0.1 1.8 %first.1 = (bf16[1024,128]{1,0:T(8,128)(2,1)S(1)}, f32[128,512]{1,0:T(8,128)S(1)}, f32[128,512]{1,0:T(8,128)S(1)}, f32[128,8]{1,0:T(8,128)S(1)}, f32[1,512]{1,0:T(1,128)S(1)}) custom-call(s32[16,128]{1,0:T(8,128)S(1)} %concatenate.6.place, s32[4]{0:T(128)} %lengths_hbm.1, bf16[14,28,128]{2,1,0:T(8,128)(2,1)} %pair_hbm.1, f32[2,128]{1,0:T(2,128)} %in_gain_hbm.1, ...), custom_call_target="tpu_custom_call" | custom-call | tf_op jit(solution)/shard_map/first/pallas_call | solution.py:269
  1.9 23.0 %all_to_all.20 = bf16[64,16,128]{2,1,0:T(8,128)(2,1)S(1)} all-to-all(bf16[64,16,128]{2,1,0:T(8,128)(2,1)S(1)} %bitcast.15), channel_id=1, replica_groups=mesh['yh'=2,'ym'=2,'yl'=2,'zl'=2,'core'=2,'xh'=2,'xl'=2,'zh'=4] {'xh','x..., dimensions={0} | all-to-all | bytes 524288 | tf_op jit(solution)/shard_map/all_to_all | solution.py:287
  24.9 4.6 %all_gather.6.both = bf16[2048,128]{1,0:T(8,128)(2,1)S(1)} all-gather(bf16[1024,128]{1,0:T(8,128)(2,1)S(1)} %bitcast.8), channel_id=1, replica_groups=mesh['yh'=2,'ym'=2,'yl'=2,'zl'=2,'core'=2,'xh'=2,'xl'=2,'zh'=4] {'core'}, dimensions={0}, use_global_device_ids=true | all-gather | bytes 786432 | tf_op jit(solution)/shard_map/all_gather | solution.py:308
  29.5 1.4 %outgoing.1 = bf16[2048,128]{1,0:T(8,128)(2,1)S(1)} custom-call(bf16[1024,128]{1,0:T(8,128)(2,1)S(1)} %bitcast.9, bf16[2048,128]{1,0:T(8,128)(2,1)S(1)} %all_gather.6.both), custom_call_target="tpu_custom_call" | custom-call | tf_op jit(solution)/shard_map/outgoing/pallas_call | solution.py:269
  30.9 0.0 copy-start
  30.9 0.0 copy-start.1
  31.0 36.2 %all_to_all.21 = bf16[256,8,128]{2,1,0:T(8,128)(2,1)S(1)} all-to-all(bf16[256,8,128]{2,1,0:T(8,128)(2,1)S(1)} %bitcast.12), channel_id=1, replica_groups=mesh['yh'=2,'ym'=2,'yl'=2,'zl'=2,'core'=2,'xh'=2,'xl'=2,'zh'=4] {'zh','x..., dimensions={0} | all-to-all | bytes 1048576 | tf_op jit(solution)/shard_map/all_to_all | solution.py:287
  67.2 0.0 copy-done
  67.2 0.0 copy-done.1
  67.2 1.0 middle.1
  68.2 15.1 %all_to_all.22 = bf16[64,16,128]{2,1,0:T(8,128)(2,1)S(1)} all-to-all(bf16[64,16,128]{2,1,0:T(8,128)(2,1)S(1)} %bitcast.14), channel_id=1, replica_groups=mesh['yh'=2,'ym'=2,'yl'=2,'zl'=2,'core'=2,'xh'=2,'xl'=2,'zh'=4] {'xh','x..., dimensions={0} | all-to-all | bytes 524288 | tf_op jit(solution)/shard_map/all_to_all | solution.py:287
  83.3 5.2 %all_gather.7.both = bf16[2048,128]{1,0:T(8,128)(2,1)S(1)} all-gather(bf16[1024,128]{1,0:T(8,128)(2,1)S(1)} %bitcast.16), channel_id=1, replica_groups=mesh['yh'=2,'ym'=2,'yl'=2,'zl'=2,'core'=2,'xh'=2,'xl'=2,'zh'=4] {'core'}, dimensions={0}, use_global_device_ids=true | all-gather | bytes 786432 | tf_op jit(solution)/shard_map/all_gather | solution.py:318
  88.5 1.5 %incoming.1 = bf16[2048,128]{1,0:T(8,128)(2,1)S(1)} custom-call(s32[16,128]{1,0:T(8,128)S(1)} %concatenate.6.place, bf16[2048,128]{1,0:T(8,128)(2,1)S(1)} %all_gather.7.both), custom_call_target="tpu_custom_call" | custom-call | tf_op jit(solution)/shard_map/incoming/pallas_call | solution.py:269
  90.0 29.0 %all_to_all.23 = bf16[256,8,128]{2,1,0:T(8,128)(2,1)S(1)} all-to-all(bf16[256,8,128]{2,1,0:T(8,128)(2,1)S(1)} %bitcast.13), channel_id=1, replica_groups=mesh['yh'=2,'ym'=2,'yl'=2,'zl'=2,'core'=2,'xh'=2,'xl'=2,'zh'=4] {'zh','x..., dimensions={0} | all-to-all | bytes 1048576 | tf_op jit(solution)/shard_map/all_to_all | solution.py:287
  118.9 1.2 %last.1 = bf16[14,28,128]{2,1,0:T(8,128)(2,1)} custom-call(bf16[2048,128]{1,0:T(8,128)(2,1)S(1)} %bitcast.11, f32[128,512]{1,0:T(8,128)S(1)} %get-tuple-element.19.gate, f32[128,512]{1,0:T(8,128)S(1)} %get-tuple-element.20.columns, f32[128,8]{1,0:T(8,128)S(1)} %get-tuple-element.16.vectors, bf16[2,128,128]{2,1,0:T(8,128)(2,1)S(1)} %copy-done.1), custom_call_target="tpu_custom_call" | custom-call | tf_op jit(solution)/shard_map/last/pallas_call | solution.py:269
  (2 shorter events, 0.0 us)
Async XLA Ops:
  30.9 36.3 %copy-start = (bf16[2,128,640]{2,1,0:T(8,128)(2,1)S(1)}, bf16[2,128,640]{2,1,0:T(8,128)(2,1)}, u32[]{:S(2)}) copy-start(bf16[2,128,640]{2,1,0:T(8,128)(2,1)} %weight.1) | copy-start | bytes 983044
  30.9 36.3 %copy-start.1 = (bf16[2,128,128]{2,1,0:T(8,128)(2,1)S(1)}, bf16[2,128,128]{2,1,0:T(8,128)(2,1)}, u32[]{:S(2)}) copy-start(bf16[2,128,128]{2,1,0:T(8,128)(2,1)} %weight_out.3) | copy-start | bytes 196612

commit v9 on v7

--- a/solution.py
+++ b/solution.py
@@ -24,7 +24,7 @@
 COL_AXES = ("xh", "xl", "zh")
 GROUP1 = ("zh", "xl", "yh", "yl", "zl")
 GROUP2 = ("zh", "xh", "xl", "yl", "zl")
-BACK = ("zh", "yh", "yl", "zl", "xh", "xl")
+BACK = ("zh", "xh", "xl", "yh", "yl", "zl")
 
 
 def nt_dot(left, right):
@@ -174,13 +174,13 @@
 
 def rows_after_first(got, xh, m):
     return stack(
-        got[pl.ds(zh * 256 + xh * 8 + xl * 4 + m, 16, stride=16), :] for zh in range(4) for xl in range(2)
+        got[pl.ds((zh * 4 + xh * 2 + xl) * 64 + m, 16, stride=4), :] for zh in range(4) for xl in range(2)
     )
 
 
 def rows_after_second(got, yh, m):
     return stack(
-        got[pl.ds((zh * 2 + yh) * 128 + x * 4 + m, 8, stride=16), :] for zh in range(4) for x in range(4)
+        got[pl.ds(((zh * 4 + x) * 2 + yh) * 32 + m, 8, stride=4), :] for zh in range(4) for x in range(4)
     )
 
 
@@ -216,7 +216,7 @@
             for x in range(4):
                 at = ((m * 2 + yh) * 4 + x) * 8
                 for zh in range(4):
-                    out_f[pl.ds((zh * 2 + yh) * 128 + x * 4 + m, 8, stride=16), :] = tiles[zh][at : at + 8]
+                    out_f[pl.ds(((zh * 4 + x) * 2 + yh) * 32 + m, 8, stride=4), :] = tiles[zh][at : at + 8]
     out_ref[...] = out_f[pl.ds(0, 1024), :].astype(BF16)
 
 

time: 115 us -> 115 us (level)
  no operation moved by 1% of the time
where the time goes in v9:
time: 115 us; the launch traced here: 114 us
  blocking collectives  109 us (95%)
  Pallas kernels  5.56 us (5%)
    all_to_all x4, blocking collectives, exchange(): return lax.all_to_all(array, axes, 0, 0, tiled=True)  98.8 us
    all_gather x2, blocking collectives, on_device(): both = lax.all_gather(mine, 'core', axis=0, tiled=True)  9.67 us
    pallas_call x5, Pallas kernels, run(): pl.pallas_call(kernel, out_shape=outs, in_specs=[pl.BlockSpec(memory_spac...  5.56 us

profile of v9, /device:TPU:1, one launch (start us, length us, event | category | flops | bytes accessed | tf_op | source)
XLA Modules:
  0.0 114.2 jit_solution(6635894125003015692)
XLA Ops:
  0.0 0.1 concatenate.6.place
  0.1 1.7 %first.1 = (bf16[1024,128]{1,0:T(8,128)(2,1)S(1)}, f32[128,512]{1,0:T(8,128)S(1)}, f32[128,512]{1,0:T(8,128)S(1)}, f32[128,8]{1,0:T(8,128)S(1)}, f32[1,512]{1,0:T(1,128)S(1)}) custom-call(s32[16,128]{1,0:T(8,128)S(1)} %concatenate.6.place, s32[4]{0:T(128)} %lengths_hbm.1, bf16[14,28,128]{2,1,0:T(8,128)(2,1)} %pair_hbm.1, f32[2,128]{1,0:T(2,128)} %in_gain_hbm.1, ...), custom_call_target="tpu_custom_call" | custom-call | tf_op jit(solution)/shard_map/first/pallas_call | solution.py:265
  1.8 32.7 %all_to_all.20 = bf16[128,8,128]{2,1,0:T(8,128)(2,1)S(1)} all-to-all(bf16[128,8,128]{2,1,0:T(8,128)(2,1)S(1)} %bitcast.15), channel_id=1, replica_groups=mesh['yh'=2,'yl'=4,'zl'=2,'core'=2,'xh'=2,'xl'=2,'zh'=4] {'zh','xl','yh'..., dimensions={0} | all-to-all | bytes 524288 | tf_op jit(solution)/shard_map/all_to_all | solution.py:283
  34.4 4.7 %all_gather.6.both = bf16[2048,128]{1,0:T(8,128)(2,1)S(1)} all-gather(bf16[1024,128]{1,0:T(8,128)(2,1)S(1)} %bitcast.8), channel_id=1, replica_groups=mesh['yh'=2,'yl'=4,'zl'=2,'core'=2,'xh'=2,'xl'=2,'zh'=4] {'core'}, dimensions={0}, use_global_device_ids=true | all-gather | bytes 786432 | tf_op jit(solution)/shard_map/all_gather | solution.py:303
  39.1 1.0 outgoing.1
  40.2 0.0 copy-start
  40.2 0.0 copy-start.1
  40.2 23.9 %all_to_all.21 = bf16[256,4,128]{2,1,0:T(4,128)(2,1)S(1)} all-to-all(bf16[256,4,128]{2,1,0:T(4,128)(2,1)S(1)} %bitcast.13), channel_id=1, replica_groups=mesh['yh'=2,'yl'=4,'zl'=2,'core'=2,'xh'=2,'xl'=2,'zh'=4] {'zh','xh','xl'..., dimensions={0} | all-to-all | bytes 524288 | tf_op jit(solution)/shard_map/all_to_all | solution.py:283
  64.1 0.0 copy-done
  64.1 0.0 copy-done.1
  64.1 0.7 middle.1
  64.8 18.2 %all_to_all.22 = bf16[128,8,128]{2,1,0:T(8,128)(2,1)S(1)} all-to-all(bf16[128,8,128]{2,1,0:T(8,128)(2,1)S(1)} %bitcast.14), channel_id=1, replica_groups=mesh['yh'=2,'yl'=4,'zl'=2,'core'=2,'xh'=2,'xl'=2,'zh'=4] {'zh','xh','xl'..., dimensions={0} | all-to-all | bytes 524288 | tf_op jit(solution)/shard_map/all_to_all | solution.py:283
  83.1 5.0 %all_gather.7.both = bf16[2048,128]{1,0:T(8,128)(2,1)S(1)} all-gather(bf16[1024,128]{1,0:T(8,128)(2,1)S(1)} %bitcast.16), channel_id=1, replica_groups=mesh['yh'=2,'yl'=4,'zl'=2,'core'=2,'xh'=2,'xl'=2,'zh'=4] {'core'}, dimensions={0}, use_global_device_ids=true | all-gather | bytes 786432 | tf_op jit(solution)/shard_map/all_gather | solution.py:313
  88.0 1.1 incoming.1
  89.1 24.0 %all_to_all.23 = bf16[256,4,128]{2,1,0:T(4,128)(2,1)S(1)} all-to-all(bf16[256,4,128]{2,1,0:T(4,128)(2,1)S(1)} %bitcast.11), channel_id=1, replica_groups=mesh['yh'=2,'yl'=4,'zl'=2,'core'=2,'xh'=2,'xl'=2,'zh'=4] {'zh','xh','xl'..., dimensions={0} | all-to-all | bytes 524288 | tf_op jit(solution)/shard_map/all_to_all | solution.py:283
  113.2 1.0 last.1
  (2 shorter events, 0.0 us)
Async XLA Ops:
  40.2 23.9 %copy-start = (bf16[2,128,640]{2,1,0:T(8,128)(2,1)S(1)}, bf16[2,128,640]{2,1,0:T(8,128)(2,1)}, u32[]{:S(2)}) copy-start(bf16[2,128,640]{2,1,0:T(8,128)(2,1)} %weight.1) | copy-start | bytes 983044
  40.2 23.9 %copy-start.1 = (bf16[2,128,128]{2,1,0:T(8,128)(2,1)S(1)}, bf16[2,128,128]{2,1,0:T(8,128)(2,1)}, u32[]{:S(2)}) copy-start(bf16[2,128,128]{2,1,0:T(8,128)(2,1)} %weight_out.3) | copy-start | bytes 196612

commit v10 on v9

--- a/solution.py
+++ b/solution.py
@@ -9,7 +9,7 @@
 F32 = jnp.float32
 BF16 = jnp.bfloat16
 
-SPARE = 16
+SPARE = 64
 
 ROWS = 14
 COLS = 28
@@ -24,7 +24,7 @@
 COL_AXES = ("xh", "xl", "zh")
 GROUP1 = ("zh", "xl", "yh", "yl", "zl")
 GROUP2 = ("zh", "xh", "xl", "yl", "zl")
-BACK = ("zh", "xh", "xl", "yh", "yl", "zl")
+BACK = ("yh", "yl", "zl", "xh", "xl", "zh")
 
 
 def nt_dot(left, right):
@@ -174,13 +174,13 @@
 
 def rows_after_first(got, xh, m):
     return stack(
-        got[pl.ds((zh * 4 + xh * 2 + xl) * 64 + m, 16, stride=4), :] for zh in range(4) for xl in range(2)
+        got[pl.ds((xh * 2 + xl) * 16 + zh * 4 + m, 16, stride=64), :] for zh in range(4) for xl in range(2)
     )
 
 
 def rows_after_second(got, yh, m):
     return stack(
-        got[pl.ds(((zh * 4 + x) * 2 + yh) * 32 + m, 8, stride=4), :] for zh in range(4) for x in range(4)
+        got[pl.ds(yh * 512 + x * 16 + zh * 4 + m, 8, stride=64), :] for zh in range(4) for x in range(4)
     )
 
 
@@ -216,7 +216,7 @@
             for x in range(4):
                 at = ((m * 2 + yh) * 4 + x) * 8
                 for zh in range(4):
-                    out_f[pl.ds(((zh * 4 + x) * 2 + yh) * 32 + m, 8, stride=4), :] = tiles[zh][at : at + 8]
+                    out_f[pl.ds(yh * 512 + x * 16 + zh * 4 + m, 8, stride=64), :] = tiles[zh][at : at + 8]
     out_ref[...] = out_f[pl.ds(0, 1024), :].astype(BF16)
 
 

time: 115 us -> 114 us (level)
  blocking collectives: 109 us -> 107 us
where the time goes in v10:
time: 114 us
  blocking collectives  107 us (94%)
  Pallas kernels  6.53 us (6%)
    all_to_all x4, blocking collectives, exchange(): return lax.all_to_all(array, axes, 0, 0, tiled=True)  97.7 us
    all_gather x2, blocking collectives, on_device(): both = lax.all_gather(mine, 'core', axis=0, tiled=True)  9.39 us
    pallas_call x5, Pallas kernels, run(): pl.pallas_call(kernel, out_shape=outs, in_specs=[pl.BlockSpec(memory_spac...  6.53 us

profile of v10, /device:TPU:1, one launch (start us, length us, event | category | flops | bytes accessed | tf_op | source)
XLA Modules:
  0.0 113.8 jit_solution(16734036358270211694)
XLA Ops:
  0.0 0.1 concatenate.6.place
  0.1 1.7 %first.1 = (bf16[1024,128]{1,0:T(8,128)(2,1)S(1)}, f32[128,512]{1,0:T(8,128)S(1)}, f32[128,512]{1,0:T(8,128)S(1)}, f32[128,8]{1,0:T(8,128)S(1)}, f32[1,512]{1,0:T(1,128)S(1)}) custom-call(s32[16,128]{1,0:T(8,128)S(1)} %concatenate.6.place, s32[4]{0:T(128)} %lengths_hbm.1, bf16[14,28,128]{2,1,0:T(8,128)(2,1)} %pair_hbm.1, f32[2,128]{1,0:T(2,128)} %in_gain_hbm.1, ...), custom_call_target="tpu_custom_call" | custom-call | tf_op jit(solution)/shard_map/first/pallas_call | solution.py:265
  1.8 32.7 %all_to_all.20 = bf16[128,8,128]{2,1,0:T(8,128)(2,1)S(1)} all-to-all(bf16[128,8,128]{2,1,0:T(8,128)(2,1)S(1)} %bitcast.15), channel_id=1, replica_groups=mesh['yh'=2,'yl'=4,'zl'=2,'core'=2,'xh'=2,'xl'=2,'zh'=4] {'zh','xl','yh'..., dimensions={0} | all-to-all | bytes 524288 | tf_op jit(solution)/shard_map/all_to_all | solution.py:283
  34.4 4.7 %all_gather.6.both = bf16[2048,128]{1,0:T(8,128)(2,1)S(1)} all-gather(bf16[1024,128]{1,0:T(8,128)(2,1)S(1)} %bitcast.8), channel_id=1, replica_groups=mesh['yh'=2,'yl'=4,'zl'=2,'core'=2,'xh'=2,'xl'=2,'zh'=4] {'core'}, dimensions={0}, use_global_device_ids=true | all-gather | bytes 786432 | tf_op jit(solution)/shard_map/all_gather | solution.py:303
  39.1 1.3 %outgoing.1 = bf16[1024,128]{1,0:T(8,128)(2,1)S(1)} custom-call(bf16[1024,128]{1,0:T(8,128)(2,1)S(1)} %bitcast.9, bf16[2048,128]{1,0:T(8,128)(2,1)S(1)} %all_gather.6.both), custom_call_target="tpu_custom_call" | custom-call | tf_op jit(solution)/shard_map/outgoing/pallas_call | solution.py:265
  40.4 0.0 copy-start
  40.4 0.0 copy-start.1
  40.5 23.2 %all_to_all.21 = bf16[256,4,128]{2,1,0:T(4,128)(2,1)S(1)} all-to-all(bf16[256,4,128]{2,1,0:T(4,128)(2,1)S(1)} %bitcast.13), channel_id=1, replica_groups=mesh['yh'=2,'yl'=4,'zl'=2,'core'=2,'xh'=2,'xl'=2,'zh'=4] {'yh','yl','zl'..., dimensions={0} | all-to-all | bytes 524288 | tf_op jit(solution)/shard_map/all_to_all | solution.py:283
  63.6 0.0 copy-done
  63.6 0.0 copy-done.1
  63.6 1.0 middle.1
  64.6 18.9 %all_to_all.22 = bf16[128,8,128]{2,1,0:T(8,128)(2,1)S(1)} all-to-all(bf16[128,8,128]{2,1,0:T(8,128)(2,1)S(1)} %bitcast.14), channel_id=1, replica_groups=mesh['yh'=2,'yl'=4,'zl'=2,'core'=2,'xh'=2,'xl'=2,'zh'=4] {'zh','xh','xl'..., dimensions={0} | all-to-all | bytes 524288 | tf_op jit(solution)/shard_map/all_to_all | solution.py:283
  83.5 4.7 %all_gather.7.both = bf16[2048,128]{1,0:T(8,128)(2,1)S(1)} all-gather(bf16[1024,128]{1,0:T(8,128)(2,1)S(1)} %bitcast.16), channel_id=1, replica_groups=mesh['yh'=2,'yl'=4,'zl'=2,'core'=2,'xh'=2,'xl'=2,'zh'=4] {'core'}, dimensions={0}, use_global_device_ids=true | all-gather | bytes 786432 | tf_op jit(solution)/shard_map/all_gather | solution.py:313
  88.2 1.3 %incoming.1 = bf16[1024,128]{1,0:T(8,128)(2,1)S(1)} custom-call(s32[16,128]{1,0:T(8,128)S(1)} %concatenate.6.place, bf16[2048,128]{1,0:T(8,128)(2,1)S(1)} %all_gather.7.both), custom_call_target="tpu_custom_call" | custom-call | tf_op jit(solution)/shard_map/incoming/pallas_call | solution.py:265
  89.5 23.0 %all_to_all.23 = bf16[256,4,128]{2,1,0:T(4,128)(2,1)S(1)} all-to-all(bf16[256,4,128]{2,1,0:T(4,128)(2,1)S(1)} %bitcast.11), channel_id=1, replica_groups=mesh['yh'=2,'yl'=4,'zl'=2,'core'=2,'xh'=2,'xl'=2,'zh'=4] {'yh','yl','zl'..., dimensions={0} | all-to-all | bytes 524288 | tf_op jit(solution)/shard_map/all_to_all | solution.py:283
  112.5 1.3 %last.1 = bf16[14,28,128]{2,1,0:T(8,128)(2,1)} custom-call(bf16[1024,128]{1,0:T(8,128)(2,1)S(1)} %bitcast.12, f32[128,512]{1,0:T(8,128)S(1)} %get-tuple-element.19.gate, f32[128,512]{1,0:T(8,128)S(1)} %get-tuple-element.20.columns, f32[128,8]{1,0:T(8,128)S(1)} %get-tuple-element.16.vectors, bf16[2,128,128]{2,1,0:T(8,128)(2,1)S(1)} %copy-done.1), custom_call_target="tpu_custom_call" | custom-call | tf_op jit(solution)/shard_map/last/pallas_call | solution.py:265
  (2 shorter events, 0.0 us)
Async XLA Ops:
  40.4 23.2 %copy-start = (bf16[2,128,640]{2,1,0:T(8,128)(2,1)S(1)}, bf16[2,128,640]{2,1,0:T(8,128)(2,1)}, u32[]{:S(2)}) copy-start(bf16[2,128,640]{2,1,0:T(8,128)(2,1)} %weight.1) | copy-start | bytes 983044
  40.4 23.2 %copy-start.1 = (bf16[2,128,128]{2,1,0:T(8,128)(2,1)S(1)}, bf16[2,128,128]{2,1,0:T(8,128)(2,1)}, u32[]{:S(2)}) copy-start(bf16[2,128,128]{2,1,0:T(8,128)(2,1)} %weight_out.3) | copy-start | bytes 196612

commit v11 on v10

--- a/solution.py
+++ b/solution.py
@@ -9,7 +9,8 @@
 F32 = jnp.float32
 BF16 = jnp.bfloat16
 
-SPARE = 64
+SPARE = 8
+PITCH = 72
 
 ROWS = 14
 COLS = 28
@@ -162,7 +163,8 @@
 
 
 def finish(home, source_rows, gain, bias, gate, columns, weight_out, got):
-    got[pl.ds(0, 1024), :] = home[...].astype(F32)
+    for at in range(16):
+        got[pl.ds(at * PITCH, 64), :] = home[pl.ds(at * 64, 64), :].astype(F32)
     parts = []
     for m in range(GROUPS):
         lanes = slice(m * LANES, (m + 1) * LANES)
@@ -174,13 +176,13 @@
 
 def rows_after_first(got, xh, m):
     return stack(
-        got[pl.ds((xh * 2 + xl) * 16 + zh * 4 + m, 16, stride=64), :] for zh in range(4) for xl in range(2)
+        got[pl.ds((xh * 2 + xl) * 16 + zh * 4 + m, 16, stride=PITCH), :] for zh in range(4) for xl in range(2)
     )
 
 
 def rows_after_second(got, yh, m):
     return stack(
-        got[pl.ds(yh * 512 + x * 16 + zh * 4 + m, 8, stride=64), :] for zh in range(4) for x in range(4)
+        got[pl.ds(yh * 8 * PITCH + x * 16 + zh * 4 + m, 8, stride=PITCH), :] for zh in range(4) for x in range(4)
     )
 
 
@@ -216,8 +218,9 @@
             for x in range(4):
                 at = ((m * 2 + yh) * 4 + x) * 8
                 for zh in range(4):
-                    out_f[pl.ds(yh * 512 + x * 16 + zh * 4 + m, 8, stride=64), :] = tiles[zh][at : at + 8]
-    out_ref[...] = out_f[pl.ds(0, 1024), :].astype(BF16)
+                    out_f[pl.ds(yh * 8 * PITCH + x * 16 + zh * 4 + m, 8, stride=PITCH), :] = tiles[zh][at : at + 8]
+    for at in range(16):
+        out_ref[pl.ds(at * 64, 64), :] = out_f[pl.ds(at * PITCH, 64), :].astype(BF16)
 
 
 def outgoing_kernel(mine, both, out_ref, mine_f, both_f, out_f):
@@ -290,7 +293,7 @@
     tile = jax.ShapeDtypeStruct((LANES, CELLS), F32)
     sent = jax.ShapeDtypeStruct((1024, LANES), BF16)
 
-    strided = (1024 + SPARE, LANES)
+    strided, spread = (1024 + SPARE, LANES), (17 * PITCH, LANES)
     small = (jax.ShapeDtypeStruct((LANES, 8), F32), jax.ShapeDtypeStruct((1, CELLS), F32))
     send, gate, columns, vectors, mask = call(
         first_kernel, (sent, tile, tile) + small, [
@@ -302,22 +305,22 @@
     mine = exchange(send.reshape(128, 8, LANES), GROUP1).reshape(1024, LANES)
     both = lax.all_gather(mine, "core", axis=0, tiled=True)
     home = call(
-        outgoing_kernel, sent, [strided, (2048 + SPARE, LANES), strided], "outgoing"
+        outgoing_kernel, sent, [strided, (2048 + SPARE, LANES), spread], "outgoing"
     )(mine, both)
     home = exchange(home.reshape(256, 4, LANES), BACK).reshape(1024, LANES)
 
     send, gate, columns = call(
-        middle_kernel, (sent, tile, tile), [strided, strided], "middle"
+        middle_kernel, (sent, tile, tile), [spread, strided], "middle"
     )(home, gate, columns, vectors, mask, weight_in, weight_out)
     mine = exchange(send.reshape(128, 8, LANES), GROUP2).reshape(1024, LANES)
     both = lax.all_gather(mine, "core", axis=0, tiled=True)
     home = call(
-        incoming_kernel, sent, [(2048 + SPARE, LANES), strided], "incoming"
+        incoming_kernel, sent, [(2048 + SPARE, LANES), spread], "incoming"
     )(place, both)
     home = exchange(home.reshape(256, 4, LANES), BACK).reshape(1024, LANES)
 
     out = jax.ShapeDtypeStruct(pair_rep.shape, BF16)
-    return call(last_kernel, out, [strided, (CELLS, LANES)], "last")(home, gate, columns, vectors, weight_out)
+    return call(last_kernel, out, [spread, (CELLS, LANES)], "last")(home, gate, columns, vectors, weight_out)
 
 
 def solution(mesh):

time: 114 us -> 113 us (level)
  no operation moved by 1% of the time
where the time goes in v11:
time: 113 us
  blocking collectives  107 us (95%)
  Pallas kernels  5.64 us (5%)
    all_to_all x4, blocking collectives, exchange(): return lax.all_to_all(array, axes, 0, 0, tiled=True)  97.7 us
    all_gather x2, blocking collectives, on_device(): both = lax.all_gather(mine, 'core', axis=0, tiled=True)  9.39 us
    pallas_call x5, Pallas kernels, run(): pl.pallas_call(kernel, out_shape=outs, in_specs=[pl.BlockSpec(memory_spac...  5.64 us

profile of v11, /device:TPU:1, one launch (start us, length us, event | category | flops | bytes accessed | tf_op | source)
XLA Modules:
  0.0 112.9 jit_solution(14407200768831567637)
XLA Ops:
  0.0 0.1 concatenate.6.place
  0.1 1.7 %first.1 = (bf16[1024,128]{1,0:T(8,128)(2,1)S(1)}, f32[128,512]{1,0:T(8,128)S(1)}, f32[128,512]{1,0:T(8,128)S(1)}, f32[128,8]{1,0:T(8,128)S(1)}, f32[1,512]{1,0:T(1,128)S(1)}) custom-call(s32[16,128]{1,0:T(8,128)S(1)} %concatenate.6.place, s32[4]{0:T(128)} %lengths_hbm.1, bf16[14,28,128]{2,1,0:T(8,128)(2,1)} %pair_hbm.1, f32[2,128]{1,0:T(2,128)} %in_gain_hbm.1, ...), custom_call_target="tpu_custom_call" | custom-call | tf_op jit(solution)/shard_map/first/pallas_call | solution.py:268
  1.8 32.7 %all_to_all.20 = bf16[128,8,128]{2,1,0:T(8,128)(2,1)S(1)} all-to-all(bf16[128,8,128]{2,1,0:T(8,128)(2,1)S(1)} %bitcast.15), channel_id=1, replica_groups=mesh['yh'=2,'yl'=4,'zl'=2,'core'=2,'xh'=2,'xl'=2,'zh'=4] {'zh','xl','yh'..., dimensions={0} | all-to-all | bytes 524288 | tf_op jit(solution)/shard_map/all_to_all | solution.py:286
  34.4 4.7 %all_gather.6.both = bf16[2048,128]{1,0:T(8,128)(2,1)S(1)} all-gather(bf16[1024,128]{1,0:T(8,128)(2,1)S(1)} %bitcast.8), channel_id=1, replica_groups=mesh['yh'=2,'yl'=4,'zl'=2,'core'=2,'xh'=2,'xl'=2,'zh'=4] {'core'}, dimensions={0}, use_global_device_ids=true | all-gather | bytes 786432 | tf_op jit(solution)/shard_map/all_gather | solution.py:306
  39.1 1.1 outgoing.1
  40.2 0.0 copy-start
  40.2 0.0 copy-start.1
  40.2 23.2 %all_to_all.21 = bf16[256,4,128]{2,1,0:T(4,128)(2,1)S(1)} all-to-all(bf16[256,4,128]{2,1,0:T(4,128)(2,1)S(1)} %bitcast.13), channel_id=1, replica_groups=mesh['yh'=2,'yl'=4,'zl'=2,'core'=2,'xh'=2,'xl'=2,'zh'=4] {'yh','yl','zl'..., dimensions={0} | all-to-all | bytes 524288 | tf_op jit(solution)/shard_map/all_to_all | solution.py:286
  63.4 0.0 copy-done
  63.4 0.0 copy-done.1
  63.4 0.7 middle.1
  64.2 18.9 %all_to_all.22 = bf16[128,8,128]{2,1,0:T(8,128)(2,1)S(1)} all-to-all(bf16[128,8,128]{2,1,0:T(8,128)(2,1)S(1)} %bitcast.14), channel_id=1, replica_groups=mesh['yh'=2,'yl'=4,'zl'=2,'core'=2,'xh'=2,'xl'=2,'zh'=4] {'zh','xh','xl'..., dimensions={0} | all-to-all | bytes 524288 | tf_op jit(solution)/shard_map/all_to_all | solution.py:286
  83.0 4.7 %all_gather.7.both = bf16[2048,128]{1,0:T(8,128)(2,1)S(1)} all-gather(bf16[1024,128]{1,0:T(8,128)(2,1)S(1)} %bitcast.16), channel_id=1, replica_groups=mesh['yh'=2,'yl'=4,'zl'=2,'core'=2,'xh'=2,'xl'=2,'zh'=4] {'core'}, dimensions={0}, use_global_device_ids=true | all-gather | bytes 786432 | tf_op jit(solution)/shard_map/all_gather | solution.py:316
  87.7 1.1 incoming.1
  88.8 23.0 %all_to_all.23 = bf16[256,4,128]{2,1,0:T(4,128)(2,1)S(1)} all-to-all(bf16[256,4,128]{2,1,0:T(4,128)(2,1)S(1)} %bitcast.11), channel_id=1, replica_groups=mesh['yh'=2,'yl'=4,'zl'=2,'core'=2,'xh'=2,'xl'=2,'zh'=4] {'yh','yl','zl'..., dimensions={0} | all-to-all | bytes 524288 | tf_op jit(solution)/shard_map/all_to_all | solution.py:286
  111.8 1.1 last.1
  (2 shorter events, 0.0 us)
Async XLA Ops:
  40.2 23.2 %copy-start = (bf16[2,128,640]{2,1,0:T(8,128)(2,1)S(1)}, bf16[2,128,640]{2,1,0:T(8,128)(2,1)}, u32[]{:S(2)}) copy-start(bf16[2,128,640]{2,1,0:T(8,128)(2,1)} %weight.1) | copy-start | bytes 983044
  40.2 23.2 %copy-start.1 = (bf16[2,128,128]{2,1,0:T(8,128)(2,1)S(1)}, bf16[2,128,128]{2,1,0:T(8,128)(2,1)}, u32[]{:S(2)}) copy-start(bf16[2,128,128]{2,1,0:T(8,128)(2,1)} %weight_out.3) | copy-start | bytes 196612

commit v12 on v11

--- a/solution.py
+++ b/solution.py
@@ -11,6 +11,7 @@
 
 SPARE = 8
 PITCH = 72
+WIDE_PITCH = 136
 
 ROWS = 14
 COLS = 28
@@ -24,7 +25,7 @@
 ROW_AXES = ("yh", "yl", "zl", "core")
 COL_AXES = ("xh", "xl", "zh")
 GROUP1 = ("zh", "xl", "yh", "yl", "zl")
-GROUP2 = ("zh", "xh", "xl", "yl", "zl")
+GROUP2 = ("yl", "zl", "xh", "xl", "zh")
 BACK = ("yh", "yl", "zl", "xh", "xl", "zh")
 
 
@@ -118,7 +119,17 @@
     return jnp.where(row & col & inside, 1.0, 0.0).astype(F32)
 
 
-def project(columns, mask, gain, bias, weight, send, send_ref, gate_ref):
+def store_in_order(send, values, row):
+    send[pl.ds(row, 128, stride=8), :] = values
+
+
+def store_across(send, values, row):
+    for at in range(16):
+        start = (at % 4 * 4 + at // 4) * 8 + row
+        send[pl.ds(start, 8, stride=WIDE_PITCH), :] = values[at * 8 : at * 8 + 8]
+
+
+def project(columns, mask, gain, bias, weight, store, send, gate_ref):
     for m in range(GROUPS):
         lanes = slice(m * LANES, (m + 1) * LANES)
         normed = norm_rows(columns[:, lanes], gain, bias)
@@ -126,10 +137,9 @@
         weighting = mask[:, lanes]
         left = weighting * jax.nn.sigmoid(projected[128:256]) * projected[0:128]
         right = weighting * jax.nn.sigmoid(projected[384:512]) * projected[256:384]
-        send[pl.ds(m, 128, stride=8), :] = left
-        send[pl.ds(4 + m, 128, stride=8), :] = right
+        store(send, left, m)
+        store(send, right, 4 + m)
         gate_ref[:, lanes] = jax.nn.sigmoid(projected[512:640])
-    send_ref[...] = send[pl.ds(0, 1024), :].astype(BF16)
 
 
 def first_kernel(
@@ -159,7 +169,8 @@
         cells[pl.ds(a * WIDE, COLS), :] = pair[a].astype(F32)
     columns = cells[...].T
     columns_ref[...] = columns
-    project(columns, mask, vectors[:, 0:1], vectors[:, 2:3], weight[...], send, send_ref, gate_ref)
+    project(columns, mask, vectors[:, 0:1], vectors[:, 2:3], weight[...], store_in_order, send, gate_ref)
+    send_ref[...] = send[pl.ds(0, 1024), :].astype(BF16)
 
 
 def finish(home, source_rows, gain, bias, gate, columns, weight_out, got):
@@ -193,7 +204,9 @@
         home, rows_after_first, vectors[:, 4:5], vectors[:, 6:7], gate, columns, weight_out[0], got
     ).astype(F32)
     columns_ref[...] = middle
-    project(middle, mask, vectors[:, 1:2], vectors[:, 3:4], weight[1], send, send_ref, gate_ref)
+    project(middle, mask, vectors[:, 1:2], vectors[:, 3:4], weight[1], store_across, send, gate_ref)
+    for at in range(8):
+        send_ref[pl.ds(at * 128, 128), :] = send[pl.ds(at * WIDE_PITCH, 128), :].astype(BF16)
 
 
 def last_kernel(home, gate, columns, vectors, weight_out, out_ref, got, cells):
@@ -245,12 +258,13 @@
 
 
 def incoming_kernel(place, both, out_ref, both_f, out_f):
-    both_f[pl.ds(0, 2048), :] = both[...].astype(F32)
+    for at in range(16):
+        both_f[pl.ds(at * WIDE_PITCH, 128), :] = both[pl.ds(at * 128, 128), :].astype(F32)
 
     def matrix(base):
         tiles = swap_groups([
             stack(
-                both_f[pl.ds(base + core * 1024 + (zh * 4 + x) * 64 + m, 8, stride=8), :]
+                both_f[pl.ds(base + core * 8 * WIDE_PITCH + (x * 4 + zh) * 8 + m, 8, stride=WIDE_PITCH), :]
                 for x in range(4) for m in range(GROUPS) for core in range(2)
             )
             for zh in range(4)
@@ -310,12 +324,12 @@
     home = exchange(home.reshape(256, 4, LANES), BACK).reshape(1024, LANES)
 
     send, gate, columns = call(
-        middle_kernel, (sent, tile, tile), [spread, strided], "middle"
+        middle_kernel, (sent, tile, tile), [spread, (9 * WIDE_PITCH, LANES)], "middle"
     )(home, gate, columns, vectors, mask, weight_in, weight_out)
     mine = exchange(send.reshape(128, 8, LANES), GROUP2).reshape(1024, LANES)
     both = lax.all_gather(mine, "core", axis=0, tiled=True)
     home = call(
-        incoming_kernel, sent, [(2048 + SPARE, LANES), spread], "incoming"
+        incoming_kernel, sent, [(17 * WIDE_PITCH, LANES), spread], "incoming"
     )(place, both)
     home = exchange(home.reshape(256, 4, LANES), BACK).reshape(1024, LANES)
 

time: 113 us -> 113 us (level)
    all_gather x2, blocking collectives: 9.39 us -> 10.7 us  [on_device(): both = lax.all_gather(mine, 'core', axis=0, tiled=True)]
    all_to_all x4, blocking collectives: 97.7 us -> 96.5 us  [exchange(): return lax.all_to_all(array, axes, 0, 0, tiled=True)]
where the time goes in v12:
time: 113 us
  blocking collectives  107 us (95%)
  Pallas kernels  5.65 us (5%)
    all_to_all x4, blocking collectives, exchange(): return lax.all_to_all(array, axes, 0, 0, tiled=True)  96.5 us
    all_gather x2, blocking collectives, on_device(): both = lax.all_gather(mine, 'core', axis=0, tiled=True)  10.7 us
    pallas_call x5, Pallas kernels, run(): pl.pallas_call(kernel, out_shape=outs, in_specs=[pl.BlockSpec(memory_spac...  5.65 us

profile of v12, /device:TPU:1, one launch (start us, length us, event | category | flops | bytes accessed | tf_op | source)
XLA Modules:
  0.0 113.1 jit_solution(7077671575145688828)
XLA Ops:
  0.0 0.1 concatenate.6.place
  0.1 1.7 %first.1 = (bf16[1024,128]{1,0:T(8,128)(2,1)S(1)}, f32[128,512]{1,0:T(8,128)S(1)}, f32[128,512]{1,0:T(8,128)S(1)}, f32[128,8]{1,0:T(8,128)S(1)}, f32[1,512]{1,0:T(1,128)S(1)}) custom-call(s32[16,128]{1,0:T(8,128)S(1)} %concatenate.6.place, s32[4]{0:T(128)} %lengths_hbm.1, bf16[14,28,128]{2,1,0:T(8,128)(2,1)} %pair_hbm.1, f32[2,128]{1,0:T(2,128)} %in_gain_hbm.1, ...), custom_call_target="tpu_custom_call" | custom-call | tf_op jit(solution)/shard_map/first/pallas_call | solution.py:282
  1.8 32.7 %all_to_all.20 = bf16[128,8,128]{2,1,0:T(8,128)(2,1)S(1)} all-to-all(bf16[128,8,128]{2,1,0:T(8,128)(2,1)S(1)} %bitcast.15), channel_id=1, replica_groups=mesh['yh'=2,'yl'=4,'zl'=2,'core'=2,'xh'=2,'xl'=2,'zh'=4] {'zh','xl','yh'..., dimensions={0} | all-to-all | bytes 524288 | tf_op jit(solution)/shard_map/all_to_all | solution.py:300
  34.4 4.7 %all_gather.6.both = bf16[2048,128]{1,0:T(8,128)(2,1)S(1)} all-gather(bf16[1024,128]{1,0:T(8,128)(2,1)S(1)} %bitcast.8), channel_id=1, replica_groups=mesh['yh'=2,'yl'=4,'zl'=2,'core'=2,'xh'=2,'xl'=2,'zh'=4] {'core'}, dimensions={0}, use_global_device_ids=true | all-gather | bytes 786432 | tf_op jit(solution)/shard_map/all_gather | solution.py:320
  39.1 1.1 outgoing.1
  40.2 0.0 copy-start
  40.2 0.0 copy-start.1
  40.2 23.2 %all_to_all.21 = bf16[256,4,128]{2,1,0:T(4,128)(2,1)S(1)} all-to-all(bf16[256,4,128]{2,1,0:T(4,128)(2,1)S(1)} %bitcast.13), channel_id=1, replica_groups=mesh['yh'=2,'yl'=4,'zl'=2,'core'=2,'xh'=2,'xl'=2,'zh'=4] {'yh','yl','zl'..., dimensions={0} | all-to-all | bytes 524288 | tf_op jit(solution)/shard_map/all_to_all | solution.py:300
  63.4 0.0 copy-done
  63.4 0.0 copy-done.1
  63.4 0.7 middle.1
  64.2 17.8 %all_to_all.22 = bf16[128,8,128]{2,1,0:T(8,128)(2,1)S(1)} all-to-all(bf16[128,8,128]{2,1,0:T(8,128)(2,1)S(1)} %bitcast.14), channel_id=1, replica_groups=mesh['yh'=2,'yl'=4,'zl'=2,'core'=2,'xh'=2,'xl'=2,'zh'=4] {'yl','zl','xh'..., dimensions={0} | all-to-all | bytes 524288 | tf_op jit(solution)/shard_map/all_to_all | solution.py:300
  82.0 6.0 %all_gather.7.both = bf16[2048,128]{1,0:T(8,128)(2,1)S(1)} all-gather(bf16[1024,128]{1,0:T(8,128)(2,1)S(1)} %bitcast.16), channel_id=1, replica_groups=mesh['yh'=2,'yl'=4,'zl'=2,'core'=2,'xh'=2,'xl'=2,'zh'=4] {'core'}, dimensions={0}, use_global_device_ids=true | all-gather | bytes 786432 | tf_op jit(solution)/shard_map/all_gather | solution.py:330
  88.0 1.1 incoming.1
  89.1 22.9 %all_to_all.23 = bf16[256,4,128]{2,1,0:T(4,128)(2,1)S(1)} all-to-all(bf16[256,4,128]{2,1,0:T(4,128)(2,1)S(1)} %bitcast.11), channel_id=1, replica_groups=mesh['yh'=2,'yl'=4,'zl'=2,'core'=2,'xh'=2,'xl'=2,'zh'=4] {'yh','yl','zl'..., dimensions={0} | all-to-all | bytes 524288 | tf_op jit(solution)/shard_map/all_to_all | solution.py:300
  112.0 1.1 last.1
  (2 shorter events, 0.0 us)
Async XLA Ops:
  40.2 23.2 %copy-start = (bf16[2,128,640]{2,1,0:T(8,128)(2,1)S(1)}, bf16[2,128,640]{2,1,0:T(8,128)(2,1)}, u32[]{:S(2)}) copy-start(bf16[2,128,640]{2,1,0:T(8,128)(2,1)} %weight.1) | copy-start | bytes 983044
  40.2 23.2 %copy-start.1 = (bf16[2,128,128]{2,1,0:T(8,128)(2,1)S(1)}, bf16[2,128,128]{2,1,0:T(8,128)(2,1)}, u32[]{:S(2)}) copy-start(bf16[2,128,128]{2,1,0:T(8,128)(2,1)} %weight_out.3) | copy-start | bytes 196612

commit v13 on v11

--- a/solution.py
+++ b/solution.py
@@ -23,7 +23,7 @@
 
 ROW_AXES = ("yh", "yl", "zl", "core")
 COL_AXES = ("xh", "xl", "zh")
-GROUP1 = ("zh", "xl", "yh", "yl", "zl")
+GROUP1 = ("yh", "yl", "zl", "xl", "zh")
 GROUP2 = ("zh", "xh", "xl", "yl", "zl")
 BACK = ("yh", "yl", "zl", "xh", "xl", "zh")
 
@@ -118,7 +118,18 @@
     return jnp.where(row & col & inside, 1.0, 0.0).astype(F32)
 
 
-def project(columns, mask, gain, bias, weight, send, send_ref, gate_ref):
+def store_across(send, values, row):
+    for zh in range(4):
+        for xl in range(2):
+            start, at = (xl * 4 + zh) * 8 + row, (zh * 2 + xl) * 16
+            send[pl.ds(start, 16, stride=PITCH), :] = values[at : at + 16]
+
+
+def store_in_order(send, values, row):
+    send[pl.ds(row, 128, stride=8), :] = values
+
+
+def project(columns, mask, gain, bias, weight, store, send, gate_ref):
     for m in range(GROUPS):
         lanes = slice(m * LANES, (m + 1) * LANES)
         normed = norm_rows(columns[:, lanes], gain, bias)
@@ -126,10 +137,9 @@
         weighting = mask[:, lanes]
         left = weighting * jax.nn.sigmoid(projected[128:256]) * projected[0:128]
         right = weighting * jax.nn.sigmoid(projected[384:512]) * projected[256:384]
-        send[pl.ds(m, 128, stride=8), :] = left
-        send[pl.ds(4 + m, 128, stride=8), :] = right
+        store(send, left, m)
+        store(send, right, 4 + m)
         gate_ref[:, lanes] = jax.nn.sigmoid(projected[512:640])
-    send_ref[...] = send[pl.ds(0, 1024), :].astype(BF16)
 
 
 def first_kernel(
@@ -159,7 +169,9 @@
         cells[pl.ds(a * WIDE, COLS), :] = pair[a].astype(F32)
     columns = cells[...].T
     columns_ref[...] = columns
-    project(columns, mask, vectors[:, 0:1], vectors[:, 2:3], weight[...], send, send_ref, gate_ref)
+    project(columns, mask, vectors[:, 0:1], vectors[:, 2:3], weight[...], store_across, send, gate_ref)
+    for at in range(16):
+        send_ref[pl.ds(at * 64, 64), :] = send[pl.ds(at * PITCH, 64), :].astype(BF16)
 
 
 def finish(home, source_rows, gain, bias, gate, columns, weight_out, got):
@@ -193,7 +205,8 @@
         home, rows_after_first, vectors[:, 4:5], vectors[:, 6:7], gate, columns, weight_out[0], got
     ).astype(F32)
     columns_ref[...] = middle
-    project(middle, mask, vectors[:, 1:2], vectors[:, 3:4], weight[1], send, send_ref, gate_ref)
+    project(middle, mask, vectors[:, 1:2], vectors[:, 3:4], weight[1], store_in_order, send, gate_ref)
+    send_ref[...] = send[pl.ds(0, 1024), :].astype(BF16)
 
 
 def last_kernel(home, gate, columns, vectors, weight_out, out_ref, got, cells):
@@ -224,13 +237,15 @@
 
 
 def outgoing_kernel(mine, both, out_ref, mine_f, both_f, out_f):
-    mine_f[pl.ds(0, 1024), :] = mine[...].astype(F32)
-    both_f[pl.ds(0, 2048), :] = both[...].astype(F32)
+    for at in range(16):
+        mine_f[pl.ds(at * PITCH, 64), :] = mine[pl.ds(at * 64, 64), :].astype(F32)
+    for at in range(32):
+        both_f[pl.ds(at * PITCH, 64), :] = both[pl.ds(at * 64, 64), :].astype(F32)
 
     def matrix(source, base):
         tiles = swap_groups([
             stack(
-                source[pl.ds(base + ((zh * 2 + xl) * 2 + yh) * 64 + m, 8, stride=8), :]
+                source[pl.ds(base + yh * 8 * PITCH + (xl * 4 + zh) * 8 + m, 8, stride=PITCH), :]
                 for xl in range(2) for m in range(GROUPS) for yh in range(2)
             )
             for zh in range(4)
@@ -239,7 +254,7 @@
         return stack(jnp.concatenate([tile[:half], tile[half:]], axis=1) for tile in tiles).astype(BF16)
 
     left = matrix(mine_f, 0)
-    right = stack(matrix(both_f, core * 1024 + 4) for core in range(2))
+    right = stack(matrix(both_f, core * 16 * PITCH + 4) for core in range(2))
     triangle = nt_dot(left, right).astype(BF16)
     send_home(nn_dot(triangle, token_matrix()), out_ref, out_f)
 
@@ -297,7 +312,7 @@
     small = (jax.ShapeDtypeStruct((LANES, 8), F32), jax.ShapeDtypeStruct((1, CELLS), F32))
     send, gate, columns, vectors, mask = call(
         first_kernel, (sent, tile, tile) + small, [
-            (CELLS, LANES), strided, (8, LANES), pltpu.SMEM(chain_lengths.shape, jnp.int32),
+            (CELLS, LANES), spread, (8, LANES), pltpu.SMEM(chain_lengths.shape, jnp.int32),
             pltpu.VMEM(pair_rep.shape, BF16), in_gain.shape, in_bias.shape, out_gain.shape, out_bias.shape,
             pltpu.VMEM(weight_in.shape[1:], BF16), pltpu.SemaphoreType.DMA((7,)),
         ], "first", range(1, 8),
@@ -305,7 +320,7 @@
     mine = exchange(send.reshape(128, 8, LANES), GROUP1).reshape(1024, LANES)
     both = lax.all_gather(mine, "core", axis=0, tiled=True)
     home = call(
-        outgoing_kernel, sent, [strided, (2048 + SPARE, LANES), spread], "outgoing"
+        outgoing_kernel, sent, [spread, (33 * PITCH, LANES), spread], "outgoing"
     )(mine, both)
     home = exchange(home.reshape(256, 4, LANES), BACK).reshape(1024, LANES)
 

time: 113 us -> 113 us (level)
  no operation moved by 1% of the time
where the time goes in v13:
time: 113 us
  blocking collectives  107 us (95%)
  Pallas kernels  5.65 us (5%)
    all_to_all x4, blocking collectives, exchange(): return lax.all_to_all(array, axes, 0, 0, tiled=True)  97.3 us
    all_gather x2, blocking collectives, on_device(): both = lax.all_gather(mine, 'core', axis=0, tiled=True)  9.64 us
    pallas_call x5, Pallas kernels, run(): pl.pallas_call(kernel, out_shape=outs, in_specs=[pl.BlockSpec(memory_spac...  5.65 us

profile of v13, /device:TPU:1, one launch (start us, length us, event | category | flops | bytes accessed | tf_op | source)
XLA Modules:
  0.0 112.7 jit_solution(8900348440415902297)
XLA Ops:
  0.0 0.1 concatenate.6.place
  0.1 1.7 %first.1 = (bf16[1024,128]{1,0:T(8,128)(2,1)S(1)}, f32[128,512]{1,0:T(8,128)S(1)}, f32[128,512]{1,0:T(8,128)S(1)}, f32[128,8]{1,0:T(8,128)S(1)}, f32[1,512]{1,0:T(1,128)S(1)}) custom-call(s32[16,128]{1,0:T(8,128)S(1)} %concatenate.6.place, s32[4]{0:T(128)} %lengths_hbm.1, bf16[14,28,128]{2,1,0:T(8,128)(2,1)} %pair_hbm.1, f32[2,128]{1,0:T(2,128)} %in_gain_hbm.1, ...), custom_call_target="tpu_custom_call" | custom-call | tf_op jit(solution)/shard_map/first/pallas_call | solution.py:283
  1.8 31.5 %all_to_all.20 = bf16[128,8,128]{2,1,0:T(8,128)(2,1)S(1)} all-to-all(bf16[128,8,128]{2,1,0:T(8,128)(2,1)S(1)} %bitcast.15), channel_id=1, replica_groups=mesh['yh'=2,'yl'=4,'zl'=2,'core'=2,'xh'=2,'xl'=2,'zh'=4] {'yh','yl','zl'..., dimensions={0} | all-to-all | bytes 524288 | tf_op jit(solution)/shard_map/all_to_all | solution.py:301
  33.2 5.0 %all_gather.6.both = bf16[2048,128]{1,0:T(8,128)(2,1)S(1)} all-gather(bf16[1024,128]{1,0:T(8,128)(2,1)S(1)} %bitcast.8), channel_id=1, replica_groups=mesh['yh'=2,'yl'=4,'zl'=2,'core'=2,'xh'=2,'xl'=2,'zh'=4] {'core'}, dimensions={0}, use_global_device_ids=true | all-gather | bytes 786432 | tf_op jit(solution)/shard_map/all_gather | solution.py:321
  38.2 1.1 outgoing.1
  39.3 0.0 copy-start
  39.3 0.0 copy-start.1
  39.3 23.9 %all_to_all.21 = bf16[256,4,128]{2,1,0:T(4,128)(2,1)S(1)} all-to-all(bf16[256,4,128]{2,1,0:T(4,128)(2,1)S(1)} %bitcast.13), channel_id=1, replica_groups=mesh['yh'=2,'yl'=4,'zl'=2,'core'=2,'xh'=2,'xl'=2,'zh'=4] {'yh','yl','zl'..., dimensions={0} | all-to-all | bytes 524288 | tf_op jit(solution)/shard_map/all_to_all | solution.py:301
  63.2 0.0 copy-done
  63.2 0.0 copy-done.1
  63.2 0.7 middle.1
  64.0 18.9 %all_to_all.22 = bf16[128,8,128]{2,1,0:T(8,128)(2,1)S(1)} all-to-all(bf16[128,8,128]{2,1,0:T(8,128)(2,1)S(1)} %bitcast.14), channel_id=1, replica_groups=mesh['yh'=2,'yl'=4,'zl'=2,'core'=2,'xh'=2,'xl'=2,'zh'=4] {'zh','xh','xl'..., dimensions={0} | all-to-all | bytes 524288 | tf_op jit(solution)/shard_map/all_to_all | solution.py:301
  82.8 4.7 %all_gather.7.both = bf16[2048,128]{1,0:T(8,128)(2,1)S(1)} all-gather(bf16[1024,128]{1,0:T(8,128)(2,1)S(1)} %bitcast.16), channel_id=1, replica_groups=mesh['yh'=2,'yl'=4,'zl'=2,'core'=2,'xh'=2,'xl'=2,'zh'=4] {'core'}, dimensions={0}, use_global_device_ids=true | all-gather | bytes 786432 | tf_op jit(solution)/shard_map/all_gather | solution.py:331
  87.5 1.1 incoming.1
  88.6 23.0 %all_to_all.23 = bf16[256,4,128]{2,1,0:T(4,128)(2,1)S(1)} all-to-all(bf16[256,4,128]{2,1,0:T(4,128)(2,1)S(1)} %bitcast.11), channel_id=1, replica_groups=mesh['yh'=2,'yl'=4,'zl'=2,'core'=2,'xh'=2,'xl'=2,'zh'=4] {'yh','yl','zl'..., dimensions={0} | all-to-all | bytes 524288 | tf_op jit(solution)/shard_map/all_to_all | solution.py:301
  111.6 1.1 last.1
  (2 shorter events, 0.0 us)
Async XLA Ops:
  39.3 24.0 %copy-start = (bf16[2,128,640]{2,1,0:T(8,128)(2,1)S(1)}, bf16[2,128,640]{2,1,0:T(8,128)(2,1)}, u32[]{:S(2)}) copy-start(bf16[2,128,640]{2,1,0:T(8,128)(2,1)} %weight.1) | copy-start | bytes 983044
  39.3 23.9 %copy-start.1 = (bf16[2,128,128]{2,1,0:T(8,128)(2,1)S(1)}, bf16[2,128,128]{2,1,0:T(8,128)(2,1)}, u32[]{:S(2)}) copy-start(bf16[2,128,128]{2,1,0:T(8,128)(2,1)} %weight_out.3) | copy-start | bytes 196612

commit v14 on v11

--- a/solution.py
+++ b/solution.py
@@ -165,13 +165,11 @@
 def finish(home, source_rows, gain, bias, gate, columns, weight_out, got):
     for at in range(16):
         got[pl.ds(at * PITCH, 64), :] = home[pl.ds(at * 64, 64), :].astype(F32)
-    parts = []
     for m in range(GROUPS):
         lanes = slice(m * LANES, (m + 1) * LANES)
         triangle = source_rows(got, 0, m) + source_rows(got, 1, m)
         change = tn_dot(weight_out, norm_rows(triangle, gain, bias))
-        parts.append(columns[:, lanes] + gate[:, lanes] * change)
-    return jnp.concatenate(parts, axis=1).astype(BF16)
+        yield (columns[:, lanes] + gate[:, lanes] * change).astype(BF16).astype(F32)
 
 
 def rows_after_first(got, xh, m):
@@ -189,20 +187,27 @@
 def middle_kernel(
     home, gate, columns, vectors, mask, weight, weight_out, send_ref, gate_ref, columns_ref, got, send
 ):
-    middle = finish(
+    middle = jnp.concatenate(list(finish(
         home, rows_after_first, vectors[:, 4:5], vectors[:, 6:7], gate, columns, weight_out[0], got
-    ).astype(F32)
+    )), axis=1)
     columns_ref[...] = middle
     project(middle, mask, vectors[:, 1:2], vectors[:, 3:4], weight[1], send, send_ref, gate_ref)
 
 
-def last_kernel(home, gate, columns, vectors, weight_out, out_ref, got, cells):
-    updated = finish(
-        home, rows_after_second, vectors[:, 5:6], vectors[:, 7:8], gate, columns, weight_out[1], got
-    ).astype(F32)
-    cells[...] = updated.T
-    for a in range(ROWS):
-        out_ref[a] = cells[pl.ds(a * WIDE, COLS), :].astype(BF16)
+def last_kernel(home, gate, columns, vectors, weight_out, out_hbm, got, cells, done, sems):
+    copies = [
+        pltpu.make_async_copy(done.at[part], out_hbm.at[part], sems.at[at])
+        for at, part in enumerate((pl.ds(0, 8), pl.ds(8, ROWS - 8)))
+    ]
+    updated = finish(home, rows_after_second, vectors[:, 5:6], vectors[:, 7:8], gate, columns, weight_out[1], got)
+    for m, part in enumerate(updated):
+        cells[pl.ds(m * LANES, LANES), :] = part.T
+        for a in range(4 * m, min(4 * m + 4, ROWS)):
+            done[a] = cells[pl.ds(a * WIDE, COLS), :].astype(BF16)
+        if m % 2 == 1:
+            copies[m // 2].start()
+    for copy in copies:
+        copy.wait()
 
 
 def send_home(triangle, out_ref, out_f):
@@ -263,13 +268,13 @@
     send_home(tn_dot(left, matrix(4)), out_ref, out_f)
 
 
-def call(kernel, outs, scratch, name, held=()):
+def call(kernel, outs, scratch, name, held=(), out_space=pltpu.VMEM):
     def run(*args):
         return pl.pallas_call(
             kernel,
             out_shape=outs,
             in_specs=[pl.BlockSpec(memory_space=pltpu.HBM if at in held else pltpu.VMEM) for at in range(len(args))],
-            out_specs=jax.tree.map(lambda _: pl.BlockSpec(memory_space=pltpu.VMEM), outs),
+            out_specs=jax.tree.map(lambda _: pl.BlockSpec(memory_space=out_space), outs),
             scratch_shapes=[pltpu.VMEM(entry, F32) if isinstance(entry, tuple) else entry for entry in scratch],
             compiler_params=pltpu.CompilerParams(vmem_limit_bytes=32 * 1024 * 1024),
             name=name,
@@ -320,7 +325,10 @@
     home = exchange(home.reshape(256, 4, LANES), BACK).reshape(1024, LANES)
 
     out = jax.ShapeDtypeStruct(pair_rep.shape, BF16)
-    return call(last_kernel, out, [spread, (CELLS, LANES)], "last")(home, gate, columns, vectors, weight_out)
+    return call(
+        last_kernel, out, [spread, (CELLS, LANES), pltpu.VMEM(out.shape, BF16), pltpu.SemaphoreType.DMA((2,))], "last",
+        out_space=pltpu.HBM,
+    )(home, gate, columns, vectors, weight_out)
 
 
 def solution(mesh):

time: 113 us -> 113 us (level)
  no operation moved by 1% of the time
where the time goes in v14:
time: 113 us
  blocking collectives  107 us (95%)
  Pallas kernels  5.63 us (5%)
    all_to_all x4, blocking collectives, exchange(): return lax.all_to_all(array, axes, 0, 0, tiled=True)  97.7 us
    all_gather x2, blocking collectives, on_device(): both = lax.all_gather(mine, 'core', axis=0, tiled=True)  9.39 us
    pallas_call x5, Pallas kernels, run(): pl.pallas_call(kernel, out_shape=outs, in_specs=[pl.BlockSpec(memory_spac...  5.63 us

profile of v14, /device:TPU:1, one launch (start us, length us, event | category | flops | bytes accessed | tf_op | source)
XLA Modules:
  0.0 113.0 jit_solution(6861310159291131490)
XLA Ops:
  0.0 0.1 concatenate.6.place
  0.1 1.7 %first.1 = (bf16[1024,128]{1,0:T(8,128)(2,1)S(1)}, f32[128,512]{1,0:T(8,128)S(1)}, f32[128,512]{1,0:T(8,128)S(1)}, f32[128,8]{1,0:T(8,128)S(1)}, f32[1,512]{1,0:T(1,128)S(1)}) custom-call(s32[16,128]{1,0:T(8,128)S(1)} %concatenate.6.place, s32[4]{0:T(128)} %lengths_hbm.1, bf16[14,28,128]{2,1,0:T(8,128)(2,1)} %pair_hbm.1, f32[2,128]{1,0:T(2,128)} %in_gain_hbm.1, ...), custom_call_target="tpu_custom_call" | custom-call | tf_op jit(solution)/shard_map/first/pallas_call | solution.py:273
  1.8 32.7 %all_to_all.20 = bf16[128,8,128]{2,1,0:T(8,128)(2,1)S(1)} all-to-all(bf16[128,8,128]{2,1,0:T(8,128)(2,1)S(1)} %bitcast.15), channel_id=1, replica_groups=mesh['yh'=2,'yl'=4,'zl'=2,'core'=2,'xh'=2,'xl'=2,'zh'=4] {'zh','xl','yh'..., dimensions={0} | all-to-all | bytes 524288 | tf_op jit(solution)/shard_map/all_to_all | solution.py:291
  34.4 4.7 %all_gather.6.both = bf16[2048,128]{1,0:T(8,128)(2,1)S(1)} all-gather(bf16[1024,128]{1,0:T(8,128)(2,1)S(1)} %bitcast.8), channel_id=1, replica_groups=mesh['yh'=2,'yl'=4,'zl'=2,'core'=2,'xh'=2,'xl'=2,'zh'=4] {'core'}, dimensions={0}, use_global_device_ids=true | all-gather | bytes 786432 | tf_op jit(solution)/shard_map/all_gather | solution.py:311
  39.1 1.1 outgoing.1
  40.2 0.0 copy-start
  40.2 0.0 copy-start.1
  40.2 23.2 %all_to_all.21 = bf16[256,4,128]{2,1,0:T(4,128)(2,1)S(1)} all-to-all(bf16[256,4,128]{2,1,0:T(4,128)(2,1)S(1)} %bitcast.13), channel_id=1, replica_groups=mesh['yh'=2,'yl'=4,'zl'=2,'core'=2,'xh'=2,'xl'=2,'zh'=4] {'yh','yl','zl'..., dimensions={0} | all-to-all | bytes 524288 | tf_op jit(solution)/shard_map/all_to_all | solution.py:291
  63.4 0.0 copy-done
  63.4 0.0 copy-done.1
  63.4 0.7 middle.1
  64.2 18.9 %all_to_all.22 = bf16[128,8,128]{2,1,0:T(8,128)(2,1)S(1)} all-to-all(bf16[128,8,128]{2,1,0:T(8,128)(2,1)S(1)} %bitcast.14), channel_id=1, replica_groups=mesh['yh'=2,'yl'=4,'zl'=2,'core'=2,'xh'=2,'xl'=2,'zh'=4] {'zh','xh','xl'..., dimensions={0} | all-to-all | bytes 524288 | tf_op jit(solution)/shard_map/all_to_all | solution.py:291
  83.0 4.7 %all_gather.7.both = bf16[2048,128]{1,0:T(8,128)(2,1)S(1)} all-gather(bf16[1024,128]{1,0:T(8,128)(2,1)S(1)} %bitcast.16), channel_id=1, replica_groups=mesh['yh'=2,'yl'=4,'zl'=2,'core'=2,'xh'=2,'xl'=2,'zh'=4] {'core'}, dimensions={0}, use_global_device_ids=true | all-gather | bytes 786432 | tf_op jit(solution)/shard_map/all_gather | solution.py:321
  87.7 1.1 incoming.1
  88.8 23.0 %all_to_all.23 = bf16[256,4,128]{2,1,0:T(4,128)(2,1)S(1)} all-to-all(bf16[256,4,128]{2,1,0:T(4,128)(2,1)S(1)} %bitcast.11), channel_id=1, replica_groups=mesh['yh'=2,'yl'=4,'zl'=2,'core'=2,'xh'=2,'xl'=2,'zh'=4] {'yh','yl','zl'..., dimensions={0} | all-to-all | bytes 524288 | tf_op jit(solution)/shard_map/all_to_all | solution.py:291
  111.8 1.1 last.1
  (2 shorter events, 0.0 us)
Async XLA Ops:
  40.2 23.2 %copy-start = (bf16[2,128,640]{2,1,0:T(8,128)(2,1)S(1)}, bf16[2,128,640]{2,1,0:T(8,128)(2,1)}, u32[]{:S(2)}) copy-start(bf16[2,128,640]{2,1,0:T(8,128)(2,1)} %weight.1) | copy-start | bytes 983044
  40.2 23.2 %copy-start.1 = (bf16[2,128,128]{2,1,0:T(8,128)(2,1)S(1)}, bf16[2,128,128]{2,1,0:T(8,128)(2,1)}, u32[]{:S(2)}) copy-start(bf16[2,128,128]{2,1,0:T(8,128)(2,1)} %weight_out.3) | copy-start | bytes 196612

commit v15 on v11

--- a/solution.py
+++ b/solution.py
@@ -225,12 +225,12 @@
 
 def outgoing_kernel(mine, both, out_ref, mine_f, both_f, out_f):
     mine_f[pl.ds(0, 1024), :] = mine[...].astype(F32)
-    both_f[pl.ds(0, 2048), :] = both[...].astype(F32)
-
-    def matrix(source, base):
+    both_f[pl.ds(0, 1024), :] = both[...].astype(F32)
+
+    def matrix(source, base, stride):
         tiles = swap_groups([
             stack(
-                source[pl.ds(base + ((zh * 2 + xl) * 2 + yh) * 64 + m, 8, stride=8), :]
+                source[pl.ds(base + ((zh * 2 + xl) * 2 + yh) * 8 * stride + m, 8, stride=stride), :]
                 for xl in range(2) for m in range(GROUPS) for yh in range(2)
             )
             for zh in range(4)
@@ -238,8 +238,8 @@
         half = tiles[0].shape[0] // 2
         return stack(jnp.concatenate([tile[:half], tile[half:]], axis=1) for tile in tiles).astype(BF16)
 
-    left = matrix(mine_f, 0)
-    right = stack(matrix(both_f, core * 1024 + 4) for core in range(2))
+    left = matrix(mine_f, 0, 8)
+    right = stack(matrix(both_f, core * 512, 4) for core in range(2))
     triangle = nt_dot(left, right).astype(BF16)
     send_home(nn_dot(triangle, token_matrix()), out_ref, out_f)
 
@@ -302,11 +302,11 @@
             pltpu.VMEM(weight_in.shape[1:], BF16), pltpu.SemaphoreType.DMA((7,)),
         ], "first", range(1, 8),
     )(place, *map(in_hbm, (chain_lengths, pair_rep, in_gain, in_bias, weight_in, out_gain, out_bias)))
-    mine = exchange(send.reshape(128, 8, LANES), GROUP1).reshape(1024, LANES)
-    both = lax.all_gather(mine, "core", axis=0, tiled=True)
+    mine = exchange(send.reshape(128, 8, LANES), GROUP1)
+    both = lax.all_gather(mine[:, 4:].reshape(512, LANES), "core", axis=0, tiled=True)
     home = call(
-        outgoing_kernel, sent, [strided, (2048 + SPARE, LANES), spread], "outgoing"
-    )(mine, both)
+        outgoing_kernel, sent, [strided, strided, spread], "outgoing"
+    )(mine.reshape(1024, LANES), both)
     home = exchange(home.reshape(256, 4, LANES), BACK).reshape(1024, LANES)
 
     send, gate, columns = call(

time: 113 us -> 113 us (level)
    all_gather x2 -> x1, blocking collectives: 9.39 us -> 4.66 us  [on_device(): both = lax.all_gather(mine, 'core', axis=0, tiled=True)]
    all_gather x0 -> x1, blocking collectives: none -> 4.54 us  [on_device(): lax.all_gather(mine[:, 4:].reshape(512, LANES), 'core', axis=0, tiled=True)]
where the time goes in v15:
time: 113 us
  blocking collectives  107 us (95%)
  Pallas kernels  5.64 us (5%)
    all_to_all x4, blocking collectives, exchange(): return lax.all_to_all(array, axes, 0, 0, tiled=True)  97.8 us
    pallas_call x5, Pallas kernels, run(): pl.pallas_call(kernel, out_shape=outs, in_specs=[pl.BlockSpec(memory_spac...  5.64 us
    all_gather x1, blocking collectives, on_device(): both = lax.all_gather(mine, 'core', axis=0, tiled=True)  4.66 us
    all_gather x1, blocking collectives, on_device(): lax.all_gather(mine[:, 4:].reshape(512, LANES), 'core', axis=0, tiled=True)  4.54 us

profile of v15, /device:TPU:1, one launch (start us, length us, event | category | flops | bytes accessed | tf_op | source)
XLA Modules:
  0.0 112.8 jit_solution(9048735723434440555)
XLA Ops:
  0.0 0.1 concatenate.6.place
  0.1 1.7 %first.1 = (bf16[1024,128]{1,0:T(8,128)(2,1)S(1)}, f32[128,512]{1,0:T(8,128)S(1)}, f32[128,512]{1,0:T(8,128)S(1)}, f32[128,8]{1,0:T(8,128)S(1)}, f32[1,512]{1,0:T(1,128)S(1)}) custom-call(s32[16,128]{1,0:T(8,128)S(1)} %concatenate.6.place, s32[4]{0:T(128)} %lengths_hbm.1, bf16[14,28,128]{2,1,0:T(8,128)(2,1)} %pair_hbm.1, f32[2,128]{1,0:T(2,128)} %in_gain_hbm.1, ...), custom_call_target="tpu_custom_call" | custom-call | tf_op jit(solution)/shard_map/first/pallas_call | solution.py:268
  1.8 32.7 %all_to_all.20 = bf16[128,8,128]{2,1,0:T(8,128)(2,1)S(1)} all-to-all(bf16[128,8,128]{2,1,0:T(8,128)(2,1)S(1)} %bitcast.15), channel_id=1, replica_groups=mesh['yh'=2,'yl'=4,'zl'=2,'core'=2,'xh'=2,'xl'=2,'zh'=4] {'zh','xl','yh'..., dimensions={0} | all-to-all | bytes 524288 | tf_op jit(solution)/shard_map/all_to_all | solution.py:286
  34.4 0.1 slice.4
  34.5 4.5 %all_gather.6.both = bf16[1024,128]{1,0:T(8,128)(2,1)S(1)} all-gather(bf16[512,128]{1,0:T(8,128)(2,1)S(1)} %bitcast.17), channel_id=1, replica_groups=mesh['yh'=2,'yl'=4,'zl'=2,'core'=2,'xh'=2,'xl'=2,'zh'=4] {'core'}, dimensions={0}, use_global_device_ids=true | all-gather | bytes 393216 | tf_op jit(solution)/shard_map/all_gather | solution.py:306
  39.0 1.1 outgoing.1
  40.1 0.0 copy-start
  40.1 0.0 copy-start.1
  40.2 23.1 %all_to_all.21 = bf16[256,4,128]{2,1,0:T(4,128)(2,1)S(1)} all-to-all(bf16[256,4,128]{2,1,0:T(4,128)(2,1)S(1)} %bitcast.11), channel_id=1, replica_groups=mesh['yh'=2,'yl'=4,'zl'=2,'core'=2,'xh'=2,'xl'=2,'zh'=4] {'yh','yl','zl'..., dimensions={0} | all-to-all | bytes 524288 | tf_op jit(solution)/shard_map/all_to_all | solution.py:286
  63.3 0.0 copy-done
  63.3 0.0 copy-done.1
  63.3 0.7 middle.1
  64.0 18.9 %all_to_all.22 = bf16[128,8,128]{2,1,0:T(8,128)(2,1)S(1)} all-to-all(bf16[128,8,128]{2,1,0:T(8,128)(2,1)S(1)} %bitcast.14), channel_id=1, replica_groups=mesh['yh'=2,'yl'=4,'zl'=2,'core'=2,'xh'=2,'xl'=2,'zh'=4] {'zh','xh','xl'..., dimensions={0} | all-to-all | bytes 524288 | tf_op jit(solution)/shard_map/all_to_all | solution.py:286
  82.9 4.7 %all_gather.7.both = bf16[2048,128]{1,0:T(8,128)(2,1)S(1)} all-gather(bf16[1024,128]{1,0:T(8,128)(2,1)S(1)} %bitcast.16), channel_id=1, replica_groups=mesh['yh'=2,'yl'=4,'zl'=2,'core'=2,'xh'=2,'xl'=2,'zh'=4] {'core'}, dimensions={0}, use_global_device_ids=true | all-gather | bytes 786432 | tf_op jit(solution)/shard_map/all_gather | solution.py:316
  87.6 1.1 incoming.1
  88.7 23.1 %all_to_all.23 = bf16[256,4,128]{2,1,0:T(4,128)(2,1)S(1)} all-to-all(bf16[256,4,128]{2,1,0:T(4,128)(2,1)S(1)} %bitcast.12), channel_id=1, replica_groups=mesh['yh'=2,'yl'=4,'zl'=2,'core'=2,'xh'=2,'xl'=2,'zh'=4] {'yh','yl','zl'..., dimensions={0} | all-to-all | bytes 524288 | tf_op jit(solution)/shard_map/all_to_all | solution.py:286
  111.8 1.1 last.1
  (2 shorter events, 0.0 us)
Async XLA Ops:
  40.1 23.2 %copy-start = (bf16[2,128,640]{2,1,0:T(8,128)(2,1)S(1)}, bf16[2,128,640]{2,1,0:T(8,128)(2,1)}, u32[]{:S(2)}) copy-start(bf16[2,128,640]{2,1,0:T(8,128)(2,1)} %weight.1) | copy-start | bytes 983044
  40.1 23.2 %copy-start.1 = (bf16[2,128,128]{2,1,0:T(8,128)(2,1)S(1)}, bf16[2,128,128]{2,1,0:T(8,128)(2,1)}, u32[]{:S(2)}) copy-start(bf16[2,128,128]{2,1,0:T(8,128)(2,1)} %weight_out.3) | copy-start | bytes 196612

commit v16 on v14

--- a/solution.py
+++ b/solution.py
@@ -23,7 +23,7 @@
 
 ROW_AXES = ("yh", "yl", "zl", "core")
 COL_AXES = ("xh", "xl", "zh")
-GROUP1 = ("zh", "xl", "yh", "yl", "zl")
+GROUP1 = ("yh", "yl", "zl", "xl", "zh")
 GROUP2 = ("zh", "xh", "xl", "yl", "zl")
 BACK = ("yh", "yl", "zl", "xh", "xl", "zh")
 
@@ -118,7 +118,18 @@
     return jnp.where(row & col & inside, 1.0, 0.0).astype(F32)
 
 
-def project(columns, mask, gain, bias, weight, send, send_ref, gate_ref):
+def store_across(send, values, row):
+    for zh in range(4):
+        for xl in range(2):
+            start, at = (xl * 4 + zh) * 8 + row, (zh * 2 + xl) * 16
+            send[pl.ds(start, 16, stride=PITCH), :] = values[at : at + 16]
+
+
+def store_in_order(send, values, row):
+    send[pl.ds(row, 128, stride=8), :] = values
+
+
+def project(columns, mask, gain, bias, weight, store, send, gate_ref):
     for m in range(GROUPS):
         lanes = slice(m * LANES, (m + 1) * LANES)
         normed = norm_rows(columns[:, lanes], gain, bias)
@@ -126,10 +137,9 @@
         weighting = mask[:, lanes]
         left = weighting * jax.nn.sigmoid(projected[128:256]) * projected[0:128]
         right = weighting * jax.nn.sigmoid(projected[384:512]) * projected[256:384]
-        send[pl.ds(m, 128, stride=8), :] = left
-        send[pl.ds(4 + m, 128, stride=8), :] = right
+        store(send, left, m)
+        store(send, right, 4 + m)
         gate_ref[:, lanes] = jax.nn.sigmoid(projected[512:640])
-    send_ref[...] = send[pl.ds(0, 1024), :].astype(BF16)
 
 
 def first_kernel(
@@ -159,7 +169,9 @@
         cells[pl.ds(a * WIDE, COLS), :] = pair[a].astype(F32)
     columns = cells[...].T
     columns_ref[...] = columns
-    project(columns, mask, vectors[:, 0:1], vectors[:, 2:3], weight[...], send, send_ref, gate_ref)
+    project(columns, mask, vectors[:, 0:1], vectors[:, 2:3], weight[...], store_across, send, gate_ref)
+    for at in range(16):
+        send_ref[pl.ds(at * 64, 64), :] = send[pl.ds(at * PITCH, 64), :].astype(BF16)
 
 
 def finish(home, source_rows, gain, bias, gate, columns, weight_out, got):
@@ -191,7 +203,8 @@
         home, rows_after_first, vectors[:, 4:5], vectors[:, 6:7], gate, columns, weight_out[0], got
     )), axis=1)
     columns_ref[...] = middle
-    project(middle, mask, vectors[:, 1:2], vectors[:, 3:4], weight[1], send, send_ref, gate_ref)
+    project(middle, mask, vectors[:, 1:2], vectors[:, 3:4], weight[1], store_in_order, send, gate_ref)
+    send_ref[...] = send[pl.ds(0, 1024), :].astype(BF16)
 
 
 def last_kernel(home, gate, columns, vectors, weight_out, out_hbm, got, cells, done, sems):
@@ -229,13 +242,15 @@
 
 
 def outgoing_kernel(mine, both, out_ref, mine_f, both_f, out_f):
-    mine_f[pl.ds(0, 1024), :] = mine[...].astype(F32)
-    both_f[pl.ds(0, 2048), :] = both[...].astype(F32)
+    for at in range(16):
+        mine_f[pl.ds(at * PITCH, 64), :] = mine[pl.ds(at * 64, 64), :].astype(F32)
+    for at in range(32):
+        both_f[pl.ds(at * PITCH, 64), :] = both[pl.ds(at * 64, 64), :].astype(F32)
 
     def matrix(source, base):
         tiles = swap_groups([
             stack(
-                source[pl.ds(base + ((zh * 2 + xl) * 2 + yh) * 64 + m, 8, stride=8), :]
+                source[pl.ds(base + yh * 8 * PITCH + (xl * 4 + zh) * 8 + m, 8, stride=PITCH), :]
                 for xl in range(2) for m in range(GROUPS) for yh in range(2)
             )
             for zh in range(4)
@@ -244,7 +259,7 @@
         return stack(jnp.concatenate([tile[:half], tile[half:]], axis=1) for tile in tiles).astype(BF16)
 
     left = matrix(mine_f, 0)
-    right = stack(matrix(both_f, core * 1024 + 4) for core in range(2))
+    right = stack(matrix(both_f, core * 16 * PITCH + 4) for core in range(2))
     triangle = nt_dot(left, right).astype(BF16)
     send_home(nn_dot(triangle, token_matrix()), out_ref, out_f)
 
@@ -302,7 +317,7 @@
     small = (jax.ShapeDtypeStruct((LANES, 8), F32), jax.ShapeDtypeStruct((1, CELLS), F32))
     send, gate, columns, vectors, mask = call(
         first_kernel, (sent, tile, tile) + small, [
-            (CELLS, LANES), strided, (8, LANES), pltpu.SMEM(chain_lengths.shape, jnp.int32),
+            (CELLS, LANES), spread, (8, LANES), pltpu.SMEM(chain_lengths.shape, jnp.int32),
             pltpu.VMEM(pair_rep.shape, BF16), in_gain.shape, in_bias.shape, out_gain.shape, out_bias.shape,
             pltpu.VMEM(weight_in.shape[1:], BF16), pltpu.SemaphoreType.DMA((7,)),
         ], "first", range(1, 8),
@@ -310,7 +325,7 @@
     mine = exchange(send.reshape(128, 8, LANES), GROUP1).reshape(1024, LANES)
     both = lax.all_gather(mine, "core", axis=0, tiled=True)
     home = call(
-        outgoing_kernel, sent, [strided, (2048 + SPARE, LANES), spread], "outgoing"
+        outgoing_kernel, sent, [spread, (33 * PITCH, LANES), spread], "outgoing"
     )(mine, both)
     home = exchange(home.reshape(256, 4, LANES), BACK).reshape(1024, LANES)
 

time: 113 us -> 113 us (level)
  no operation moved by 1% of the time
where the time goes in v16:
time: 113 us
  blocking collectives  107 us (95%)
  Pallas kernels  5.64 us (5%)
    all_to_all x4, blocking collectives, exchange(): return lax.all_to_all(array, axes, 0, 0, tiled=True)  97.3 us
    all_gather x2, blocking collectives, on_device(): both = lax.all_gather(mine, 'core', axis=0, tiled=True)  9.64 us
    pallas_call x5, Pallas kernels, run(): pl.pallas_call(kernel, out_shape=outs, in_specs=[pl.BlockSpec(memory_spac...  5.64 us

profile of v16, /device:TPU:1, one launch (start us, length us, event | category | flops | bytes accessed | tf_op | source)
XLA Modules:
  0.0 112.9 jit_solution(2157907183563063127)
XLA Ops:
  0.0 0.1 concatenate.6.place
  0.1 1.7 %first.1 = (bf16[1024,128]{1,0:T(8,128)(2,1)S(1)}, f32[128,512]{1,0:T(8,128)S(1)}, f32[128,512]{1,0:T(8,128)S(1)}, f32[128,8]{1,0:T(8,128)S(1)}, f32[1,512]{1,0:T(1,128)S(1)}) custom-call(s32[16,128]{1,0:T(8,128)S(1)} %concatenate.6.place, s32[4]{0:T(128)} %lengths_hbm.1, bf16[14,28,128]{2,1,0:T(8,128)(2,1)} %pair_hbm.1, f32[2,128]{1,0:T(2,128)} %in_gain_hbm.1, ...), custom_call_target="tpu_custom_call" | custom-call | tf_op jit(solution)/shard_map/first/pallas_call | solution.py:288
  1.8 31.5 %all_to_all.20 = bf16[128,8,128]{2,1,0:T(8,128)(2,1)S(1)} all-to-all(bf16[128,8,128]{2,1,0:T(8,128)(2,1)S(1)} %bitcast.15), channel_id=1, replica_groups=mesh['yh'=2,'yl'=4,'zl'=2,'core'=2,'xh'=2,'xl'=2,'zh'=4] {'yh','yl','zl'..., dimensions={0} | all-to-all | bytes 524288 | tf_op jit(solution)/shard_map/all_to_all | solution.py:306
  33.2 5.0 %all_gather.6.both = bf16[2048,128]{1,0:T(8,128)(2,1)S(1)} all-gather(bf16[1024,128]{1,0:T(8,128)(2,1)S(1)} %bitcast.8), channel_id=1, replica_groups=mesh['yh'=2,'yl'=4,'zl'=2,'core'=2,'xh'=2,'xl'=2,'zh'=4] {'core'}, dimensions={0}, use_global_device_ids=true | all-gather | bytes 786432 | tf_op jit(solution)/shard_map/all_gather | solution.py:326
  38.2 1.1 outgoing.1
  39.3 0.0 copy-start
  39.3 0.0 copy-start.1
  39.3 23.9 %all_to_all.21 = bf16[256,4,128]{2,1,0:T(4,128)(2,1)S(1)} all-to-all(bf16[256,4,128]{2,1,0:T(4,128)(2,1)S(1)} %bitcast.13), channel_id=1, replica_groups=mesh['yh'=2,'yl'=4,'zl'=2,'core'=2,'xh'=2,'xl'=2,'zh'=4] {'yh','yl','zl'..., dimensions={0} | all-to-all | bytes 524288 | tf_op jit(solution)/shard_map/all_to_all | solution.py:306
  63.2 0.0 copy-done
  63.2 0.0 copy-done.1
  63.2 0.7 middle.1
  64.0 18.9 %all_to_all.22 = bf16[128,8,128]{2,1,0:T(8,128)(2,1)S(1)} all-to-all(bf16[128,8,128]{2,1,0:T(8,128)(2,1)S(1)} %bitcast.14), channel_id=1, replica_groups=mesh['yh'=2,'yl'=4,'zl'=2,'core'=2,'xh'=2,'xl'=2,'zh'=4] {'zh','xh','xl'..., dimensions={0} | all-to-all | bytes 524288 | tf_op jit(solution)/shard_map/all_to_all | solution.py:306
  82.8 4.7 %all_gather.7.both = bf16[2048,128]{1,0:T(8,128)(2,1)S(1)} all-gather(bf16[1024,128]{1,0:T(8,128)(2,1)S(1)} %bitcast.16), channel_id=1, replica_groups=mesh['yh'=2,'yl'=4,'zl'=2,'core'=2,'xh'=2,'xl'=2,'zh'=4] {'core'}, dimensions={0}, use_global_device_ids=true | all-gather | bytes 786432 | tf_op jit(solution)/shard_map/all_gather | solution.py:336
  87.5 1.1 incoming.1
  88.6 23.0 %all_to_all.23 = bf16[256,4,128]{2,1,0:T(4,128)(2,1)S(1)} all-to-all(bf16[256,4,128]{2,1,0:T(4,128)(2,1)S(1)} %bitcast.11), channel_id=1, replica_groups=mesh['yh'=2,'yl'=4,'zl'=2,'core'=2,'xh'=2,'xl'=2,'zh'=4] {'yh','yl','zl'..., dimensions={0} | all-to-all | bytes 524288 | tf_op jit(solution)/shard_map/all_to_all | solution.py:306
  111.6 1.1 last.1
  (2 shorter events, 0.0 us)
Async XLA Ops:
  39.3 24.0 %copy-start = (bf16[2,128,640]{2,1,0:T(8,128)(2,1)S(1)}, bf16[2,128,640]{2,1,0:T(8,128)(2,1)}, u32[]{:S(2)}) copy-start(bf16[2,128,640]{2,1,0:T(8,128)(2,1)} %weight.1) | copy-start | bytes 983044
  39.3 23.9 %copy-start.1 = (bf16[2,128,128]{2,1,0:T(8,128)(2,1)S(1)}, bf16[2,128,128]{2,1,0:T(8,128)(2,1)}, u32[]{:S(2)}) copy-start(bf16[2,128,128]{2,1,0:T(8,128)(2,1)} %weight_out.3) | copy-start | bytes 196612
